TPU v7x, 128 devices: a whole 4x4x4 slice. The times are simulated.
128 devices in a mesh: dp: 32 (over z, x, core), tensor: 4 (over y).
Axes of the slice: x: 4, y: 4, z: 4, core: 2. Of those that a mesh axis runs over, the one named last changes fastest.
Arguments:
- text_input: bfloat16 [16384, 768], P(('dp', 'tensor')), may hold values from -6 to 6
- segment_ids: int32 [1024, 16], P('dp'), may hold values from 0 to 1, as said below
- pad_mask: int32 [1024, 16], P('dp'), may hold values from 0 to 1, as said below
- pairing: int32 [2048], P(('dp', 'tensor')), may hold values from 0 to 2047, each once
- ln_first: float32 [768], replicated, may hold values from 0.1 to 1.9
- w_qkv: bfloat16 [3, 768, 768], P(None, None, 'tensor'), may hold values from -0.21875 to 0.21875
- w_out: bfloat16 [768, 768], P('tensor'), may hold values from -0.4375 to 0.4375
- ln_second: float32 [768], replicated, may hold values from 0.1 to 1.9
- w_up: bfloat16 [768, 3072], P(None, 'tensor'), may hold values from -0.21875 to 0.21875
- w_down: bfloat16 [3072, 768], P('tensor'), may hold values from -0.109375 to 0.109375
- text_proj: bfloat16 [768, 768], replicated, may hold values from -0.21875 to 0.21875
- image_tokens: bfloat16 [2048, 50, 768], P(('dp', 'tensor')), may hold values from -6 to 6
- img_ln_first: float32 [768], replicated, may hold values from 0.1 to 1.9
- img_w_qkv: bfloat16 [3, 768, 768], replicated, may hold values from -0.21875 to 0.21875
- img_w_out: bfloat16 [768, 768], replicated, may hold values from -0.875 to 0.875
- img_ln_second: float32 [768], replicated, may hold values from 0.1 to 1.9
- img_w_up: bfloat16 [768, 3072], replicated, may hold values from -0.21875 to 0.21875
- img_w_down: bfloat16 [3072, 768], replicated, may hold values from -0.109375 to 0.109375
- img_proj: bfloat16 [768, 768], replicated, may hold values from -0.21875 to 0.21875
Outputs:
- loss: float32 [], replicated
- input_grad: float32 [16384, 768], P(('dp', 'tensor'))
- ln_first_grad: float32 [768], replicated
- qkv_grad: float32 [3, 768, 768], P(None, None, 'tensor')
- out_grad: float32 [768, 768], P('tensor')
- ln_second_grad: float32 [768], replicated
- up_grad: float32 [768, 3072], P(None, 'tensor')
- down_grad: float32 [3072, 768], P('tensor')
- proj_grad: float32 [768, 768], replicated
Inputs may be any that keep to these rules, and one draw needn't show every extreme that they name: `segment_ids`: each sequence holds two captions of 3 to 8 rows each, numbered 0 then 1 in order; padding rows after the second caption carry 1. `pad_mask`: 1 on the rows of the two captions of a sequence, 0 on the padding rows that follow them. `pairing`: a permutation: each image belongs to exactly one caption.
All inputs are finite; a program needn't handle non-finite values.
Results may differ from a plain program's by a relative error of at most 0.02.
Values may be sent and summed in bfloat16 or wider, within the bound.
A program may use at most 128 MiB of HBM per device.

v0:
```python
from functools import partial

import jax
import jax.numpy as jnp
from jax import lax
from jax.sharding import PartitionSpec as P

HEAD_DIM = 64
SEQ_LEN = 16
CAP_SEQ = 2


EXACT = lax.Precision.HIGHEST
NORM_EPS = 1e-06
SCORE_SCALE = 0.125
LOGIT_SCALE = 40.0
MASKED = -1e30


def layer_norm(values, gain_row):
    centred = values - jnp.mean(values, axis=-1, keepdims=True)
    spread = jnp.mean(centred * centred, axis=-1, keepdims=True)
    return centred * lax.rsqrt(spread + NORM_EPS) * gain_row


def lowered(values):
    return values.astype(jnp.bfloat16)


def unit_rows(values):
    return values * lax.rsqrt(jnp.sum(values * values, axis=-1, keepdims=True) + NORM_EPS)


def image_tower(image_tokens, ln_one, w_triple, w_output, ln_two, w_upper, w_lower, w_project):
    image_count, length, model_width = image_tokens.shape
    all_heads = model_width // HEAD_DIM
    stream = image_tokens.astype(jnp.float32).reshape(image_count * length, model_width)
    normed = lowered(layer_norm(stream, ln_one))
    triple = lowered(
        jnp.einsum("rd,kde->kre", normed, w_triple, preferred_element_type=jnp.float32)
    )
    shaped = triple.reshape(3, image_count, length, all_heads, HEAD_DIM)
    scores = (
        jnp.einsum("bqhd,bkhd->bhqk", shaped[0], shaped[1], preferred_element_type=jnp.float32)
        * SCORE_SCALE
    )
    weights = lowered(jax.nn.softmax(scores, axis=-1))
    attended = jnp.einsum("bhqk,bkhd->bqhd", weights, shaped[2], preferred_element_type=jnp.float32)
    attended = lowered(attended.reshape(image_count * length, model_width))
    stream = stream + jnp.dot(attended, w_output, preferred_element_type=jnp.float32)
    second = lowered(layer_norm(stream, ln_two))
    hidden = lowered(
        jax.nn.gelu(jnp.dot(second, w_upper, preferred_element_type=jnp.float32), approximate=False)
    )
    stream = stream + jnp.dot(hidden, w_lower, preferred_element_type=jnp.float32)
    pooled = lowered(jnp.mean(stream.reshape(image_count, length, model_width), axis=1))
    return lowered(unit_rows(jnp.dot(pooled, w_project, preferred_element_type=jnp.float32)))


def block_mask(segments, kept_rows):
    block_size = segments.shape[0]
    sequence = lax.broadcasted_iota(jnp.int32, (block_size,), 0) // SEQ_LEN
    same_caption = (sequence[:, None] == sequence[None, :]) & (
        segments[:, None] == segments[None, :]
    )
    return same_caption & (kept_rows[None, :] == 1)


def masked_scores(query_rows, key_rows, segments, kept_rows):
    scores = (
        jnp.einsum("qhd,khd->hqk", query_rows, key_rows, preferred_element_type=jnp.float32)
        * SCORE_SCALE
    )
    return jnp.where(block_mask(segments, kept_rows)[None], scores, MASKED)


def attend_forward(operands):
    query_rows, key_rows, value_rows, segments, kept_rows = operands
    masked = masked_scores(query_rows, key_rows, segments, kept_rows)
    row_top = jnp.max(masked, axis=-1, keepdims=True)
    exponent = jnp.exp(masked - row_top)
    row_total = jnp.sum(exponent, axis=-1, keepdims=True)
    weights = lowered(exponent / row_total)
    attended = lowered(
        jnp.einsum("hqk,khd->qhd", weights, value_rows, preferred_element_type=jnp.float32)
    )
    return (attended, row_top + jnp.log(row_total))


def attend_backward(operands):
    query_rows, key_rows, value_rows, segments, kept_rows, grad_rows, log_total = operands
    masked = masked_scores(query_rows, key_rows, segments, kept_rows)
    weights = jnp.exp(masked - log_total)
    grad_weights = jnp.einsum(
        "qhd,khd->hqk", grad_rows, value_rows, preferred_element_type=jnp.float32
    )
    grad_values = jnp.einsum(
        "hqk,qhd->khd", lowered(weights), grad_rows, preferred_element_type=jnp.float32
    )
    centre = jnp.sum(weights * grad_weights, axis=-1, keepdims=True)
    grad_scores = lowered(weights * (grad_weights - centre))
    grad_query = (
        jnp.einsum("hqk,khd->qhd", grad_scores, key_rows, preferred_element_type=jnp.float32)
        * SCORE_SCALE
    )
    grad_keys = (
        jnp.einsum("hqk,qhd->khd", grad_scores, query_rows, preferred_element_type=jnp.float32)
        * SCORE_SCALE
    )
    return (grad_query, grad_keys, grad_values)


def on_device(
    text_input,
    segment_ids,
    pad_mask,
    pairing,
    ln_first,
    w_qkv,
    w_out,
    ln_second,
    w_up,
    w_down,
    text_proj,
    image_tokens,
    img_ln_first,
    img_w_qkv,
    img_w_out,
    img_ln_second,
    img_w_up,
    img_w_down,
    img_proj,
):
    image_rows = image_tower(
        image_tokens,
        img_ln_first,
        img_w_qkv,
        img_w_out,
        img_ln_second,
        img_w_up,
        img_w_down,
        img_proj,
    )
    local_rows = text_input.shape[0]
    group_rows = local_rows * lax.axis_size("tensor")
    tensor_rank = lax.axis_index("tensor")
    local_width = w_qkv.shape[2]
    local_heads = local_width // HEAD_DIM
    block_rows = min(group_rows, 512)
    blocks = group_rows // block_rows

    def head_blocks(values):
        return values.reshape(blocks, block_rows, local_heads, HEAD_DIM)

    seg_blocks = segment_ids.reshape(blocks, block_rows)
    kept_blocks = pad_mask.reshape(blocks, block_rows)
    stream = text_input.astype(jnp.float32)
    normed_one = lax.all_gather(lowered(layer_norm(stream, ln_first)), "tensor", axis=0, tiled=True)
    triple = lowered(
        jnp.einsum("rd,kde->kre", normed_one, w_qkv, preferred_element_type=jnp.float32)
    )
    query_blocks = head_blocks(triple[0])
    key_blocks = head_blocks(triple[1])
    value_blocks = head_blocks(triple[2])
    attended, log_total = lax.map(
        attend_forward, (query_blocks, key_blocks, value_blocks, seg_blocks, kept_blocks)
    )
    attended = attended.reshape(group_rows, local_width)
    middle = stream + lax.psum_scatter(
        jnp.dot(attended, w_out, preferred_element_type=jnp.float32).astype(jnp.bfloat16),
        "tensor",
        scatter_dimension=0,
        tiled=True,
    ).astype(jnp.float32)
    second = lax.all_gather(lowered(layer_norm(middle, ln_second)), "tensor", axis=0, tiled=True)
    before = jnp.dot(second, w_up, preferred_element_type=jnp.float32)
    hidden = lowered(jax.nn.gelu(before, approximate=False))
    output_rows = middle + lax.psum_scatter(
        jnp.dot(hidden, w_down, preferred_element_type=jnp.float32).astype(jnp.bfloat16),
        "tensor",
        scatter_dimension=0,
        tiled=True,
    ).astype(jnp.float32)
    seq_local = local_rows // SEQ_LEN
    own_captions = CAP_SEQ * seq_local
    own_segments = lax.dynamic_slice_in_dim(
        segment_ids, tensor_rank * seq_local, seq_local, 0
    ).reshape(-1)
    own_kept = lax.dynamic_slice_in_dim(pad_mask, tensor_rank * seq_local, seq_local, 0).reshape(-1)
    caption_of = (
        lax.broadcasted_iota(jnp.int32, (local_rows,), 0) // SEQ_LEN * CAP_SEQ + own_segments
    )
    caption_ids = lax.broadcasted_iota(jnp.int32, (own_captions,), 0)
    member = ((caption_of[None, :] == caption_ids[:, None]) & (own_kept[None, :] == 1)).astype(
        jnp.float32
    )
    pool_weights = member / jnp.sum(member, axis=1, keepdims=True)
    pooled = lowered(jnp.dot(pool_weights, output_rows, precision=EXACT))
    embedding = jnp.dot(pooled, text_proj, preferred_element_type=jnp.float32)
    row_scale = lax.rsqrt(jnp.sum(embedding * embedding, axis=-1, keepdims=True) + NORM_EPS)
    unit_text = embedding * row_scale
    text_rows = lowered(unit_text)
    all_text, all_images = (
        lax.all_gather(text_rows, ("dp", "tensor"), axis=0, tiled=True),
        lax.all_gather(image_rows, ("dp", "tensor"), axis=0, tiled=True),
    )
    captions = own_captions * lax.axis_size(("dp", "tensor"))
    row_scores = LOGIT_SCALE * jnp.einsum(
        "ce,ie->ci", text_rows, all_images, preferred_element_type=jnp.float32
    )
    row_totals = jax.nn.logsumexp(row_scores, axis=1)
    column_scores = LOGIT_SCALE * jnp.einsum(
        "ce,ie->ci", all_text, image_rows, preferred_element_type=jnp.float32
    )
    own_columns = jax.nn.logsumexp(column_scores, axis=0)
    column_totals = lax.all_gather(own_columns, ("dp", "tensor"), axis=0, tiled=True)
    target = (pairing[:, None] == lax.broadcasted_iota(jnp.int32, (1, captions), 1)).astype(
        jnp.float32
    )
    loss_part = jnp.sum(row_totals) + jnp.sum(own_columns) - 2.0 * jnp.sum(row_scores * target)
    grad_scores = lowered(
        0.5
        * (
            jnp.exp(row_scores - row_totals[:, None])
            + jnp.exp(row_scores - column_totals[None, :])
            - 2.0 * target
        )
    )
    grad_unit = LOGIT_SCALE * jnp.dot(grad_scores, all_images, preferred_element_type=jnp.float32)
    grad_embed = lowered(
        row_scale * (grad_unit - unit_text * jnp.sum(unit_text * grad_unit, axis=-1, keepdims=True))
    )
    proj_part = jnp.einsum("cd,ce->de", pooled, grad_embed, preferred_element_type=jnp.float32)
    grad_pooled = jnp.einsum("ce,de->cd", grad_embed, text_proj, preferred_element_type=jnp.float32)
    grad_output = jnp.einsum("cr,cd->rd", pool_weights, grad_pooled, precision=EXACT)
    grad_rows = lax.all_gather(lowered(grad_output), "tensor", axis=0, tiled=True)
    grad_down = jnp.einsum("rf,rd->fd", hidden, grad_rows, preferred_element_type=jnp.float32)
    grad_hidden = jnp.einsum("rd,fd->rf", grad_rows, w_down, preferred_element_type=jnp.float32)
    _, gelu_back = jax.vjp(partial(jax.nn.gelu, approximate=False), before)
    grad_before = lowered(gelu_back(grad_hidden)[0])
    grad_up = jnp.einsum("rd,rf->df", second, grad_before, preferred_element_type=jnp.float32)
    piece = grad_before
    grad_second = lax.psum_scatter(
        jnp.einsum("rf,df->rd", piece, w_up, preferred_element_type=jnp.float32).astype(
            jnp.bfloat16
        ),
        "tensor",
        scatter_dimension=0,
        tiled=True,
    ).astype(jnp.float32)
    _, second_back = jax.vjp(layer_norm, middle, ln_second)
    grad_middle_norm, grad_ln_second = second_back(grad_second)
    grad_middle = grad_output + grad_middle_norm
    grad_attn_rows = lax.all_gather(lowered(grad_middle), "tensor", axis=0, tiled=True)
    grad_out = jnp.einsum("rc,rd->cd", attended, grad_attn_rows, preferred_element_type=jnp.float32)
    grad_attended = lowered(
        jnp.einsum("rd,cd->rc", grad_attn_rows, w_out, preferred_element_type=jnp.float32)
    )
    grad_query, grad_keys, grad_values = lax.map(
        attend_backward,
        (
            query_blocks,
            key_blocks,
            value_blocks,
            seg_blocks,
            kept_blocks,
            head_blocks(grad_attended),
            log_total,
        ),
    )
    grad_triple = lowered(
        jnp.stack(
            [
                gradient_piece.reshape(group_rows, local_width)
                for gradient_piece in (grad_query, grad_keys, grad_values)
            ]
        )
    )
    grad_qkv = jnp.einsum(
        "rd,kre->kde", normed_one, grad_triple, preferred_element_type=jnp.float32
    )
    piece = grad_triple
    grad_first = lax.psum_scatter(
        jnp.einsum("kre,kde->rd", piece, w_qkv, preferred_element_type=jnp.float32).astype(
            jnp.bfloat16
        ),
        "tensor",
        scatter_dimension=0,
        tiled=True,
    ).astype(jnp.float32)
    _, first_back = jax.vjp(layer_norm, stream, ln_first)
    grad_stream_norm, grad_ln_first = first_back(grad_first)
    input_grad = grad_middle + grad_stream_norm
    grad_qkv, grad_out, grad_up, grad_down = (
        lax.psum(grad_qkv.astype(jnp.bfloat16), "dp").astype(jnp.float32),
        lax.psum(grad_out.astype(jnp.bfloat16), "dp").astype(jnp.float32),
        lax.psum(grad_up.astype(jnp.bfloat16), "dp").astype(jnp.float32),
        lax.psum(grad_down.astype(jnp.bfloat16), "dp").astype(jnp.float32),
    )
    loss_total, grad_ln_first, grad_ln_second, grad_proj = lax.psum(
        (loss_part, grad_ln_first, grad_ln_second, proj_part), ("dp", "tensor")
    )
    loss_value = loss_total / (2.0 * captions)
    return (
        loss_value,
        input_grad,
        grad_ln_first,
        grad_qkv,
        grad_out,
        grad_ln_second,
        grad_up,
        grad_down,
        grad_proj,
    )


def solution(mesh):
    in_specs = (
        P(("dp", "tensor"), None),
        P("dp", None),
        P("dp", None),
        P(("dp", "tensor")),
        P(),
        P(None, None, "tensor"),
        P("tensor", None),
        P(),
        P(None, "tensor"),
        P("tensor", None),
        P(),
        P(("dp", "tensor"), None, None),
        P(),
        P(),
        P(),
        P(),
        P(),
        P(),
        P(),
    )
    out_specs = (
        P(),
        P(("dp", "tensor"), None),
        P(),
        P(None, None, "tensor"),
        P("tensor", None),
        P(),
        P(None, "tensor"),
        P("tensor", None),
        P(),
    )
    return jax.shard_map(
        on_device, mesh=mesh, in_specs=in_specs, out_specs=out_specs, check_vma=False
    )
```

profile of v0, /device:TPU:1, one launch (start us, length us, event | category | flops | bytes accessed | tf_op | source)
XLA Modules:
  0.0 732.9 jit_solution(7979908267299709083)
XLA Ops:
  12.8 13.3 %all_gather.21 = bf16[512,768]{1,0:T(8,128)(2,1)S(1)} all-gather(bf16[128,768]{1,0:T(8,128)(2,1)S(1)} %fusion.68), channel_id=1, replica_groups=mesh['dp'=32,'tensor'=4] {'tensor'}, dimensions={0}, use_global_device_ids=true | all-gather | bytes 983040 | tf_op jit(solution)/shard_map/all_gather | solution.py:158
  26.1 2.1 fusion.153
  38.5 3.3 copy.91
  44.9 3.0 reshape.341
  47.8 2.4 multiply_reduce_fusion.3
  51.2 5.7 convert_bitcast_fusion
  58.7 3.9 squeeze.46
  62.6 4.8 squeeze.47
  67.4 3.5 fusion.19
  70.9 4.0 fusion.148
  75.0 3.4 squeeze.45
  78.3 5.2 convert_bitcast_fusion.1
  84.1 3.3 convert_element_type.176
  87.4 3.7 fusion.149
  95.2 10.4 %all_gather.22 = bf16[512,768]{1,0:T(8,128)(2,1)S(1)} all-gather(bf16[128,768]{1,0:T(8,128)(2,1)S(1)} %multiply_convert_fusion.9), channel_id=1, replica_groups=mesh['dp'=32,'tensor'=4] {'tensor'}, dimensions={0}, use_global_device_ids=true | all-gather | bytes 983040 | tf_op jit(solution)/shard_map/all_gather | solution.py:175
  105.7 6.6 multiply_convert_fusion.3
  114.9 31.8 %fusion.27 = f32[800,768]{1,0:T(8,128)} fusion(f32[800,768]{1,0:T(8,128)S(1)} %get-tuple-element.99, bf16[3072,768]{1,0:T(8,128)(2,1)} %param.36, bf16[768,3072]{1,0:T(8,128)(2,1)} %param.35, f32[768]{0:T(1024)S(1)} %copy-done.73, f32[800]{0:T(1024)S(1)} %add_rsqrt_fusion.1, f32[800]{0:T(1024)S(1)} %broadcast_multiply_fusion.1), kind=kOutput, calls=%fused_computation.50 | convolution fusion | flops 7712563200 | bytes 14361856 | tf_op jit(solution)/shard_map/dot_general | solution.py:55
  156.2 69.1 %all-gather.3.cloned.1.call-done = bf16[2048,768]{1,0:T(8,128)(2,1)} async-done(((bf16[16,768]{1,0:T(8,128)(2,1)}), bf16[2048,768]{1,0:T(8,128)(2,1)}) %all-gather.3.cloned.1.call-update) | async-done | bytes 3145744 | tf_op jit(solution)/shard_map/all_gather | solution.py:205
  225.3 2.9 fusion.150
  230.1 61.4 %all-gather.5.cloned.1.call-done = bf16[2048,768]{1,0:T(8,128)(2,1)} async-done(((bf16[16,768]{1,0:T(8,128)(2,1)}), bf16[2048,768]{1,0:T(8,128)(2,1)}) %all-gather.5.cloned.1.call-update) | async-done | bytes 3145744 | tf_op jit(solution)/shard_map/all_gather | solution.py:204
  291.5 2.9 fusion.151
  296.0 62.3 %all-reduce = f32[2048]{0:T(1024)S(1)} all-reduce(f32[2048]{0:T(1024)} %copy-done.50), channel_id=1, replica_groups=mesh['dp'=32,'tensor'=4] {'dp','tensor'}, use_global_device_ids=true, to_apply=%add | all-reduce | flops 2048 | bytes 16384
  363.3 12.0 %all_gather.26 = bf16[512,768]{1,0:T(8,128)(2,1)S(1)} all-gather(bf16[128,768]{1,0:T(8,128)(2,1)S(1)} %get-tuple-element.108), channel_id=1, replica_groups=mesh['dp'=32,'tensor'=4] {'tensor'}, dimensions={0}, use_global_device_ids=true | all-gather | bytes 983040 | tf_op jit(solution)/shard_map/all_gather | solution.py:236
  379.6 20.3 %reduce-scatter.9.cloned.1.call-done = bf16[128,768]{1,0:T(8,128)(2,1)} async-done(((bf16[512,768]{1,0:T(8,128)(2,1)}), bf16[128,768]{1,0:T(8,128)(2,1)}) %reduce-scatter.9.cloned.1.call-update) | async-done | bytes 196624 | tf_op jit(solution)/shard_map/reduce_scatter | solution.py:243
  405.4 10.8 %all_gather.27 = bf16[512,768]{1,0:T(8,128)(2,1)S(1)} all-gather(bf16[128,768]{1,0:T(8,128)(2,1)S(1)} %fusion.85), channel_id=1, replica_groups=mesh['dp'=32,'tensor'=4] {'tensor'}, dimensions={0}, use_global_device_ids=true | all-gather | bytes 983040 | tf_op jit(solution)/shard_map/all_gather | solution.py:254
  425.7 3.1 convolution_convert_fusion.1
  436.1 12.9 %reduce-scatter.11.cloned.1.call-done = bf16[128,768]{1,0:T(8,128)(2,1)} async-done(((bf16[512,768]{1,0:T(8,128)(2,1)}), bf16[128,768]{1,0:T(8,128)(2,1)}) %reduce-scatter.11.cloned.1.call-update) | async-done | bytes 196624 | tf_op jit(solution)/shard_map/reduce_scatter | solution.py:283
  451.4 66.3 %all-reduce.1 = (f32[]{:T(128)}, f32[768]{0:T(1024)}, f32[768]{0:T(1024)}) all-reduce(f32[]{:T(128)S(6)} %sub.168, f32[768]{0:T(1024)S(1)} %get-tuple-element.57, f32[768]{0:T(1024)S(1)} %copy-done.51), channel_id=1, replica_groups=mesh['dp'=32,'tensor'=4] {'dp','tensor'}, use_global_device_ids=true, to_apply=%region_25.26 | all-reduce | flops 1537 | bytes 12296 | tf_op jit(solution)/shard_map/psum | solution.py:300
  520.4 44.4 %all-reduce.8.cloned.1.call-done = (bf16[3,768,192]{1,2,0:T(8,128)(2,1)}, bf16[192,768]{1,0:T(8,128)(2,1)}, bf16[768,768]{1,0:T(8,128)(2,1)}, bf16[768,768]{1,0:T(8,128)(2,1)}) async-done(((bf16[3,768,192]{1,2,0:T(8,128)(2,1)}, bf16[192,768]{1,0:T(8,128)(2,1)}, bf16[768,768]{1,0:T(8,128)(2,1)}, bf16[768,768]{1,0:T(8,128)(2,1)}), (bf16[3,768,192]{1,2,0:T(8,128)(2,1)}, bf16[192,768]{1,0:T(8,128)(2,1)}, ...) | async-done | bytes 3538960 | tf_op jit(solution)/shard_map/psum | solution.py:295
  564.9 2.9 convert_element_type.199
  571.6 149.3 %all-reduce.6.cloned.1.call-done = f32[768,768]{1,0:T(8,128)} async-done(((f32[768,768]{1,0:T(8,128)}), f32[768,768]{1,0:T(8,128)}) %all-reduce.6.cloned.1.call-update) | async-done | bytes 2359312 | tf_op jit(solution)/shard_map/psum | solution.py:300
  720.9 3.2 copy.123
  (268 shorter events, 78.0 us)
Async XLA Ops:
  8.0 43.2 %copy-start = (bf16[3,768,768]{2,1,0:T(8,128)(2,1)S(1)}, bf16[3,768,768]{2,1,0:T(8,128)(2,1)}, u32[]{:S(2)}) copy-start(bf16[3,768,768]{2,1,0:T(8,128)(2,1)} %param.32) | copy-start | bytes 10616836
  8.0 83.5 %reduce-scatter.5.cloned.1.call-start = ((), (), s32[]{:S(2)}) async-start(), calls=%async_computation.4 | async-start | bytes 983040 | tf_op jit(solution)/shard_map/reduce_scatter | solution.py:169
  10.0 16.1 %copy-start.52 = (f32[128]{0:T(128)}, f32[128]{0:T(128)S(1)}, u32[]{:S(2)}) copy-start(f32[128]{0:T(128)S(1)} %broadcast_multiply_fusion.3) | copy-start | bytes 1540
  38.2 113.6 %reduce-scatter.7.cloned.1.call-start = ((), (), s32[]{:S(2)}) async-start(), calls=%async_computation.5 | async-start | bytes 983040 | tf_op jit(solution)/shard_map/reduce_scatter | solution.py:178
  94.1 18.1 %copy-start.69 = (f32[128]{0:T(128)}, f32[128]{0:T(128)S(1)}, u32[]{:S(2)}) copy-start(f32[128]{0:T(128)S(1)} %multiply_reduce_fusion.4) | copy-start | bytes 1540
  94.2 18.1 %copy-start.54 = (f32[128]{0:T(128)}, f32[128]{0:T(128)S(1)}, u32[]{:S(2)}) copy-start(f32[128]{0:T(128)S(1)} %fusion.102) | copy-start | bytes 1540
  114.8 110.5 %all-gather.3.cloned.1.call-start = ((), (), s32[]{:S(2)}) async-start(), calls=%async_computation.6 | async-start | bytes 3170304 | tf_op jit(solution)/shard_map/all_gather | solution.py:205
  151.2 140.3 %all-gather.5.cloned.1.call-start = ((), (), s32[]{:S(2)}) async-start(), calls=%async_computation.7 | async-start | bytes 3170304 | tf_op jit(solution)/shard_map/all_gather | solution.py:204
  151.5 76.7 %copy-start.64 = (pred[128]{0:T(512)(128)(4,1)}, pred[128]{0:T(512)(128)(4,1)S(1)}, u32[]{:S(2)}) copy-start(pred[128]{0:T(512)(128)(4,1)S(1)} %eq.134) | copy-start | bytes 388
  153.6 74.6 %copy-start.61 = (s32[16]{0:T(128)S(1)}, s32[16]{0:T(128)}, u32[]{:S(2)}) copy-start(s32[16]{0:T(128)} %param.22) | copy-start | bytes 196
  156.1 243.9 %reduce-scatter.9.cloned.1.call-start = ((), (), s32[]{:S(2)}) async-start(), calls=%async_computation.8 | async-start | bytes 983040 | tf_op jit(solution)/shard_map/reduce_scatter | solution.py:243
  230.1 128.3 %copy-start.5 = (bf16[2048,768]{1,0:T(8,128)(2,1)S(1)}, bf16[2048,768]{1,0:T(8,128)(2,1)}, u32[]{:S(2)}) copy-start(bf16[2048,768]{1,0:T(8,128)(2,1)} %all-gather.3.cloned.1.call-done) | copy-start | bytes 9437188
  358.4 17.0 %copy-start.71 = (bf16[768,768]{1,0:T(8,128)(2,1)S(1)}, bf16[768,768]{1,0:T(8,128)(2,1)}, u32[]{:S(2)}) copy-start(bf16[768,768]{1,0:T(8,128)(2,1)} %param.28) | copy-start | bytes 3538948
  358.4 17.0 %copy-start.77 = (f32[512,768]{1,0:T(8,128)S(1)}, f32[512,768]{1,0:T(8,128)}, u32[]{:S(2)}) copy-start(f32[512,768]{1,0:T(8,128)} %get-tuple-element.82) | copy-start | bytes 4718596
  358.4 17.0 %copy-start.78 = (f32[512,768]{1,0:T(8,128)S(1)}, f32[512,768]{1,0:T(8,128)}, u32[]{:S(2)}) copy-start(f32[512,768]{1,0:T(8,128)} %get-tuple-element.93) | copy-start | bytes 4718596
  360.9 14.5 %copy-start.36 = (bf16[16,768]{1,0:T(8,128)(2,1)}, bf16[16,768]{1,0:T(8,128)(2,1)S(1)}, u32[]{:S(2)}) copy-start(bf16[16,768]{1,0:T(8,128)(2,1)S(1)} %multiply_convert_fusion.12) | copy-start | bytes 73732
  378.7 39.1 %copy-start.3 = (f32[3,512,512]{1,2,0:T(8,128)S(1)}, f32[3,512,512]{1,2,0:T(8,128)}, u32[]{:S(2)}) copy-start(f32[3,512,512]{1,2,0:T(8,128)} %copy-done.2) | copy-start | bytes 9437188
  378.7 70.3 %reduce-scatter.11.cloned.1.call-start = ((), (), s32[]{:S(2)}) async-start(), calls=%async_computation.9 | async-start | bytes 983040 | tf_op jit(solution)/shard_map/reduce_scatter | solution.py:283
  399.9 17.8 %copy-start.24 = (bf16[1,512,192]{1,2,0:T(8,128)(2,1)S(1)}, bf16[1,512,192]{1,2,0:T(8,128)(2,1)}, u32[]{:S(2)}) copy-start(bf16[1,512,192]{1,2,0:T(8,128)(2,1)} %get-tuple-element.88) | copy-start | bytes 589828
  423.6 141.3 %all-reduce.8.cloned.1.call-start = ((), (), s32[]{:S(2)}) async-start(), calls=%async_computation.11 | async-start | bytes 7077888 | tf_op jit(solution)/shard_map/psum | solution.py:295
  431.5 17.5 %copy-start.46 = (f32[768]{0:T(1024)S(1)}, f32[768]{0:T(1024)}, u32[]{:S(2)}) copy-start(f32[768]{0:T(1024)} %param.23) | copy-start | bytes 9220
  431.5 17.5 %copy-start.53 = (f32[128]{0:T(128)S(1)}, f32[128]{0:T(128)}, u32[]{:S(2)}) copy-start(f32[128]{0:T(128)} %copy-done.52) | copy-start | bytes 1540
  431.5 18.7 %copy-start.68 = (f32[128]{0:T(128)S(1)}, f32[128]{0:T(128)}, u32[]{:S(2)}) copy-start(f32[128]{0:T(128)} %copy-done.67) | copy-start | bytes 1540
  431.5 18.7 %copy-start.57 = (f32[128]{0:T(128)S(1)}, f32[128]{0:T(128)}, u32[]{:S(2)}) copy-start(f32[128]{0:T(128)} %copy-done.56) | copy-start | bytes 1540
  431.5 19.9 %copy-start.51 = (f32[768]{0:T(1024)S(1)}, f32[768]{0:T(1024)}, u32[]{:S(2)}) copy-start(f32[768]{0:T(1024)} %get-tuple-element.55) | copy-start | bytes 9220
  431.5 86.9 %copy-start.12 = (f32[128,768]{1,0:T(8,128)S(1)}, f32[128,768]{1,0:T(8,128)}, u32[]{:S(2)}) copy-start(f32[128,768]{1,0:T(8,128)} %get-tuple-element.109) | copy-start | bytes 1179652
  431.5 86.9 %copy-start.13 = (bf16[128,768]{1,0:T(8,128)(2,1)S(1)}, bf16[128,768]{1,0:T(8,128)(2,1)}, u32[]{:S(2)}) copy-start(bf16[128,768]{1,0:T(8,128)(2,1)} %reduce-scatter.9.cloned.1.call-done) | copy-start | bytes 589828
  431.5 86.9 %copy-start.55 = (f32[128]{0:T(128)S(1)}, f32[128]{0:T(128)}, u32[]{:S(2)}) copy-start(f32[128]{0:T(128)} %copy-done.54) | copy-start | bytes 1540
  431.6 86.9 %copy-start.59 = (f32[128]{0:T(128)S(1)}, f32[128]{0:T(128)}, u32[]{:S(2)}) copy-start(f32[128]{0:T(128)} %copy-done.58) | copy-start | bytes 1540
  431.6 86.9 %copy-start.63 = (f32[128]{0:T(128)S(1)}, f32[128]{0:T(128)}, u32[]{:S(2)}) copy-start(f32[128]{0:T(128)} %copy-done.62) | copy-start | bytes 1540
  431.6 289.3 %all-reduce.6.cloned.1.call-start = ((), (), s32[]{:S(2)}) async-start(), calls=%async_computation.10 | async-start | bytes 4718592 | tf_op jit(solution)/shard_map/psum | solution.py:300
  570.8 153.4 %copy-start.1 = (bf16[3,768,768]{2,1,0:T(8,128)(2,1)S(1)}, bf16[3,768,768]{2,1,0:T(8,128)(2,1)}, u32[]{:S(2)}) copy-start(bf16[3,768,768]{2,1,0:T(8,128)(2,1)} %param.32) | copy-start | bytes 10616836
  (55 other events, 128.1 us)
Sparse Core Ops, SparseCore 0:
  38.3 25.3 reduce-scatter.4
  114.9 29.0 reduce-scatter.6
  378.8 21.0 reduce-scatter.8
  423.7 25.2 reduce-scatter.10
  453.2 111.6 all-reduce.7
  570.1 150.7 all-reduce.5
Sparse Core Ops, SparseCore 1:
  151.3 74.0 all-gather.2
  228.2 63.3 all-gather.4
where the time goes:
time: 738 us; the launch traced here: 733 us
  waiting for transfers between devices  358 us (49%)
  blocking collectives  175 us (24%)
  matrix products  96.5 us (13%)
  local copies, waits for them, and re-layouts  41.9 us (6%)
  other arithmetic  40.3 us (5%)
  between operations  20.6 us (3%)
    psum x1, waiting for transfers between devices, on_device(): lax.psum((loss_part, grad_ln_first, grad_ln_second, proj_part), ('dp', 't...  149 us
    all_gather x1, waiting for transfers between devices, on_device(): lax.all_gather(image_rows, ('dp', 'tensor'), axis=0, tiled=True)  69.1 us
    psum x1, blocking collectives, on_device(): lax.psum((loss_part, grad_ln_first, grad_ln_second, proj_part), ('dp', 't...  66.3 us
    unnamed x1, blocking collectives  62.3 us
    all_gather x1, waiting for transfers between devices, on_device(): lax.all_gather(text_rows, ('dp', 'tensor'), axis=0, tiled=True)  61.4 us
    psum x1, waiting for transfers between devices, on_device(): lax.psum(grad_qkv.astype(jnp.bfloat16), 'dp').astype(jnp.float32)  44.4 us
    dot_general x1, matrix products, image_tower(): jnp.dot(hidden, w_lower, preferred_element_type=jnp.float32)  31.8 us
    reduce_scatter x1, waiting for transfers between devices, on_device(): lax.psum_scatter(jnp.einsum('rf,df->rd', piece, w_up, preferred_element_t...  20.3 us
  transfers between devices with their start and end apart: 8, of which 6 were waited for; matrix products, arithmetic and copies ran while one was open for 16% of the time, Pallas kernels for 0%

commit v1 on v0

v1 whole, which is shorter than its diff:
```python
import jax, jax.numpy as jnp
from jax import lax
from jax.experimental import pallas as pl
from jax.experimental.pallas import tpu as pltpu
from jax.sharding import PartitionSpec as P

F32, BF16, I32 = jnp.float32, jnp.bfloat16, jnp.int32
VM = pltpu.VMEM
EPS = 1e-6
NEG = -1e30
D, FF, HID = 768, 3072, 768
IMGS, POS = 16, 50
IROWS = IMGS * POS
PAIR = 112
PROWS = PAIR * (IMGS // 2)
TILE = 256


def dot(a, b):
    return jnp.dot(a, b, preferred_element_type=F32)


def dot_t(a, b):
    return lax.dot_general(a, b, (((1,), (1,)), ((), ())), preferred_element_type=F32)


def t_dot(a, b):
    return lax.dot_general(a, b, (((0,), (0,)), ((), ())), preferred_element_type=F32)


def iota(shape, axis):
    return lax.broadcasted_iota(I32, shape, axis)


def normalized(values):
    centred = values - jnp.mean(values, axis=-1, keepdims=True)
    spread = jnp.mean(centred * centred, axis=-1, keepdims=True)
    scale = lax.rsqrt(spread + EPS)
    return centred * scale, scale


def normal_cdf(u):
    bell = jnp.exp(u * u * -0.5)
    t = 1.0 / (1.0 + (0.3275911 * 0.7071067811865476) * jnp.abs(u))
    poly = t * (0.5 * 0.254829592 + t * (0.5 * -0.284496736 + t * (0.5 * 1.421413741 + t * (0.5 * -1.453152027 + t * (0.5 * 1.061405429)))))
    tail = poly * bell
    return jnp.where(u < 0.0, tail, 1.0 - tail), bell


def image_masks(perm, back, bias):
    lanes = iota((PAIR, IROWS), 1)
    w = iota((PAIR, IROWS), 0)
    second = (w >= POS).astype(I32)
    for p in range(IMGS // 2):
        src = jnp.where(w < 2 * POS, (w - POS * second) * IMGS + 2 * p + second, -1)
        perm[pl.ds(p * PAIR, PAIR), :] = jnp.where(src == lanes, 1.0, 0.0).astype(BF16)

    def rows(i, c):
        r = i * 160 + iota((160, PROWS), 0)
        img, pos = r & 15, r >> 4
        col = (img >> 1) * PAIR + (img & 1) * POS + pos
        back[pl.ds(pl.multiple_of(i * 160, 160), 160), :] = jnp.where(col == iota((160, PROWS), 1), 1.0, 0.0).astype(BF16)
        return c

    lax.fori_loop(0, 5, rows, 0)
    q = iota((2 * PAIR, PAIR), 0)
    q = jnp.where(q >= PAIR, q - PAIR, q)
    k = iota((2 * PAIR, PAIR), 1)
    bias[...] = jnp.where(((q >= POS) == (k >= POS)) & (k < 2 * POS), 0.0, NEG)


def image_norm_one(tok, gain, ia):
    def rows(i, c):
        s = pl.ds(pl.multiple_of(i * 160, 160), 160)
        n, _ = normalized(tok[s, :].astype(F32))
        ia[s, :] = (n * gain).astype(BF16)
        return c

    lax.fori_loop(0, 5, rows, 0)


def tiles(n, body):
    def step(i, c):
        body(i, pl.ds(pl.multiple_of(i * TILE, TILE), TILE))
        return c

    lax.fori_loop(0, n, step, 0)


def image_permute(perm, ia, iap):
    def body(i, s):
        iap[:, s] = dot(perm[...], ia[:, s]).astype(BF16)

    tiles(3, body)


def image_qkv(iap, w, iqkv):
    for j in range(3):
        def body(i, s):
            iqkv[j, :, s] = dot(iap[...], w[j, :, s]).astype(BF16)

        tiles(3, body)


def image_attention(iqkv, bias, iatt, first, last):
    low = iota((PAIR, 128), 1) < 64

    def pair(p, c):
        rows = pl.ds(pl.multiple_of(p * PAIR, PAIR), PAIR)
        ones = jnp.ones((PAIR, 128), BF16)
        zero = jnp.zeros((PAIR, 128), BF16)
        for h in range(6):
            cols = pl.ds(h * 128, 128)
            q, k, v = iqkv[0, rows, cols], iqkv[1, rows, cols], iqkv[2, rows, cols]
            q2 = jnp.concatenate([jnp.where(low, q, zero), jnp.where(low, zero, q)], axis=0)
            s = dot_t(q2, k) * 0.125 + bias[...]
            e = jnp.exp(s - jnp.max(s, axis=-1, keepdims=True)).astype(BF16)
            o = dot(e, jnp.concatenate([v, ones], axis=1))
            o = o[:, :128] / o[:, 128:]
            iatt[rows, cols] = jnp.where(low, o[:PAIR], o[PAIR:]).astype(BF16)
        return c

    lax.fori_loop(first, last, pair, 0)


def image_out(back, iatt, spare, tok, w, iy):
    def body(i, s):
        spare[:, s] = dot(back[...], iatt[:, s]).astype(BF16)

    tiles(3, body)

    def body2(i, s):
        iy[:, s] = tok[:, s].astype(F32) + dot(spare[...], w[:, s])

    tiles(3, body2)


def image_norm_two(iy, gain, ia, ypool):
    ypool[...] = jnp.zeros_like(ypool)

    def rows(i, c):
        s = pl.ds(pl.multiple_of(i * 160, 160), 160)
        y = iy[s, :]
        ypool[...] += jnp.sum(y.reshape(10, IMGS, D), axis=0)
        n, _ = normalized(y)
        ia[s, :] = (n * gain).astype(BF16)
        return c

    lax.fori_loop(0, 5, rows, 0)


def image_up(ia, w, hsum, first, last):
    def step(i, c):
        s = pl.ds(pl.multiple_of(i * TILE, TILE), TILE)
        u = dot(ia[...], w[:, s])
        phi, _ = normal_cdf(u)
        hsum[:, s] = jnp.sum((u * phi).reshape(POS, IMGS, TILE), axis=0)
        return c

    lax.fori_loop(first, last, step, 0)


def split_rows(x):
    hi = x.astype(BF16)
    return jnp.concatenate([hi, (x - hi.astype(F32)).astype(BF16)], axis=0)


def image_finish(hsum, ypool, w_down, w_proj):
    both = dot(split_rows(hsum[...]), w_down[...])
    pooled = ((ypool[...] + both[:IMGS] + both[IMGS:]) * (1.0 / POS)).astype(BF16)
    e = dot(pooled, w_proj[...])
    return (e * lax.rsqrt(jnp.sum(e * e, axis=-1, keepdims=True) + EPS)).astype(BF16)


GROUP, RANKS, CHIPS = 4, 32, 16
OWN, ROWS = 128, 512
CAPS, OWN_CAPS = 64, 16
BAND = 192
HALF = 384
MESH = pl.DeviceIdType.MESH
VEC = 1664


class Links:
    def __init__(self):
        self.dp, self.t = lax.axis_index("dp"), lax.axis_index("tensor")
        self.core, self.chip = lax.rem(self.dp, 2), self.dp // 2

    def rank(self, k):
        return lax.rem(self.t + k, GROUP)

    def group_peer(self, k):
        return {"dp": self.dp, "tensor": self.rank(k)}

    def rank_peer(self, k):
        return {"dp": lax.rem(self.dp + k, RANKS), "tensor": self.t}

    def chip_of(self, k):
        return lax.rem(self.chip + k, CHIPS)

    def chip_peer(self, k):
        return {"dp": 2 * self.chip_of(k) + self.core, "tensor": self.t}

    def sibling(self):
        return {"dp": self.dp + 1 - 2 * self.core, "tensor": self.t}

    def greet(self):
        barrier = pltpu.get_barrier_semaphore()
        for k in range(1, GROUP):
            pl.semaphore_signal(barrier, 1, device_id=self.group_peer(k), device_id_type=MESH)
        for k in range(1, RANKS):
            pl.semaphore_signal(barrier, 1, device_id=self.rank_peer(k), device_id_type=MESH)
        pl.semaphore_wait(barrier, GROUP - 1 + RANKS - 1)


def send(src, dst, sems, at, peer):
    copy = pltpu.make_async_remote_copy(
        src, dst, sems.at[0, at], sems.at[1, at], device_id=peer, device_id_type=MESH
    )
    copy.start()
    return copy


def finish(copies):
    for copy in copies:
        copy.wait()


def group_share(links, buf, sems):
    own = buf.at[links.t]
    return [send(own, own, sems, k - 1, links.group_peer(k)) for k in (2, 1, 3)]


def group_scatter(links, parts, landed, sems):
    return [send(parts.at[links.rank(k)], landed.at[k - 1], sems, k - 1, links.group_peer(k)) for k in (2, 1, 3)]


def rank_share(links, buf, sems):
    own = buf.at[links.dp]
    return [send(own, own, sems, k - 1, links.rank_peer(k)) for k in range(1, RANKS)]


def text_masks(seg_t, pad_t, bias, mem, mem_t):
    seg, pad = seg_t[...].astype(F32).astype(BF16), pad_t[...].astype(F32).astype(BF16)

    def as_column(values):
        pick = jnp.where(iota((ROWS, 32), 0) >> 4 == iota((ROWS, 32), 1), 1.0, 0.0).astype(BF16)
        wide = dot_t(pick, values)
        return jnp.sum(jnp.where(iota((ROWS, 16), 0) & 15 == iota((ROWS, 16), 1), wide, 0.0), axis=1, keepdims=True)

    def as_row(values):
        pick = jnp.where(iota((32, ROWS), 1) >> 4 == iota((32, ROWS), 0), 1.0, 0.0).astype(BF16)
        wide = dot(values, pick)
        return jnp.sum(jnp.where(iota((16, ROWS), 1) & 15 == iota((16, ROWS), 0), wide, 0.0), axis=0, keepdims=True)

    cap_col = as_column(seg) + ((iota((ROWS, 1), 0) >> 4) * 2).astype(F32)
    key_col = jnp.where(as_column(pad) > 0.5, cap_col, -1.0)
    cap_row = as_row(seg) + ((iota((1, ROWS), 1) >> 4) * 2).astype(F32)
    key_row = jnp.where(as_row(pad) > 0.5, cap_row, -1.0)
    for b in range(4):
        rows = slice(128 * b, 128 * b + 128)
        bias[b] = jnp.where(cap_col[rows] == key_row[:, rows], 0.0, NEG)
    mem[...] = jnp.where(iota((CAPS, ROWS), 0).astype(F32) == key_row, 1.0, 0.0).astype(BF16)
    mem_t[...] = jnp.where((iota((ROWS, 128), 1) & 63).astype(F32) == key_col, 1.0, 0.0).astype(BF16)


def text_norm_one(x, gain, a1, t):
    n, _ = normalized(x[...].astype(F32))
    a1[t] = (n * gain).astype(BF16)


def low_half():
    return iota((OWN, 128), 1) < 64


def stacked(values, low):
    zero = jnp.zeros_like(values)
    return jnp.concatenate([jnp.where(low, values, zero), jnp.where(low, zero, values)], axis=0)


def text_attention(a1, w_t, bias, w_out, qkv, probs, att, parts):
    rows_all = a1[...].reshape(ROWS, D)
    for j in range(3):
        qkv[j] = dot_t(rows_all, w_t[j]).astype(BF16)
    low = low_half()

    def soft(s):
        e = jnp.exp(s - jnp.max(s, axis=-1, keepdims=True))
        return e / jnp.sum(e, axis=-1, keepdims=True)

    for b in range(4):
        rows = slice(128 * b, 128 * b + 128)
        q, k, v = qkv[0, rows, :128], qkv[1, rows, :128], qkv[2, rows, :128]
        mask = bias[b]
        p = soft(dot_t(stacked(q, low), k) * 0.125 + jnp.concatenate([mask, mask], axis=0))
        probs[b, :256] = p
        o = dot(p.astype(BF16), v)
        att[rows, :128] = jnp.where(low, o[:128], o[128:]).astype(BF16)
        q, k, v = qkv[0, rows, 128:], qkv[1, rows, 128:], qkv[2, rows, 128:]
        p = soft(dot_t(q, k) * 0.125 + mask)
        probs[b, 256:] = p
        att[rows, 128:] = dot(p.astype(BF16), v).astype(BF16)
    parts[...] = dot(att[...], w_out[...]).astype(BF16).reshape(GROUP, OWN, D)


def summed(parts, landed, t):
    return parts[t].astype(F32) + landed[0].astype(F32) + landed[1].astype(F32) + landed[2].astype(F32)


def split3(x):
    hi = x.astype(BF16)
    rest = x - hi.astype(F32)
    mid = rest.astype(BF16)
    return jnp.concatenate([hi, mid, (rest - mid.astype(F32)).astype(BF16)], axis=0)


def own_member(mem, t):
    return mem[pl.ds(pl.multiple_of(t * OWN_CAPS, OWN_CAPS), OWN_CAPS), pl.ds(pl.multiple_of(t * OWN, OWN), OWN)]


def text_norm_two(x, parts, landed, gain, mem, x1, a2, x1_pool, t):
    y = x[...].astype(F32) + summed(parts, landed, t)
    x1[...] = y
    n, _ = normalized(y)
    a2[t] = (n * gain).astype(BF16)


def text_pool_one(x1, mem, x1_pool, t):
    own = own_member(mem, t)
    x1_pool[...] = dot(jnp.concatenate([own, own, own], axis=1), split3(x1[...]))


def text_up(a2, w_up, mem, w_down, dgelu, hsum, parts):
    def body(i, s):
        u = dot(a2[...].reshape(ROWS, D), w_up[:, s])
        phi, bell = normal_cdf(u)
        dgelu[:, s] = phi + u * bell * 0.3989422804014327
        hsum[:, s] = dot(mem[...], (u * phi).astype(BF16))

    tiles(3, body)
    both = dot(split_rows(hsum[...]), w_down[...])
    parts[...] = (both[:CAPS] + both[CAPS:]).reshape(GROUP, OWN_CAPS, D)


def counts_of(mem):
    return jnp.sum(mem.astype(F32), axis=1, keepdims=True)


def text_embed(parts, landed, x1_pool, mem, w_proj, tf, scale, emb, t):
    total = x1_pool[...] + parts[t] + landed[0] + landed[1] + landed[2]
    pooled = (total / counts_of(own_member(mem, t))).astype(BF16)
    e = dot(pooled, w_proj[...])
    rs = lax.rsqrt(jnp.sum(e * e, axis=-1, keepdims=True) + EPS)
    tf[...] = rs * e
    scale[...] = jnp.broadcast_to(rs, (OWN_CAPS, 128))
    emb[t, :OWN_CAPS] = (rs * e).astype(BF16)
    emb[t, OWN_CAPS:] = pooled


def score_sums(emb, images, s_ref, e_ref, row_sums, col_sums, t, dp):
    text = emb[:, :OWN_CAPS].reshape(CAPS, D)
    s = 40.0 * dot_t(text, images[...].reshape(ROWS, D))
    s_ref[...] = s
    e = jnp.exp(s - 40.0)
    e_ref[...] = e
    row_sums[t] = jnp.broadcast_to(jnp.sum(e, axis=1, keepdims=True), (CAPS, 128))
    col_sums[dp] = jnp.sum(e, axis=0, keepdims=True)


def score_grad(s_ref, e_ref, row_sums, col_sums, pair, images, parts, vec, t):
    rows = jnp.sum(row_sums[...], axis=0)[:, :1]
    cols = col_sums[0]
    for i in range(1, RANKS):
        cols = cols + col_sums[i]
    lane = iota((CAPS, ROWS), 1)
    target = jnp.where(pair[...].reshape(CAPS, 128)[:, :1] == (lane >> 4) * CAPS + OWN_CAPS * t + (lane & 15), 1.0, 0.0)
    g = 0.5 * (e_ref[...] / rows + e_ref[...] / cols) - target
    parts[...] = (40.0 * dot(g.astype(BF16), images[...].reshape(ROWS, D))).reshape(GROUP, OWN_CAPS, D)
    loss = (
        jnp.sum(40.0 + jnp.log(rows), axis=0, keepdims=True) * (1.0 / GROUP)
        + jnp.sum(40.0 + jnp.log(cols), axis=1, keepdims=True) * (1.0 / RANKS)
        - 2.0 * jnp.sum(jnp.sum(s_ref[...] * target, axis=1, keepdims=True), axis=0, keepdims=True)
    )
    vec[t, :, 1536:] = jnp.broadcast_to(loss, (1, 128))


def embed_grad(parts, landed, tf, scale, w_proj, mem, back, dx2, t):
    dt = parts[t] + landed[0] + landed[1] + landed[2]
    f = tf[...]
    de = (scale[:, :1] * (dt - f * jnp.sum(f * dt, axis=-1, keepdims=True))).astype(BF16)
    own = own_member(mem, t)
    gp = dot_t(de, w_proj[...]) / counts_of(own)
    back[t, :OWN_CAPS] = de
    back[t, OWN_CAPS:] = gp.astype(BF16)
    dx2[...] = t_dot(jnp.concatenate([own, own, own], axis=0), split3(gp))


def hidden_grad(back, w_down, mem_t, dgelu, du):
    dz = back[:, OWN_CAPS:].reshape(CAPS, D)
    dh = split_rows(dot_t(dz, w_down[...]))
    for i in range(3):
        s = slice(i * TILE, i * TILE + TILE)
        du[:, s] = (dot(mem_t[...], dh[:, s]) * dgelu[:, s]).astype(BF16)


def hidden_spread(du, w_up, parts):
    parts[...] = dot_t(du[...], w_up[...]).astype(BF16).reshape(GROUP, OWN, D)


def put_halves(g, first, count, rows, values):
    for j in range(2):
        g[j, first : first + count] = values[:, j * HALF : (j + 1) * HALF].reshape(count, rows, HALF).astype(BF16)


def down_proj_grad(hsum, back, emb, proj, g, t):
    dz = back[:, OWN_CAPS:].reshape(CAPS, D)
    hs = split_rows(hsum[...])
    dz2 = jnp.concatenate([dz, dz], axis=0)
    for i in range(3):
        put_halves(g, 4 * i, 4, 64, t_dot(hs[:, i * TILE : (i + 1) * TILE], dz2))
    proj[...] = t_dot(emb[:, OWN_CAPS:].reshape(CAPS, D), back[:, :OWN_CAPS].reshape(CAPS, D)).astype(BF16).reshape(GROUP, BAND, D)
    put_halves(g, 12, 3, 64, proj[t])
    g[:, 15] = jnp.zeros((2, 64, HALF), BF16)


def up_grad(a2, du, g):
    for i in range(2):
        rows = a2[:, :, i * HALF : (i + 1) * HALF].reshape(ROWS, HALF)
        put_halves(g, 8 * i, 8, 48, t_dot(rows, du[...]))


def norm_two_grad(parts, landed, x1, gain, dx2, dx1, dy, vec, t):
    da = summed(parts, landed, t)
    n, scale = normalized(x1[...])
    vec[t, :, 768:1536] = jnp.sum(da * n, axis=0, keepdims=True)
    h = da * gain
    g = dx2[...] + (h - jnp.mean(h, axis=-1, keepdims=True) - n * jnp.mean(h * n, axis=-1, keepdims=True)) * scale
    dx1[...] = g
    dy[t] = g.astype(BF16)


def attention_grad(dy, w_out, w_t, qkv, probs, dqkv, parts):
    datt = dot_t(dy[...].reshape(ROWS, D), w_out[...]).astype(BF16)
    low = low_half()

    def scores(p, d, v):
        dp = dot_t(d, v)
        return (p * (dp - jnp.sum(p * dp, axis=-1, keepdims=True))).astype(BF16)

    for b in range(4):
        rows = slice(128 * b, 128 * b + 128)
        q, k, v = stacked(qkv[0, rows, :128], low), qkv[1, rows, :128], qkv[2, rows, :128]
        d = stacked(datt[rows, :128], low)
        p = probs[b, :256]
        ds = scores(p, d, v)
        o = dot(ds, k)
        dqkv[0, rows, :128] = (jnp.where(low, o[:128], o[128:]) * 0.125).astype(BF16)
        dqkv[1, rows, :128] = (t_dot(ds, q) * 0.125).astype(BF16)
        dqkv[2, rows, :128] = t_dot(p.astype(BF16), d).astype(BF16)
        q, k, v = qkv[0, rows, 128:], qkv[1, rows, 128:], qkv[2, rows, 128:]
        d = datt[rows, 128:]
        p = probs[b, 256:]
        ds = scores(p, d, v)
        dqkv[0, rows, 128:] = (dot(ds, k) * 0.125).astype(BF16)
        dqkv[1, rows, 128:] = (t_dot(ds, q) * 0.125).astype(BF16)
        dqkv[2, rows, 128:] = t_dot(p.astype(BF16), d).astype(BF16)
    total = dot(dqkv[0], w_t[0]) + dot(dqkv[1], w_t[1]) + dot(dqkv[2], w_t[2])
    parts[...] = total.astype(BF16).reshape(GROUP, OWN, D)


def out_qkv_grad(att, dy, dqkv, a1, g):
    put_halves(g, 0, 4, 48, t_dot(att[...], dy[...].reshape(ROWS, D)))
    for j in range(3):
        put_halves(g, 4 + 4 * j, 4, 48, t_dot(dqkv[j], a1[...].reshape(ROWS, D)))


def norm_one_grad(parts, landed, x, gain, dx1, out, vec, t):
    da = summed(parts, landed, t)
    n, scale = normalized(x[...].astype(F32))
    vec[t, :, :768] = jnp.sum(da * n, axis=0, keepdims=True)
    h = da * gain
    out[...] = dx1[...] + (h - jnp.mean(h, axis=-1, keepdims=True) - n * jnp.mean(h * n, axis=-1, keepdims=True)) * scale


class Reduction:
    def __init__(self, links, g, met, landed, full, sems):
        self.links, self.g, self.met, self.landed, self.full, self.sems = links, g, met, landed, full, sems

    def cores(self):
        other = 1 - self.links.core
        self.copies = [send(self.g.at[other], self.met, self.sems, 0, self.links.sibling())]

    def scatter(self):
        finish(self.copies)
        core = self.links.core
        self.met[...] = (self.g[core].astype(F32) + self.met[...].astype(F32)).astype(BF16)
        self.copies = [
            send(self.met.at[self.links.chip_of(k)], self.landed.at[k - 1], self.sems, k, self.links.chip_peer(k))
            for k in range(1, CHIPS)
        ]

    def gather(self):
        finish(self.copies)
        total = self.met[self.links.chip].astype(F32)
        for k in range(CHIPS - 1):
            total = total + self.landed[k].astype(F32)
        core, chip = self.links.core, self.links.chip
        self.full[core, chip] = total.astype(BF16)
        own = self.full.at[core, chip]
        self.copies = [send(own, own, self.sems, 15 + k, self.links.chip_peer(k)) for k in range(1, CHIPS)]

    def share(self):
        finish(self.copies)
        own = self.full.at[self.links.core]
        self.copies = [send(own, own, self.sems, 31, self.links.sibling())]

    def done(self):
        finish(self.copies)


def body(
    x, seg_t, pad_t, pair_in, gain_one, gain_two, img_gain_one, img_gain_two,
    h_tok, h_iqkv, h_iout, h_iup, h_idown, h_iproj, h_qkv, h_out, h_up, h_down, h_proj,
    o_loss, o_input, o_norms, o_a, o_b, o_c, o_proj,
    tok, iw_qkv, iw_out, iw_up, iw_down, iw_proj, w_qkv, w_out, w_up, w_down, w_proj, load,
    perm, back, ibias, ia, iap, iqkv, iy, ypool, ihsum, images,
    bias, mem, mem_t, pair, a1, qkv, probs, att, p_att, l_att, x1, x1_pool, a2, dgelu, hsum, p_pool, l_pool,
    tf, scale, emb, s_ref, e_ref, row_sums, col_sums, p_dt, l_dt, d_back, dx2, du, p_da2, l_da2, dx1, dy,
    dqkv, p_da1, l_da1, proj, proj_all, vec, vec_all,
    g_a, g_b, g_c, m_a, m_b, m_c, r_a, r_b, r_c, f_a, f_b, f_c,
    group_sems, rank_sems, sum_sems, proj_sems, store,
):
    links = Links()
    t, dp = links.t, links.dp
    loads = {}
    for i, (name, src, dst) in enumerate((
        ("tok", h_tok, tok), ("iqkv", h_iqkv, iw_qkv), ("qkv", h_qkv, w_qkv), ("out", h_out, w_out), ("iout", h_iout, iw_out),
        ("iup", h_iup, iw_up), ("up", h_up, w_up), ("down", h_down, w_down), ("idown", h_idown, iw_down),
        ("iproj", h_iproj, iw_proj), ("proj", h_proj, w_proj),
    )):
        loads[name] = pltpu.make_async_copy(src, dst, load.at[i])
        loads[name].start()

    links.greet()
    pair[t] = pair_in[...]
    pair_copies = group_share(links, pair, group_sems.at[0])
    text_norm_one(x, gain_one[...], a1, t)
    copies = group_share(links, a1, group_sems.at[1])

    text_masks(seg_t, pad_t, bias, mem, mem_t)
    image_masks(perm, back, ibias)
    loads["tok"].wait()
    image_norm_one(tok, img_gain_one[...], ia)
    image_permute(perm, ia, iap)
    loads["iqkv"].wait()
    image_qkv(iap, iw_qkv, iqkv)

    finish(copies)
    loads["qkv"].wait()
    loads["out"].wait()
    text_attention(a1, w_qkv, bias, w_out, qkv, probs, att, p_att)
    copies = group_scatter(links, p_att, l_att, group_sems.at[2])

    image_attention(iqkv, ibias, iap, 0, 8)

    finish(copies)
    text_norm_two(x, p_att, l_att, gain_two[...], mem, x1, a2, x1_pool, t)
    copies = group_share(links, a2, group_sems.at[3])
    text_pool_one(x1, mem, x1_pool, t)

    loads["iout"].wait()
    image_out(back, iap, ia, tok, iw_out, iy)
    image_norm_two(iy, img_gain_two[...], ia, ypool)
    loads["iup"].wait()
    image_up(ia, iw_up, ihsum, 0, 6)

    finish(copies)
    loads["up"].wait()
    loads["down"].wait()
    text_up(a2, w_up, mem, w_down, dgelu, hsum, p_pool)
    copies = group_scatter(links, p_pool, l_pool, group_sems.at[4])

    image_up(ia, iw_up, ihsum, 6, 12)
    loads["idown"].wait()
    loads["iproj"].wait()
    images[dp] = image_finish(ihsum, ypool, iw_down, iw_proj)
    image_copies = rank_share(links, images, rank_sems.at[0])

    finish(copies)
    loads["proj"].wait()
    text_embed(p_pool, l_pool, x1_pool, mem, w_proj, tf, scale, emb, t)
    finish(group_share(links, emb, group_sems.at[5]))
    finish(image_copies)
    finish(pair_copies)

    score_sums(emb, images, s_ref, e_ref, row_sums, col_sums, t, dp)
    row_copies = group_share(links, row_sums, group_sems.at[6])
    finish(rank_share(links, col_sums, rank_sems.at[1]))
    finish(row_copies)
    score_grad(s_ref, e_ref, row_sums, col_sums, pair, images, p_dt, vec, t)
    finish(group_scatter(links, p_dt, l_dt, group_sems.at[7]))
    embed_grad(p_dt, l_dt, tf, scale, w_proj, mem, d_back, dx2, t)
    finish(group_share(links, d_back, group_sems.at[8]))

    red_a = Reduction(links, g_a, m_a, r_a, f_a, sum_sems.at[0])
    red_b = Reduction(links, g_b, m_b, r_b, f_b, sum_sems.at[1])
    red_c = Reduction(links, g_c, m_c, r_c, f_c, sum_sems.at[2])

    hidden_grad(d_back, w_down, mem_t, dgelu, du)
    hidden_spread(du, w_up, p_da2)
    copies = group_scatter(links, p_da2, l_da2, group_sems.at[9])
    down_proj_grad(hsum, d_back, emb, proj, g_a, t)
    red_a.cores()
    up_grad(a2, du, g_b)
    red_b.cores()
    red_a.scatter()
    finish(copies)
    norm_two_grad(p_da2, l_da2, x1, gain_two[...], dx2, dx1, dy, vec, t)
    copies = group_share(links, dy, group_sems.at[10])
    red_b.scatter()
    finish(copies)
    attention_grad(dy, w_out, w_qkv, qkv, probs, dqkv, p_da1)
    copies = group_scatter(links, p_da1, l_da1, group_sems.at[11])
    out_qkv_grad(att, dy, dqkv, a1, g_c)
    red_c.cores()
    red_a.gather()
    red_b.gather()
    red_c.scatter()
    finish(copies)
    norm_one_grad(p_da1, l_da1, x, gain_one[...], dx1, o_input, vec, t)
    vec_copies = group_share(links, vec, group_sems.at[12])
    red_a.share()
    red_b.share()
    core = links.core
    proj_all[core, t] = f_a[core, 12:15]
    own = proj_all.at[core, t]
    proj_copies = [send(own, own, proj_sems, k, links.group_peer(k)) for k in (2, 1, 3)]
    red_c.gather()
    finish(vec_copies)
    vec_all[dp] = vec[0] + vec[1] + vec[2] + vec[3]
    vec_copies = rank_share(links, vec_all, rank_sems.at[2])
    finish(proj_copies)
    own = proj_all.at[core]
    proj_copies = [send(own, own, proj_sems, 0, links.sibling())]
    red_a.done()
    red_b.done()
    stores = [pltpu.make_async_copy(f_a, o_a, store.at[0]), pltpu.make_async_copy(f_b, o_b, store.at[1])]
    for copy in stores:
        copy.start()
    finish(vec_copies)
    total = vec_all[0]
    for i in range(1, RANKS):
        total = total + vec_all[i]
    o_norms[...] = total[:, :1536]
    o_loss[...] = total[:, 1536:] * (1.0 / 4096.0)
    finish(proj_copies)
    stores.append(pltpu.make_async_copy(proj_all, o_proj, store.at[2]))
    stores[-1].start()
    red_c.share()
    red_c.done()
    stores.append(pltpu.make_async_copy(f_c, o_c, store.at[3]))
    stores[-1].start()
    for copy in stores:
        copy.wait()


def on_device(
    text_input, segment_ids, pad_mask, pairing, ln_first, w_qkv, w_out, ln_second, w_up, w_down, text_proj,
    image_tokens, img_ln_first, img_w_qkv, img_w_out, img_ln_second, img_w_up, img_w_down, img_proj,
):
    vmem = pl.BlockSpec(memory_space=VM)
    hbm = pl.BlockSpec(memory_space=pl.ANY)
    shape = jax.ShapeDtypeStruct
    sums = ((16, 64, HALF), (16, 48, HALF), (16, 48, HALF))
    dma = pltpu.SemaphoreType.DMA
    scratch = [
        VM((IROWS, D), BF16), VM((3, D, D), BF16), VM((D, D), BF16), VM((D, FF), BF16), VM((FF, D), BF16), VM((D, D), BF16),
        VM((3, BAND, D), BF16), VM((BAND, D), BF16), VM((D, HID), BF16), VM((HID, D), BF16), VM((D, D), BF16), dma((11,)),
        VM((PROWS, IROWS), BF16), VM((IROWS, PROWS), BF16), VM((2 * PAIR, PAIR), F32), VM((IROWS, D), BF16), VM((PROWS, D), BF16),
        VM((3, PROWS, D), BF16), VM((IROWS, D), F32), VM((IMGS, D), F32),
        VM((IMGS, FF), F32), VM((RANKS, IMGS, D), BF16),
        VM((4, 128, 128), F32), VM((CAPS, ROWS), BF16), VM((ROWS, 128), BF16), VM((GROUP, OWN_CAPS, 128), I32),
        VM((GROUP, OWN, D), BF16), VM((3, ROWS, BAND), BF16), VM((4, HALF, 128), F32), VM((ROWS, BAND), BF16),
        VM((GROUP, OWN, D), BF16), VM((3, OWN, D), BF16), VM((OWN, D), F32), VM((OWN_CAPS, D), F32), VM((GROUP, OWN, D), BF16),
        VM((ROWS, HID), F32), VM((CAPS, HID), F32), VM((GROUP, OWN_CAPS, D), F32), VM((3, OWN_CAPS, D), F32),
        VM((OWN_CAPS, D), F32), VM((OWN_CAPS, 128), F32), VM((GROUP, 2 * OWN_CAPS, D), BF16), VM((CAPS, ROWS), F32),
        VM((CAPS, ROWS), F32), VM((GROUP, CAPS, 128), F32), VM((RANKS, 1, ROWS), F32), VM((GROUP, OWN_CAPS, D), F32),
        VM((3, OWN_CAPS, D), F32), VM((GROUP, 2 * OWN_CAPS, D), BF16),
        VM((OWN, D), F32), VM((ROWS, HID), BF16), VM((GROUP, OWN, D), BF16), VM((3, OWN, D), BF16), VM((OWN, D), F32),
        VM((GROUP, OWN, D), BF16), VM((3, ROWS, BAND), BF16), VM((GROUP, OWN, D), BF16), VM((3, OWN, D), BF16),
        VM((GROUP, BAND, D), BF16), VM((2, GROUP, 3, 64, HALF), BF16), VM((GROUP, 1, VEC), F32), VM((RANKS, 1, VEC), F32),
    ]
    scratch += [VM((2,) + s, BF16) for s in sums] + [VM(s, BF16) for s in sums]
    scratch += [VM((15,) + s[1:], BF16) for s in sums] + [VM((2,) + s, BF16) for s in sums]
    scratch += [dma((13, 2, 3)), dma((3, 2, 31)), dma((3, 2, 32)), dma((2, 4)), dma((4,))]
    loss, input_grad, norms, full_a, full_b, full_c, full_proj = pl.pallas_call(
        body,
        out_shape=(
            shape((1, 128), F32), shape((OWN, D), F32), shape((1, 1536), F32),
            *(shape((2,) + s, BF16) for s in sums), shape((2, GROUP, 3, 64, HALF), BF16),
        ),
        in_specs=[vmem] * 8 + [hbm] * 11,
        out_specs=(vmem, vmem, vmem, hbm, hbm, hbm, hbm),
        scratch_shapes=scratch,
        compiler_params=pltpu.CompilerParams(collective_id=0, has_side_effects=True, vmem_limit_bytes=63 << 20),
        name="lit",
    )(
        text_input, segment_ids.T, pad_mask.T, jnp.broadcast_to(pairing[:, None], (OWN_CAPS, 128)),
        ln_first[None], ln_second[None], img_ln_first[None], img_ln_second[None],
        image_tokens.transpose(1, 0, 2).reshape(IROWS, D), img_w_qkv, img_w_out, img_w_up, img_w_down, img_proj,
        w_qkv.swapaxes(1, 2), w_out, w_up, w_down, text_proj,
    )

    def wide(full, first, last):
        rows = (last - first) * full.shape[2]
        return jnp.concatenate([full[j, first:last].reshape(rows, HALF) for j in range(2)], axis=1).astype(F32)

    proj = jnp.concatenate([full_proj[j].reshape(D, HALF) for j in range(2)], axis=1).astype(F32)
    qkv = wide(full_c, 4, 16).reshape(3, BAND, D).swapaxes(1, 2)
    return (
        loss[0, 0], input_grad, norms[0, :D], qkv, wide(full_c, 0, 4), norms[0, D:], wide(full_b, 0, 16),
        wide(full_a, 0, 12), proj,
    )


def solution(mesh):
    rows = P(("dp", "tensor"))
    in_specs = (
        P(("dp", "tensor"), None), P("dp", None), P("dp", None), rows, P(), P(None, None, "tensor"), P("tensor", None), P(),
        P(None, "tensor"), P("tensor", None), P(), P(("dp", "tensor"), None, None), P(), P(), P(), P(), P(), P(), P(),
    )
    out_specs = (
        P(), P(("dp", "tensor"), None), P(), P(None, None, "tensor"), P("tensor", None), P(), P(None, "tensor"),
        P("tensor", None), P(),
    )
    return jax.shard_map(on_device, mesh=mesh, in_specs=in_specs, out_specs=out_specs, check_vma=False)
```

time: 738 us -> 173 us (0.23)
  waiting for transfers between devices: 358 us -> 0 us
  blocking collectives: 175 us -> 0 us
  Pallas kernels: 0 us -> 155 us
  matrix products: 96.5 us -> 0 us
  other arithmetic: 40.3 us -> 6.3 us
  local copies, waits for them, and re-layouts: 41.9 us -> 10.3 us
  between operations: 20.6 us -> 1.91 us
    psum x2 -> x0, waiting for transfers between devices: 194 us -> none  [the longest x1 149 us: on_device(): lax.psum((loss_part, grad_ln_first, grad_ln_second, proj_part), ('dp', 't...]
    pallas_call x0 -> x1, Pallas kernels: none -> 155 us  [on_device(): pl.pallas_call(body, out_shape=(shape((1, 128), F32), shape((OWN, D), F32...]
    all_gather x2 -> x0, waiting for transfers between devices: 131 us -> none  [the longest x1 69.1 us: on_device(): lax.all_gather(image_rows, ('dp', 'tensor'), axis=0, tiled=True)]
    dot_general x31 -> x0, matrix products: 94.4 us -> none  [the longest x1 31.8 us: image_tower(): jnp.dot(hidden, w_lower, preferred_element_type=jnp.float32)]
    psum x1 -> x0, blocking collectives: 66.3 us -> none  [on_device(): lax.psum((loss_part, grad_ln_first, grad_ln_second, proj_part), ('dp', 't...]
    unnamed x1 -> x0, blocking collectives: 62.3 us -> none
    all_gather x4 -> x0, blocking collectives: 46.6 us -> none  [the longest x1 13.3 us: on_device(): lax.all_gather(lowered(layer_norm(stream, ln_first)), 'tensor', axis=0, t...]
    reduce_scatter x4 -> x0, waiting for transfers between devices: 33.3 us -> none  [the longest x1 20.3 us: on_device(): lax.psum_scatter(jnp.einsum('rf,df->rd', piece, w_up, preferred_element_t...]
  transfers between devices with their start and end apart: 8 -> 0, of which waited for: 6 -> 0; matrix products, arithmetic and copies ran while one was open for 16% -> 0% of each run, Pallas kernels for 0% -> 0%
where the time goes in v1:
time: 173 us
  Pallas kernels  155 us (90%)
  local copies, waits for them, and re-layouts  10.3 us (6%)
  other arithmetic  6.3 us (4%)
  between operations  1.91 us (1%)
    pallas_call x1, Pallas kernels, on_device(): pl.pallas_call(body, out_shape=(shape((1, 128), F32), shape((OWN, D), F32...  155 us

profile of v1, /device:TPU:1, one launch (start us, length us, event | category | flops | bytes accessed | tf_op | source)
XLA Modules:
  0.0 173.0 jit_solution(4927620441753759783)
XLA Ops:
  0.6 1.3 broadcast_in_dim.18.pair_in
  2.0 1.3 broadcast_in_dim.19.gain_one
  3.2 1.3 broadcast_in_dim.20.gain_two
  4.5 1.3 broadcast_in_dim.21.img_gain_one
  5.8 1.3 broadcast_in_dim.22.img_gain_two
  7.0 154.6 %lit.1 = (f32[1,128]{1,0:T(1,128)}, f32[128,768]{1,0:T(8,128)}, f32[1,1536]{1,0:T(1,128)}, bf16[2,16,64,384]{3,2,1,0:T(8,128)(2,1)}, bf16[2,16,48,384]{3,2,1,0:T...) custom-call(bf16[128,768]{1,0:T(8,128)(2,1)} %x.1, s32[16,32]{1,0:T(8,128)} %bitcast.32, ...), custom_call_target="tpu_custom_call" | custom-call | tf_op jit(solution)/shard_map/lit/pallas_call | solution.py:696
  161.6 0.0 copy-start.2
  161.6 1.5 fusion.2
  163.1 0.3 copy-done.2
  163.4 0.1 fusion
  163.5 0.0 copy-start
  163.5 2.5 %maximum_convert_fusion = (f32[768,768]{1,0:T(8,128)}, f32[768,768]{1,0:T(8,128)}) fusion(bf16[768,384]{1,0:T(8,128)(2,1)S(1)} %bitcast.21, bf16[768,384]{1,0:T(8,128)(2,1)S(1)} %bitcast.20, bf16[768,384]{1,0:T(8,128)(2,1)S(1)} %bitcast.23, bf16[768,384]{1,0:T(8,128)(2,1)S(1)} %bitcast.22), kind=kLoop, calls=%fused_computation.1 | loop fusion | flops 4718592 | bytes 7077888 | tf_op jit(solution)/shard_map/convert_element_type | solution.py:716
  166.0 0.0 copy-done
  166.1 0.9 maximum_convert_fusion.3
  166.9 0.1 fusion.4
  167.0 0.0 copy-start.1
  167.0 1.3 convert_bitcast_fusion
  168.4 0.4 copy-done.1
  168.8 0.1 fusion.1
  168.9 0.0 copy-start.4
  168.9 0.0 copy-start.5
  168.9 0.0 copy-start.3
  168.9 1.6 maximum_convert_fusion.2
  170.5 0.0 copy-done.4
  170.5 0.6 slice_reduce_fusion
  171.1 0.0 copy-done.5
  171.2 0.0 copy-done.3
  171.2 0.7 copy.31
  (1 shorter events, 0.0 us)
Async XLA Ops:
  161.6 1.8 %copy-start.2 = (bf16[2,16,64,384]{3,2,1,0:T(8,128)(2,1)S(1)}, bf16[2,16,64,384]{3,2,1,0:T(8,128)(2,1)}, u32[]{:S(2)}) copy-start(bf16[2,16,64,384]{3,2,1,0:T(8,128)(2,1)} %get-tuple-element.21) | copy-start | bytes 4718596
  163.5 2.5 %copy-start = (bf16[2,16,48,384]{3,2,1,0:T(8,128)(2,1)S(1)}, bf16[2,16,48,384]{3,2,1,0:T(8,128)(2,1)}, u32[]{:S(2)}) copy-start(bf16[2,16,48,384]{3,2,1,0:T(8,128)(2,1)} %get-tuple-element.19) | copy-start | bytes 3538948
  167.0 1.7 %copy-start.1 = (bf16[2,4,3,64,384]{4,3,2,1,0:T(8,128)(2,1)S(1)}, bf16[2,4,3,64,384]{4,3,2,1,0:T(8,128)(2,1)}, u32[]{:S(2)}) copy-start(bf16[2,4,3,64,384]{4,3,2,1,0:T(8,128)(2,1)} %get-tuple-element.22) | copy-start | bytes 3538948
  168.9 1.6 copy-start.4
  168.9 2.2 %copy-start.5 = (f32[1,128]{1,0:T(1,128)S(1)}, f32[1,128]{1,0:T(1,128)}, u32[]{:S(2)}) copy-start(f32[1,128]{1,0:T(1,128)} %get-tuple-element.16) | copy-start | bytes 1540
  168.9 2.2 %copy-start.3 = (f32[128,768]{1,0:T(8,128)S(1)}, f32[128,768]{1,0:T(8,128)}, u32[]{:S(2)}) copy-start(f32[128,768]{1,0:T(8,128)} %get-tuple-element.47) | copy-start | bytes 1179652

commit v2 on v1

--- a/solution.py
+++ b/solution.py
@@ -160,6 +160,18 @@
     lax.fori_loop(first, last, step, 0)
 
 
+def as_row(gain):
+    return gain[...].reshape(1, D)
+
+
+def column(values):
+    rows = iota((OWN_CAPS, 128), 0)
+    out = jnp.zeros((OWN_CAPS, 128), I32)
+    for i in range(OWN_CAPS):
+        out = jnp.where(rows == i, values[i], out)
+    return out
+
+
 def split_rows(x):
     hi = x.astype(BF16)
     return jnp.concatenate([hi, (x - hi.astype(F32)).astype(BF16)], axis=0)
@@ -185,6 +197,7 @@
     def __init__(self):
         self.dp, self.t = lax.axis_index("dp"), lax.axis_index("tensor")
         self.core, self.chip = lax.rem(self.dp, 2), self.dp // 2
+        self.place = {"x": lax.rem(self.chip, 4), "z": self.chip // 4}
 
     def rank(self, k):
         return lax.rem(self.t + k, GROUP)
@@ -200,6 +213,14 @@
 
     def chip_peer(self, k):
         return {"dp": 2 * self.chip_of(k) + self.core, "tensor": self.t}
+
+    def axis_rank(self, axis, k):
+        return lax.rem(self.place[axis] + k, 4)
+
+    def axis_peer(self, axis, k):
+        place = dict(self.place)
+        place[axis] = self.axis_rank(axis, k)
+        return {"dp": 2 * (place["z"] * 4 + place["x"]) + self.core, "tensor": self.t}
 
     def sibling(self):
         return {"dp": self.dp + 1 - 2 * self.core, "tensor": self.t}
@@ -346,20 +367,20 @@
     return jnp.sum(mem.astype(F32), axis=1, keepdims=True)
 
 
-def text_embed(parts, landed, x1_pool, mem, w_proj, tf, scale, emb, t):
+def text_pool(parts, landed, x1_pool, mem, pooled, t):
     total = x1_pool[...] + parts[t] + landed[0] + landed[1] + landed[2]
-    pooled = (total / counts_of(own_member(mem, t))).astype(BF16)
-    e = dot(pooled, w_proj[...])
+    pooled[t] = (total / counts_of(own_member(mem, t))).astype(BF16)
+
+
+def text_embed(pooled, w_proj, tf, scale):
+    e = dot(pooled[...].reshape(CAPS, D), w_proj[...])
     rs = lax.rsqrt(jnp.sum(e * e, axis=-1, keepdims=True) + EPS)
     tf[...] = rs * e
-    scale[...] = jnp.broadcast_to(rs, (OWN_CAPS, 128))
-    emb[t, :OWN_CAPS] = (rs * e).astype(BF16)
-    emb[t, OWN_CAPS:] = pooled
-
-
-def score_sums(emb, images, s_ref, e_ref, row_sums, col_sums, t, dp):
-    text = emb[:, :OWN_CAPS].reshape(CAPS, D)
-    s = 40.0 * dot_t(text, images[...].reshape(ROWS, D))
+    scale[...] = jnp.broadcast_to(rs, (CAPS, 128))
+
+
+def score_sums(tf, images, s_ref, e_ref, row_sums, col_sums, t, dp):
+    s = 40.0 * dot_t(tf[...].astype(BF16), images[...].reshape(ROWS, D))
     s_ref[...] = s
     e = jnp.exp(s - 40.0)
     e_ref[...] = e
@@ -367,15 +388,16 @@
     col_sums[dp] = jnp.sum(e, axis=0, keepdims=True)
 
 
-def score_grad(s_ref, e_ref, row_sums, col_sums, pair, images, parts, vec, t):
+def score_grad(s_ref, e_ref, row_sums, col_sums, pair, images, dts, vec, t):
     rows = jnp.sum(row_sums[...], axis=0)[:, :1]
     cols = col_sums[0]
     for i in range(1, RANKS):
         cols = cols + col_sums[i]
     lane = iota((CAPS, ROWS), 1)
-    target = jnp.where(pair[...].reshape(CAPS, 128)[:, :1] == (lane >> 4) * CAPS + OWN_CAPS * t + (lane & 15), 1.0, 0.0)
+    image = ((lane >> 4) & 15) * (2 * CAPS) + (lane >> 8) * CAPS + (lane & 15) + OWN_CAPS * t
+    target = jnp.where(pair[...].reshape(CAPS, 128)[:, :1] == image, 1.0, 0.0)
     g = 0.5 * (e_ref[...] / rows + e_ref[...] / cols) - target
-    parts[...] = (40.0 * dot(g.astype(BF16), images[...].reshape(ROWS, D))).reshape(GROUP, OWN_CAPS, D)
+    dts[t] = (40.0 * dot(g.astype(BF16), images[...].reshape(ROWS, D))).astype(BF16)
     loss = (
         jnp.sum(40.0 + jnp.log(rows), axis=0, keepdims=True) * (1.0 / GROUP)
         + jnp.sum(40.0 + jnp.log(cols), axis=1, keepdims=True) * (1.0 / RANKS)
@@ -384,20 +406,24 @@
     vec[t, :, 1536:] = jnp.broadcast_to(loss, (1, 128))
 
 
-def embed_grad(parts, landed, tf, scale, w_proj, mem, back, dx2, t):
-    dt = parts[t] + landed[0] + landed[1] + landed[2]
+def embed_grad(dts, tf, scale, w_proj, mem, de_ref, dz_ref, gp_ref):
+    dt = dts[0].astype(F32) + dts[1].astype(F32) + dts[2].astype(F32) + dts[3].astype(F32)
     f = tf[...]
     de = (scale[:, :1] * (dt - f * jnp.sum(f * dt, axis=-1, keepdims=True))).astype(BF16)
+    gp = dot_t(de, w_proj[...]) / counts_of(mem[...])
+    de_ref[...] = de
+    gp_ref[...] = gp
+    dz_ref[...] = gp.astype(BF16)
+
+
+def row_grad(gp_ref, mem, dx2, t):
     own = own_member(mem, t)
-    gp = dot_t(de, w_proj[...]) / counts_of(own)
-    back[t, :OWN_CAPS] = de
-    back[t, OWN_CAPS:] = gp.astype(BF16)
+    gp = gp_ref[pl.ds(pl.multiple_of(t * OWN_CAPS, OWN_CAPS), OWN_CAPS), :]
     dx2[...] = t_dot(jnp.concatenate([own, own, own], axis=0), split3(gp))
 
 
-def hidden_grad(back, w_down, mem_t, dgelu, du):
-    dz = back[:, OWN_CAPS:].reshape(CAPS, D)
-    dh = split_rows(dot_t(dz, w_down[...]))
+def hidden_grad(dz, w_down, mem_t, dgelu, du):
+    dh = split_rows(dot_t(dz[...], w_down[...]))
     for i in range(3):
         s = slice(i * TILE, i * TILE + TILE)
         du[:, s] = (dot(mem_t[...], dh[:, s]) * dgelu[:, s]).astype(BF16)
@@ -409,18 +435,23 @@
 
 def put_halves(g, first, count, rows, values):
     for j in range(2):
-        g[j, first : first + count] = values[:, j * HALF : (j + 1) * HALF].reshape(count, rows, HALF).astype(BF16)
-
-
-def down_proj_grad(hsum, back, emb, proj, g, t):
-    dz = back[:, OWN_CAPS:].reshape(CAPS, D)
+        part = values[:, j * HALF : (j + 1) * HALF].reshape(count, rows, HALF).astype(BF16)
+        if len(g.shape) == 4:
+            g[j, first : first + count] = part
+        elif count == 3:
+            g[j, first // 4, :3] = part
+        else:
+            g[j, first // 4 : (first + count) // 4] = part.reshape(count // 4, 4, rows, HALF)
+
+
+def down_proj_grad(hsum, dz, de, pooled, proj, g, t):
     hs = split_rows(hsum[...])
-    dz2 = jnp.concatenate([dz, dz], axis=0)
+    dz2 = jnp.concatenate([dz[...], dz[...]], axis=0)
     for i in range(3):
         put_halves(g, 4 * i, 4, 64, t_dot(hs[:, i * TILE : (i + 1) * TILE], dz2))
-    proj[...] = t_dot(emb[:, OWN_CAPS:].reshape(CAPS, D), back[:, :OWN_CAPS].reshape(CAPS, D)).astype(BF16).reshape(GROUP, BAND, D)
+    proj[...] = t_dot(pooled[...].reshape(CAPS, D), de[...]).astype(BF16).reshape(GROUP, BAND, D)
     put_halves(g, 12, 3, 64, proj[t])
-    g[:, 15] = jnp.zeros((2, 64, HALF), BF16)
+    g[:, 3, 3] = jnp.zeros((2, 64, HALF), BF16)
 
 
 def up_grad(a2, du, g):
@@ -490,10 +521,12 @@
         other = 1 - self.links.core
         self.copies = [send(self.g.at[other], self.met, self.sems, 0, self.links.sibling())]
 
+    def both_cores(self):
+        finish(self.copies)
+        self.met[...] = (self.g[self.links.core].astype(F32) + self.met[...].astype(F32)).astype(BF16)
+
     def scatter(self):
-        finish(self.copies)
-        core = self.links.core
-        self.met[...] = (self.g[core].astype(F32) + self.met[...].astype(F32)).astype(BF16)
+        self.both_cores()
         self.copies = [
             send(self.met.at[self.links.chip_of(k)], self.landed.at[k - 1], self.sems, k, self.links.chip_peer(k))
             for k in range(1, CHIPS)
@@ -518,6 +551,47 @@
         finish(self.copies)
 
 
+class TwoAxes(Reduction):
+    def __init__(self, links, g, met, landed, near, full, sems, first, second):
+        super().__init__(links, g, met, landed, full, sems)
+        self.near, self.first, self.second = near, first, second
+        self.i, self.j = links.place[first], links.place[second]
+
+    def scatter(self):
+        self.both_cores()
+        rank, peer = self.links.axis_rank, self.links.axis_peer
+        self.copies = [
+            send(self.met.at[rank(self.first, k)], self.landed.at[k - 1], self.sems, k, peer(self.first, k)) for k in (2, 1, 3)
+        ]
+
+    def scatter_second(self):
+        finish(self.copies)
+        total = self.met[self.i].astype(F32)
+        for k in range(3):
+            total = total + self.landed[k].astype(F32)
+        self.met[self.i] = total.astype(BF16)
+        rank, peer = self.links.axis_rank, self.links.axis_peer
+        self.copies = [
+            send(self.met.at[self.i, rank(self.second, k)], self.near.at[k - 1], self.sems, 3 + k, peer(self.second, k))
+            for k in (2, 1, 3)
+        ]
+
+    def gather(self):
+        finish(self.copies)
+        total = self.met[self.i, self.j].astype(F32)
+        for k in range(3):
+            total = total + self.near[k].astype(F32)
+        core = self.links.core
+        self.full[core, self.i, self.j] = total.astype(BF16)
+        own = self.full.at[core, self.i, self.j]
+        self.copies = [send(own, own, self.sems, 6 + k, self.links.axis_peer(self.second, k)) for k in (2, 1, 3)]
+
+    def gather_second(self):
+        finish(self.copies)
+        own = self.full.at[self.links.core, self.i]
+        self.copies = [send(own, own, self.sems, 9 + k, self.links.axis_peer(self.first, k)) for k in (2, 1, 3)]
+
+
 def body(
     x, seg_t, pad_t, pair_in, gain_one, gain_two, img_gain_one, img_gain_two,
     h_tok, h_iqkv, h_iout, h_iup, h_idown, h_iproj, h_qkv, h_out, h_up, h_down, h_proj,
@@ -525,10 +599,10 @@
     tok, iw_qkv, iw_out, iw_up, iw_down, iw_proj, w_qkv, w_out, w_up, w_down, w_proj, load,
     perm, back, ibias, ia, iap, iqkv, iy, ypool, ihsum, images,
     bias, mem, mem_t, pair, a1, qkv, probs, att, p_att, l_att, x1, x1_pool, a2, dgelu, hsum, p_pool, l_pool,
-    tf, scale, emb, s_ref, e_ref, row_sums, col_sums, p_dt, l_dt, d_back, dx2, du, p_da2, l_da2, dx1, dy,
+    tf, scale, pooled, s_ref, e_ref, row_sums, col_sums, dts, de, dz, gp, dx2, du, p_da2, l_da2, dx1, dy,
     dqkv, p_da1, l_da1, proj, proj_all, vec, vec_all,
-    g_a, g_b, g_c, m_a, m_b, m_c, r_a, r_b, r_c, f_a, f_b, f_c,
-    group_sems, rank_sems, sum_sems, proj_sems, store,
+    g_a, g_b, g_c, m_a, m_b, m_c, r_a, r_b, r_c, n_a, n_b, f_a, f_b, f_c,
+    group_sems, image_sems, rank_sems, sum_sems, proj_sems, store,
 ):
     links = Links()
     t, dp = links.t, links.dp
@@ -542,15 +616,15 @@
         loads[name].start()
 
     links.greet()
-    pair[t] = pair_in[...]
+    pair[t] = column(pair_in)
     pair_copies = group_share(links, pair, group_sems.at[0])
-    text_norm_one(x, gain_one[...], a1, t)
+    text_norm_one(x, as_row(gain_one), a1, t)
     copies = group_share(links, a1, group_sems.at[1])
 
     text_masks(seg_t, pad_t, bias, mem, mem_t)
     image_masks(perm, back, ibias)
     loads["tok"].wait()
-    image_norm_one(tok, img_gain_one[...], ia)
+    image_norm_one(tok, as_row(img_gain_one), ia)
     image_permute(perm, ia, iap)
     loads["iqkv"].wait()
     image_qkv(iap, iw_qkv, iqkv)
@@ -564,13 +638,13 @@
     image_attention(iqkv, ibias, iap, 0, 8)
 
     finish(copies)
-    text_norm_two(x, p_att, l_att, gain_two[...], mem, x1, a2, x1_pool, t)
+    text_norm_two(x, p_att, l_att, as_row(gain_two), mem, x1, a2, x1_pool, t)
     copies = group_share(links, a2, group_sems.at[3])
     text_pool_one(x1, mem, x1_pool, t)
 
     loads["iout"].wait()
     image_out(back, iap, ia, tok, iw_out, iy)
-    image_norm_two(iy, img_gain_two[...], ia, ypool)
+    image_norm_two(iy, as_row(img_gain_two), ia, ypool)
     loads["iup"].wait()
     image_up(ia, iw_up, ihsum, 0, 6)
 
@@ -580,65 +654,78 @@
     text_up(a2, w_up, mem, w_down, dgelu, hsum, p_pool)
     copies = group_scatter(links, p_pool, l_pool, group_sems.at[4])
 
-    image_up(ia, iw_up, ihsum, 6, 12)
+    image_up(ia, iw_up, ihsum, 6, 10)
+    finish(copies)
+    text_pool(p_pool, l_pool, x1_pool, mem, pooled, t)
+    copies = group_share(links, pooled, group_sems.at[5])
+
+    image_up(ia, iw_up, ihsum, 10, 12)
     loads["idown"].wait()
     loads["iproj"].wait()
-    images[dp] = image_finish(ihsum, ypool, iw_down, iw_proj)
-    image_copies = rank_share(links, images, rank_sems.at[0])
+    core, chip = links.core, links.chip
+    images[core, chip] = image_finish(ihsum, ypool, iw_down, iw_proj)
+    own = images.at[core, chip]
+    image_copies = [send(own, own, image_sems, k, links.chip_peer(k)) for k in range(1, CHIPS)]
 
     finish(copies)
     loads["proj"].wait()
-    text_embed(p_pool, l_pool, x1_pool, mem, w_proj, tf, scale, emb, t)
-    finish(group_share(links, emb, group_sems.at[5]))
+    text_embed(pooled, w_proj, tf, scale)
     finish(image_copies)
+    own = images.at[core]
+    image_copies = [send(own, own, image_sems, 0, links.sibling())]
     finish(pair_copies)
-
-    score_sums(emb, images, s_ref, e_ref, row_sums, col_sums, t, dp)
+    finish(image_copies)
+
+    score_sums(tf, images, s_ref, e_ref, row_sums, col_sums, t, dp)
+    col_copies = rank_share(links, col_sums, rank_sems.at[0])
     row_copies = group_share(links, row_sums, group_sems.at[6])
-    finish(rank_share(links, col_sums, rank_sems.at[1]))
+    finish(col_copies)
     finish(row_copies)
-    score_grad(s_ref, e_ref, row_sums, col_sums, pair, images, p_dt, vec, t)
-    finish(group_scatter(links, p_dt, l_dt, group_sems.at[7]))
-    embed_grad(p_dt, l_dt, tf, scale, w_proj, mem, d_back, dx2, t)
-    finish(group_share(links, d_back, group_sems.at[8]))
-
-    red_a = Reduction(links, g_a, m_a, r_a, f_a, sum_sems.at[0])
-    red_b = Reduction(links, g_b, m_b, r_b, f_b, sum_sems.at[1])
+    score_grad(s_ref, e_ref, row_sums, col_sums, pair, images, dts, vec, t)
+    finish(group_share(links, dts, group_sems.at[7]))
+    embed_grad(dts, tf, scale, w_proj, mem, de, dz, gp)
+
+    red_a = TwoAxes(links, g_a, m_a, r_a, n_a, f_a, sum_sems.at[0], "x", "z")
+    red_b = TwoAxes(links, g_b, m_b, r_b, n_b, f_b, sum_sems.at[1], "z", "x")
     red_c = Reduction(links, g_c, m_c, r_c, f_c, sum_sems.at[2])
 
-    hidden_grad(d_back, w_down, mem_t, dgelu, du)
+    hidden_grad(dz, w_down, mem_t, dgelu, du)
     hidden_spread(du, w_up, p_da2)
-    copies = group_scatter(links, p_da2, l_da2, group_sems.at[9])
-    down_proj_grad(hsum, d_back, emb, proj, g_a, t)
+    copies = group_scatter(links, p_da2, l_da2, group_sems.at[8])
+    down_proj_grad(hsum, dz, de, pooled, proj, g_a, t)
     red_a.cores()
+    row_grad(gp, mem, dx2, t)
     up_grad(a2, du, g_b)
     red_b.cores()
     red_a.scatter()
-    finish(copies)
-    norm_two_grad(p_da2, l_da2, x1, gain_two[...], dx2, dx1, dy, vec, t)
-    copies = group_share(links, dy, group_sems.at[10])
     red_b.scatter()
     finish(copies)
+    norm_two_grad(p_da2, l_da2, x1, as_row(gain_two), dx2, dx1, dy, vec, t)
+    copies = group_share(links, dy, group_sems.at[9])
+    red_a.scatter_second()
+    red_b.scatter_second()
+    red_a.gather()
+    red_b.gather()
+    finish(copies)
     attention_grad(dy, w_out, w_qkv, qkv, probs, dqkv, p_da1)
-    copies = group_scatter(links, p_da1, l_da1, group_sems.at[11])
+    copies = group_scatter(links, p_da1, l_da1, group_sems.at[10])
     out_qkv_grad(att, dy, dqkv, a1, g_c)
     red_c.cores()
-    red_a.gather()
-    red_b.gather()
+    red_a.gather_second()
+    red_b.gather_second()
     red_c.scatter()
     finish(copies)
-    norm_one_grad(p_da1, l_da1, x, gain_one[...], dx1, o_input, vec, t)
-    vec_copies = group_share(links, vec, group_sems.at[12])
+    norm_one_grad(p_da1, l_da1, x, as_row(gain_one), dx1, o_input, vec, t)
+    vec_copies = group_share(links, vec, group_sems.at[11])
     red_a.share()
     red_b.share()
-    core = links.core
-    proj_all[core, t] = f_a[core, 12:15]
+    proj_all[core, t] = f_a[core, 3, :3]
     own = proj_all.at[core, t]
     proj_copies = [send(own, own, proj_sems, k, links.group_peer(k)) for k in (2, 1, 3)]
-    red_c.gather()
     finish(vec_copies)
     vec_all[dp] = vec[0] + vec[1] + vec[2] + vec[3]
-    vec_copies = rank_share(links, vec_all, rank_sems.at[2])
+    vec_copies = rank_share(links, vec_all, rank_sems.at[1])
+    red_c.gather()
     finish(proj_copies)
     own = proj_all.at[core]
     proj_copies = [send(own, own, proj_sems, 0, links.sibling())]
@@ -664,6 +751,48 @@
         copy.wait()
 
 
+def widen(
+    loss, norms, h_input, h_a, h_b, h_c, h_proj,
+    o_loss, o_input, o_one, o_two, o_down, o_up, o_out, o_qkv, o_proj,
+    grad, full_a, full_b, full_c, full_proj, down, up, out, qkv, proj, loaded, stored,
+):
+    sources = ((h_a, full_a), (h_b, full_b), (h_proj, full_proj), (h_c, full_c), (h_input, grad))
+    loads = [pltpu.make_async_copy(src, dst, loaded.at[i]) for i, (src, dst) in enumerate(sources)]
+    for copy in loads:
+        copy.start()
+    stores = []
+
+    def write(buf, target):
+        stores.append(pltpu.make_async_copy(buf, target, stored.at[len(stores)]))
+        stores[-1].start()
+
+    def halves(target, parts, rows):
+        for j in range(2):
+            target[:, j * HALF : (j + 1) * HALF] = parts[j].reshape(rows, HALF).astype(F32)
+
+    loads[0].wait()
+    halves(down, full_a[:, :3], HID)
+    write(down, o_down)
+    loads[1].wait()
+    halves(up, full_b, D)
+    write(up, o_up)
+    loads[2].wait()
+    halves(proj, full_proj, D)
+    write(proj, o_proj)
+    loads[3].wait()
+    halves(out, full_c[:, :4], BAND)
+    write(out, o_out)
+    halves(qkv, full_c[:, 4:], 3 * BAND)
+    write(qkv, o_qkv)
+    loads[4].wait()
+    write(grad, o_input)
+    o_loss[0, 0] = loss[0, 0]
+    o_one[...] = norms[:, :D].reshape(D)
+    o_two[...] = norms[:, D:].reshape(D)
+    for copy in stores:
+        copy.wait()
+
+
 def on_device(
     text_input, segment_ids, pad_mask, pairing, ln_first, w_qkv, w_out, ln_second, w_up, w_down, text_proj,
     image_tokens, img_ln_first, img_w_qkv, img_w_out, img_ln_second, img_w_up, img_w_down, img_proj,
@@ -671,56 +800,63 @@
     vmem = pl.BlockSpec(memory_space=VM)
     hbm = pl.BlockSpec(memory_space=pl.ANY)
     shape = jax.ShapeDtypeStruct
-    sums = ((16, 64, HALF), (16, 48, HALF), (16, 48, HALF))
+    sums = ((4, 4, 64, HALF), (4, 4, 48, HALF), (16, 48, HALF))
     dma = pltpu.SemaphoreType.DMA
     scratch = [
         VM((IROWS, D), BF16), VM((3, D, D), BF16), VM((D, D), BF16), VM((D, FF), BF16), VM((FF, D), BF16), VM((D, D), BF16),
         VM((3, BAND, D), BF16), VM((BAND, D), BF16), VM((D, HID), BF16), VM((HID, D), BF16), VM((D, D), BF16), dma((11,)),
         VM((PROWS, IROWS), BF16), VM((IROWS, PROWS), BF16), VM((2 * PAIR, PAIR), F32), VM((IROWS, D), BF16), VM((PROWS, D), BF16),
         VM((3, PROWS, D), BF16), VM((IROWS, D), F32), VM((IMGS, D), F32),
-        VM((IMGS, FF), F32), VM((RANKS, IMGS, D), BF16),
+        VM((IMGS, FF), F32), VM((2, CHIPS, IMGS, D), BF16),
         VM((4, 128, 128), F32), VM((CAPS, ROWS), BF16), VM((ROWS, 128), BF16), VM((GROUP, OWN_CAPS, 128), I32),
         VM((GROUP, OWN, D), BF16), VM((3, ROWS, BAND), BF16), VM((4, HALF, 128), F32), VM((ROWS, BAND), BF16),
         VM((GROUP, OWN, D), BF16), VM((3, OWN, D), BF16), VM((OWN, D), F32), VM((OWN_CAPS, D), F32), VM((GROUP, OWN, D), BF16),
         VM((ROWS, HID), F32), VM((CAPS, HID), F32), VM((GROUP, OWN_CAPS, D), F32), VM((3, OWN_CAPS, D), F32),
-        VM((OWN_CAPS, D), F32), VM((OWN_CAPS, 128), F32), VM((GROUP, 2 * OWN_CAPS, D), BF16), VM((CAPS, ROWS), F32),
-        VM((CAPS, ROWS), F32), VM((GROUP, CAPS, 128), F32), VM((RANKS, 1, ROWS), F32), VM((GROUP, OWN_CAPS, D), F32),
-        VM((3, OWN_CAPS, D), F32), VM((GROUP, 2 * OWN_CAPS, D), BF16),
+        VM((CAPS, D), F32), VM((CAPS, 128), F32), VM((GROUP, OWN_CAPS, D), BF16), VM((CAPS, ROWS), F32),
+        VM((CAPS, ROWS), F32), VM((GROUP, CAPS, 128), F32), VM((RANKS, 1, ROWS), F32), VM((GROUP, CAPS, D), BF16),
+        VM((CAPS, D), BF16), VM((CAPS, D), BF16), VM((CAPS, D), F32),
         VM((OWN, D), F32), VM((ROWS, HID), BF16), VM((GROUP, OWN, D), BF16), VM((3, OWN, D), BF16), VM((OWN, D), F32),
         VM((GROUP, OWN, D), BF16), VM((3, ROWS, BAND), BF16), VM((GROUP, OWN, D), BF16), VM((3, OWN, D), BF16),
         VM((GROUP, BAND, D), BF16), VM((2, GROUP, 3, 64, HALF), BF16), VM((GROUP, 1, VEC), F32), VM((RANKS, 1, VEC), F32),
     ]
     scratch += [VM((2,) + s, BF16) for s in sums] + [VM(s, BF16) for s in sums]
-    scratch += [VM((15,) + s[1:], BF16) for s in sums] + [VM((2,) + s, BF16) for s in sums]
-    scratch += [dma((13, 2, 3)), dma((3, 2, 31)), dma((3, 2, 32)), dma((2, 4)), dma((4,))]
+    scratch += [VM((3,) + sums[0][1:], BF16), VM((3,) + sums[1][1:], BF16), VM((15,) + sums[2][1:], BF16)]
+    scratch += [VM((3,) + s[2:], BF16) for s in sums[:2]] + [VM((2,) + s, BF16) for s in sums]
+    scratch += [dma((12, 2, 3)), dma((2, 16)), dma((2, 2, 31)), dma((3, 2, 32)), dma((2, 4)), dma((4,))]
     loss, input_grad, norms, full_a, full_b, full_c, full_proj = pl.pallas_call(
         body,
         out_shape=(
             shape((1, 128), F32), shape((OWN, D), F32), shape((1, 1536), F32),
             *(shape((2,) + s, BF16) for s in sums), shape((2, GROUP, 3, 64, HALF), BF16),
         ),
-        in_specs=[vmem] * 8 + [hbm] * 11,
+        in_specs=[vmem] * 3 + [pl.BlockSpec(memory_space=pltpu.SMEM)] + [vmem] * 4 + [hbm] * 11,
         out_specs=(vmem, vmem, vmem, hbm, hbm, hbm, hbm),
         scratch_shapes=scratch,
         compiler_params=pltpu.CompilerParams(collective_id=0, has_side_effects=True, vmem_limit_bytes=63 << 20),
         name="lit",
     )(
-        text_input, segment_ids.T, pad_mask.T, jnp.broadcast_to(pairing[:, None], (OWN_CAPS, 128)),
-        ln_first[None], ln_second[None], img_ln_first[None], img_ln_second[None],
+        text_input, segment_ids.T, pad_mask.T, pairing, ln_first, ln_second, img_ln_first, img_ln_second,
         image_tokens.transpose(1, 0, 2).reshape(IROWS, D), img_w_qkv, img_w_out, img_w_up, img_w_down, img_proj,
         w_qkv.swapaxes(1, 2), w_out, w_up, w_down, text_proj,
     )
 
-    def wide(full, first, last):
-        rows = (last - first) * full.shape[2]
-        return jnp.concatenate([full[j, first:last].reshape(rows, HALF) for j in range(2)], axis=1).astype(F32)
-
-    proj = jnp.concatenate([full_proj[j].reshape(D, HALF) for j in range(2)], axis=1).astype(F32)
-    qkv = wide(full_c, 4, 16).reshape(3, BAND, D).swapaxes(1, 2)
-    return (
-        loss[0, 0], input_grad, norms[0, :D], qkv, wide(full_c, 0, 4), norms[0, D:], wide(full_b, 0, 16),
-        wide(full_a, 0, 12), proj,
-    )
+    loss, input_grad, one, two, down, up, out, qkv, proj = pl.pallas_call(
+        widen,
+        out_shape=(
+            shape((1, 1), F32), shape((OWN, D), F32), shape((D,), F32), shape((D,), F32), shape((HID, D), F32),
+            shape((D, HID), F32), shape((BAND, D), F32), shape((3 * BAND, D), F32), shape((D, D), F32),
+        ),
+        in_specs=[vmem] * 2 + [hbm] * 5,
+        out_specs=(pl.BlockSpec(memory_space=pltpu.SMEM), hbm, vmem, vmem, hbm, hbm, hbm, hbm, hbm),
+        scratch_shapes=[
+            VM((OWN, D), F32), *(VM((2,) + s, BF16) for s in sums), VM((2, GROUP, 3, 64, HALF), BF16),
+            VM((HID, D), F32), VM((D, HID), F32), VM((BAND, D), F32), VM((3 * BAND, D), F32), VM((D, D), F32),
+            dma((5,)), dma((6,)),
+        ],
+        compiler_params=pltpu.CompilerParams(vmem_limit_bytes=60 << 20),
+        name="widen",
+    )(loss, norms, input_grad, full_a, full_b, full_c, full_proj)
+    return (loss.reshape(()), input_grad, one, qkv.reshape(3, BAND, D).swapaxes(1, 2), out, two, up, down, proj)
 
 
 def solution(mesh):

time: 173 us -> 148 us (0.86)
  local copies, waits for them, and re-layouts: 10.3 us -> 0 us
  Pallas kernels: 155 us -> 147 us
  other arithmetic: 6.3 us -> 0 us
    pallas_call x1, Pallas kernels: 155 us -> 140 us  [on_device(): pl.pallas_call(body, out_shape=(shape((1, 128), F32), shape((OWN, D), F32...]
    pallas_call x0 -> x1, Pallas kernels: none -> 6.66 us  [on_device(): pl.pallas_call(widen, out_shape=(shape((1, 1), F32), shape((OWN, D), F32)...]
    broadcast_in_dim x5 -> x0, local copies, waits for them, and re-layouts: 6.39 us -> none  [the longest x1 1.32 us: on_device(): jnp.broadcast_to(pairing[:, None], (OWN_CAPS, 128))]
    convert_element_type x3 -> x0, other arithmetic: 4.95 us -> none  [the longest x2 3.38 us: wide(): jnp.concatenate([full[j, first:last].reshape(rows, HALF) for j in range(2...]
    slice x6 -> x0, local copies, waits for them, and re-layouts: 2.46 us -> none  [the longest x4 1.72 us: wide(): full[j, first:last].reshape(rows, HALF)]
where the time goes in v2:
time: 148 us; the launch traced here: 147 us
  Pallas kernels  147 us (99%)
    pallas_call x1, Pallas kernels, on_device(): pl.pallas_call(body, out_shape=(shape((1, 128), F32), shape((OWN, D), F32...  140 us
    pallas_call x1, Pallas kernels, on_device(): pl.pallas_call(widen, out_shape=(shape((1, 1), F32), shape((OWN, D), F32)...  6.66 us

profile of v2, /device:TPU:1, one launch (start us, length us, event | category | flops | bytes accessed | tf_op | source)
XLA Modules:
  0.0 147.5 jit_solution(2762497956883920720)
XLA Ops:
  0.7 140.0 %lit.1 = (f32[1,128]{1,0:T(1,128)}, f32[128,768]{1,0:T(8,128)}, f32[1,1536]{1,0:T(1,128)}, bf16[2,4,4,64,384]{4,3,2,1,0:T(8,128)(2,1)}, bf16[2,4,4,48,384]{4,3,2...) custom-call(bf16[128,768]{1,0:T(8,128)(2,1)} %x.1, s32[16,32]{1,0:T(8,128)} %bitcast.12, ...), custom_call_target="tpu_custom_call" | custom-call | tf_op jit(solution)/shard_map/lit/pallas_call | solution.py:826
  140.7 6.7 %widen.1 = (f32[1,1]{1,0:T(1,128)}, f32[128,768]{1,0:T(8,128)}, f32[768]{0:T(1024)}, f32[768]{0:T(1024)}, f32[768,768]{1,0:T(8,128)}, /*index=5*/f32[768,768]{1,...) custom-call(f32[1,128]{1,0:T(1,128)} %get-tuple-element.25.loss, f32[1,1536]{1,0:T(1,128)} %get-tuple-element.26.norms, ...), custom_call_target="tpu_custom_call" | custom-call | tf_op jit(solution)/shard_map/widen/pallas_call | solution.py:843

commit v3 on v2

--- a/solution.py
+++ b/solution.py
@@ -11,9 +11,11 @@
 D, FF, HID = 768, 3072, 768
 IMGS, POS = 16, 50
 IROWS = IMGS * POS
-PAIR = 112
+HALFP = 56
+PAIR = 2 * HALFP
 PROWS = PAIR * (IMGS // 2)
 TILE = 256
+UP_TILE = 768
 
 
 def dot(a, b):
@@ -40,43 +42,27 @@
 
 
 def normal_cdf(u):
-    bell = jnp.exp(u * u * -0.5)
-    t = 1.0 / (1.0 + (0.3275911 * 0.7071067811865476) * jnp.abs(u))
-    poly = t * (0.5 * 0.254829592 + t * (0.5 * -0.284496736 + t * (0.5 * 1.421413741 + t * (0.5 * -1.453152027 + t * (0.5 * 1.061405429)))))
-    tail = poly * bell
-    return jnp.where(u < 0.0, tail, 1.0 - tail), bell
-
-
-def image_masks(perm, back, bias):
-    lanes = iota((PAIR, IROWS), 1)
-    w = iota((PAIR, IROWS), 0)
-    second = (w >= POS).astype(I32)
-    for p in range(IMGS // 2):
-        src = jnp.where(w < 2 * POS, (w - POS * second) * IMGS + 2 * p + second, -1)
-        perm[pl.ds(p * PAIR, PAIR), :] = jnp.where(src == lanes, 1.0, 0.0).astype(BF16)
-
-    def rows(i, c):
-        r = i * 160 + iota((160, PROWS), 0)
-        img, pos = r & 15, r >> 4
-        col = (img >> 1) * PAIR + (img & 1) * POS + pos
-        back[pl.ds(pl.multiple_of(i * 160, 160), 160), :] = jnp.where(col == iota((160, PROWS), 1), 1.0, 0.0).astype(BF16)
-        return c
-
-    lax.fori_loop(0, 5, rows, 0)
-    q = iota((2 * PAIR, PAIR), 0)
+    return 0.5 + 0.5 * lax.erf(u * 0.7071067811865476)
+
+
+def image_bias(bias):
+    q, k = iota((2 * PAIR, PAIR), 0), iota((2 * PAIR, PAIR), 1)
     q = jnp.where(q >= PAIR, q - PAIR, q)
-    k = iota((2 * PAIR, PAIR), 1)
-    bias[...] = jnp.where(((q >= POS) == (k >= POS)) & (k < 2 * POS), 0.0, NEG)
-
-
-def image_norm_one(tok, gain, ia):
+    place = jnp.where(k >= HALFP, k - HALFP, k)
+    bias[...] = jnp.where(((q >= HALFP) == (k >= HALFP)) & (place < POS), 0.0, NEG)
+
+
+def image_norm_one(tok, gain, stage):
     def rows(i, c):
         s = pl.ds(pl.multiple_of(i * 160, 160), 160)
         n, _ = normalized(tok[s, :].astype(F32))
-        ia[s, :] = (n * gain).astype(BF16)
+        n = n * gain
+        for h in range(6):
+            stage[h, s, :] = n[:, h * 128 : h * 128 + 128]
         return c
 
     lax.fori_loop(0, 5, rows, 0)
+    stage[:, IROWS:, :] = jnp.zeros((6, PROWS - IROWS, 128), F32)
 
 
 def tiles(n, body):
@@ -87,57 +73,56 @@
     lax.fori_loop(0, n, step, 0)
 
 
-def image_permute(perm, ia, iap):
-    def body(i, s):
-        iap[:, s] = dot(perm[...], ia[:, s]).astype(BF16)
-
-    tiles(3, body)
+def image_permute(stage, iap):
+    def pair(p, c):
+        for h in range(6):
+            both = [stage[h, pl.ds(2 * p + i, HALFP, stride=IMGS), :] for i in range(2)]
+            iap[pl.ds(pl.multiple_of(p * PAIR, PAIR), PAIR), h * 128 : h * 128 + 128] = jnp.concatenate(both, axis=0).astype(BF16)
+        return c
+    lax.fori_loop(0, IMGS // 2, pair, 0)
 
 
 def image_qkv(iap, w, iqkv):
-    for j in range(3):
-        def body(i, s):
-            iqkv[j, :, s] = dot(iap[...], w[j, :, s]).astype(BF16)
-
-        tiles(3, body)
-
-
-def image_attention(iqkv, bias, iatt, first, last):
+    def step(j, c):
+        iqkv[j] = dot(iap[...], w[j]).astype(BF16)
+        return c
+    lax.fori_loop(0, 3, step, 0)
+
+
+def stacked(values, low):
+    zero = jnp.zeros_like(values)
+    return jnp.concatenate([jnp.where(low, values, zero), jnp.where(low, zero, values)], axis=0)
+
+
+def image_attention(iqkv, bias, stage, first, last, unroll=1):
     low = iota((PAIR, 128), 1) < 64
 
     def pair(p, c):
         rows = pl.ds(pl.multiple_of(p * PAIR, PAIR), PAIR)
         ones = jnp.ones((PAIR, 128), BF16)
-        zero = jnp.zeros((PAIR, 128), BF16)
-        for h in range(6):
-            cols = pl.ds(h * 128, 128)
-            q, k, v = iqkv[0, rows, cols], iqkv[1, rows, cols], iqkv[2, rows, cols]
-            q2 = jnp.concatenate([jnp.where(low, q, zero), jnp.where(low, zero, q)], axis=0)
-            s = dot_t(q2, k) * 0.125 + bias[...]
-            e = jnp.exp(s - jnp.max(s, axis=-1, keepdims=True)).astype(BF16)
-            o = dot(e, jnp.concatenate([v, ones], axis=1))
-            o = o[:, :128] / o[:, 128:]
-            iatt[rows, cols] = jnp.where(low, o[:PAIR], o[PAIR:]).astype(BF16)
+        cols = [pl.ds(h * 128, 128) for h in range(6)]
+        s = [dot_t(stacked(iqkv[0, rows, h], low), iqkv[1, rows, h]) * 0.125 + bias[...] for h in cols]
+        e = [jnp.exp(x - jnp.max(x, axis=-1, keepdims=True)).astype(BF16) for x in s]
+        for i, (h, x) in enumerate(zip(cols, e)):
+            o = dot(x, jnp.concatenate([iqkv[2, rows, h], ones], axis=1))
+            o = jnp.where(low, o[:PAIR, :128], o[PAIR:, :128]) / jnp.where(low, o[:PAIR, 128:], o[PAIR:, 128:])
+            stage[i, pl.ds(2 * p, HALFP, stride=IMGS), :] = o[:HALFP]
+            stage[i, pl.ds(2 * p + 1, HALFP, stride=IMGS), :] = o[HALFP:]
         return c
 
-    lax.fori_loop(first, last, pair, 0)
-
-
-def image_out(back, iatt, spare, tok, w, iy):
-    def body(i, s):
-        spare[:, s] = dot(back[...], iatt[:, s]).astype(BF16)
-
-    tiles(3, body)
-
-    def body2(i, s):
-        iy[:, s] = tok[:, s].astype(F32) + dot(spare[...], w[:, s])
-
-    tiles(3, body2)
+    lax.fori_loop(first, last, pair, 0, unroll=unroll)
+
+
+def image_out(stage, tok, w, iy):
+    def rows(i, c):
+        s = pl.ds(pl.multiple_of(i * 160, 160), 160)
+        iy[s, :] = tok[s, :].astype(F32) + dot(jnp.concatenate([stage[h, s, :].astype(BF16) for h in range(6)], axis=1), w[...])
+        return c
+    lax.fori_loop(0, 5, rows, 0)
 
 
 def image_norm_two(iy, gain, ia, ypool):
     ypool[...] = jnp.zeros_like(ypool)
-
     def rows(i, c):
         s = pl.ds(pl.multiple_of(i * 160, 160), 160)
         y = iy[s, :]
@@ -145,18 +130,18 @@
         n, _ = normalized(y)
         ia[s, :] = (n * gain).astype(BF16)
         return c
-
     lax.fori_loop(0, 5, rows, 0)
 
 
 def image_up(ia, w, hsum, first, last):
     def step(i, c):
-        s = pl.ds(pl.multiple_of(i * TILE, TILE), TILE)
-        u = dot(ia[...], w[:, s])
-        phi, _ = normal_cdf(u)
-        hsum[:, s] = jnp.sum((u * phi).reshape(POS, IMGS, TILE), axis=0)
+        s = pl.ds(pl.multiple_of(i * UP_TILE, UP_TILE), UP_TILE)
+        for m in range(5):
+            u = dot(ia[160 * m : 160 * m + 160, :], w[:, s])
+            part = jnp.sum((u * normal_cdf(u)).reshape(10, IMGS, UP_TILE), axis=0)
+            total = part if m == 0 else total + part
+        hsum[:, s] = total
         return c
-
     lax.fori_loop(first, last, step, 0)
 
 
@@ -231,7 +216,9 @@
             pl.semaphore_signal(barrier, 1, device_id=self.group_peer(k), device_id_type=MESH)
         for k in range(1, RANKS):
             pl.semaphore_signal(barrier, 1, device_id=self.rank_peer(k), device_id_type=MESH)
-        pl.semaphore_wait(barrier, GROUP - 1 + RANKS - 1)
+
+    def met(self):
+        pl.semaphore_wait(pltpu.get_barrier_semaphore(), GROUP - 1 + RANKS - 1)
 
 
 def send(src, dst, sems, at, peer):
@@ -294,33 +281,25 @@
     return iota((OWN, 128), 1) < 64
 
 
-def stacked(values, low):
-    zero = jnp.zeros_like(values)
-    return jnp.concatenate([jnp.where(low, values, zero), jnp.where(low, zero, values)], axis=0)
-
-
 def text_attention(a1, w_t, bias, w_out, qkv, probs, att, parts):
     rows_all = a1[...].reshape(ROWS, D)
     for j in range(3):
         qkv[j] = dot_t(rows_all, w_t[j]).astype(BF16)
     low = low_half()
-
-    def soft(s):
-        e = jnp.exp(s - jnp.max(s, axis=-1, keepdims=True))
-        return e / jnp.sum(e, axis=-1, keepdims=True)
-
-    for b in range(4):
-        rows = slice(128 * b, 128 * b + 128)
-        q, k, v = qkv[0, rows, :128], qkv[1, rows, :128], qkv[2, rows, :128]
+    blocks = [slice(128 * b, 128 * b + 128) for b in range(4)]
+    scores = []
+    for b, rows in enumerate(blocks):
         mask = bias[b]
-        p = soft(dot_t(stacked(q, low), k) * 0.125 + jnp.concatenate([mask, mask], axis=0))
-        probs[b, :256] = p
-        o = dot(p.astype(BF16), v)
+        scores.append(dot_t(stacked(qkv[0, rows, :128], low), qkv[1, rows, :128]) * 0.125 + jnp.concatenate([mask, mask], axis=0))
+        scores.append(dot_t(qkv[0, rows, 128:], qkv[1, rows, 128:]) * 0.125 + mask)
+    powers = [jnp.exp(x - jnp.max(x, axis=-1, keepdims=True)) for x in scores]
+    shares = [x / jnp.sum(x, axis=-1, keepdims=True) for x in powers]
+    for b, rows in enumerate(blocks):
+        probs[b, :256] = shares[2 * b]
+        probs[b, 256:] = shares[2 * b + 1]
+        o = dot(shares[2 * b].astype(BF16), qkv[2, rows, :128])
         att[rows, :128] = jnp.where(low, o[:128], o[128:]).astype(BF16)
-        q, k, v = qkv[0, rows, 128:], qkv[1, rows, 128:], qkv[2, rows, 128:]
-        p = soft(dot_t(q, k) * 0.125 + mask)
-        probs[b, 256:] = p
-        att[rows, 128:] = dot(p.astype(BF16), v).astype(BF16)
+        att[rows, 128:] = dot(shares[2 * b + 1].astype(BF16), qkv[2, rows, 128:]).astype(BF16)
     parts[...] = dot(att[...], w_out[...]).astype(BF16).reshape(GROUP, OWN, D)
 
 
@@ -351,29 +330,29 @@
     x1_pool[...] = dot(jnp.concatenate([own, own, own], axis=1), split3(x1[...]))
 
 
-def text_up(a2, w_up, mem, w_down, dgelu, hsum, parts):
-    def body(i, s):
-        u = dot(a2[...].reshape(ROWS, D), w_up[:, s])
-        phi, bell = normal_cdf(u)
-        dgelu[:, s] = phi + u * bell * 0.3989422804014327
-        hsum[:, s] = dot(mem[...], (u * phi).astype(BF16))
-
-    tiles(3, body)
+def text_up(a2, w_up, mem, w_down, x1_pool, dgelu, hidden, hsum, part, parts, t):
+    for r in range(GROUP):
+        rows = slice(r * OWN, r * OWN + OWN)
+        u = dot(a2[r], w_up[...])
+        phi = normal_cdf(u)
+        dgelu[rows, :] = phi + u * (jnp.exp(u * u * -0.5) * 0.3989422804014327)
+        hidden[rows, :] = (u * phi).astype(BF16)
+    hsum[...] = dot(mem[...], hidden[...])
     both = dot(split_rows(hsum[...]), w_down[...])
-    parts[...] = (both[:CAPS] + both[CAPS:]).reshape(GROUP, OWN_CAPS, D)
+    part[...] = (both[:CAPS] + both[CAPS:]).reshape(GROUP, OWN_CAPS, D)
+    part[t] += x1_pool[...]
+    parts[t] = part[...].reshape(CAPS, D).astype(BF16)
 
 
 def counts_of(mem):
     return jnp.sum(mem.astype(F32), axis=1, keepdims=True)
 
 
-def text_pool(parts, landed, x1_pool, mem, pooled, t):
-    total = x1_pool[...] + parts[t] + landed[0] + landed[1] + landed[2]
-    pooled[t] = (total / counts_of(own_member(mem, t))).astype(BF16)
-
-
-def text_embed(pooled, w_proj, tf, scale):
-    e = dot(pooled[...].reshape(CAPS, D), w_proj[...])
+def text_embed(parts, mem, w_proj, pooled, tf, scale):
+    total = parts[0].astype(F32) + parts[1].astype(F32) + parts[2].astype(F32) + parts[3].astype(F32)
+    rows = (total / counts_of(mem[...])).astype(BF16)
+    pooled[...] = rows
+    e = dot(rows, w_proj[...])
     rs = lax.rsqrt(jnp.sum(e * e, axis=-1, keepdims=True) + EPS)
     tf[...] = rs * e
     scale[...] = jnp.broadcast_to(rs, (CAPS, 128))
@@ -449,7 +428,7 @@
     dz2 = jnp.concatenate([dz[...], dz[...]], axis=0)
     for i in range(3):
         put_halves(g, 4 * i, 4, 64, t_dot(hs[:, i * TILE : (i + 1) * TILE], dz2))
-    proj[...] = t_dot(pooled[...].reshape(CAPS, D), de[...]).astype(BF16).reshape(GROUP, BAND, D)
+    proj[...] = t_dot(pooled[...], de[...]).astype(BF16).reshape(GROUP, BAND, D)
     put_halves(g, 12, 3, 64, proj[t])
     g[:, 3, 3] = jnp.zeros((2, 64, HALF), BF16)
 
@@ -473,28 +452,23 @@
 def attention_grad(dy, w_out, w_t, qkv, probs, dqkv, parts):
     datt = dot_t(dy[...].reshape(ROWS, D), w_out[...]).astype(BF16)
     low = low_half()
-
-    def scores(p, d, v):
-        dp = dot_t(d, v)
-        return (p * (dp - jnp.sum(p * dp, axis=-1, keepdims=True))).astype(BF16)
-
-    for b in range(4):
-        rows = slice(128 * b, 128 * b + 128)
-        q, k, v = stacked(qkv[0, rows, :128], low), qkv[1, rows, :128], qkv[2, rows, :128]
-        d = stacked(datt[rows, :128], low)
-        p = probs[b, :256]
-        ds = scores(p, d, v)
-        o = dot(ds, k)
-        dqkv[0, rows, :128] = (jnp.where(low, o[:128], o[128:]) * 0.125).astype(BF16)
-        dqkv[1, rows, :128] = (t_dot(ds, q) * 0.125).astype(BF16)
-        dqkv[2, rows, :128] = t_dot(p.astype(BF16), d).astype(BF16)
-        q, k, v = qkv[0, rows, 128:], qkv[1, rows, 128:], qkv[2, rows, 128:]
-        d = datt[rows, 128:]
-        p = probs[b, 256:]
-        ds = scores(p, d, v)
-        dqkv[0, rows, 128:] = (dot(ds, k) * 0.125).astype(BF16)
-        dqkv[1, rows, 128:] = (t_dot(ds, q) * 0.125).astype(BF16)
-        dqkv[2, rows, 128:] = t_dot(p.astype(BF16), d).astype(BF16)
+    blocks = [slice(128 * b, 128 * b + 128) for b in range(4)]
+    sides, raw = [], []
+    for b, rows in enumerate(blocks):
+        sides.append((stacked(qkv[0, rows, :128], low), stacked(datt[rows, :128], low)))
+        sides.append((qkv[0, rows, 128:], datt[rows, 128:]))
+        raw.append(dot_t(sides[-2][1], qkv[2, rows, :128]))
+        raw.append(dot_t(sides[-1][1], qkv[2, rows, 128:]))
+    probs_of = [probs[b, part] for b in range(4) for part in (slice(0, 256), slice(256, 384))]
+    ds = [(p * (x - jnp.sum(p * x, axis=-1, keepdims=True))).astype(BF16) for p, x in zip(probs_of, raw)]
+    for b, rows in enumerate(blocks):
+        for i, cols in ((2 * b, slice(0, 128)), (2 * b + 1, slice(128, BAND))):
+            o = dot(ds[i], qkv[1, rows, cols])
+            if i % 2 == 0:
+                o = jnp.where(low, o[:128], o[128:])
+            dqkv[0, rows, cols] = (o * 0.125).astype(BF16)
+            dqkv[1, rows, cols] = (t_dot(ds[i], sides[i][0]) * 0.125).astype(BF16)
+            dqkv[2, rows, cols] = t_dot(probs_of[i].astype(BF16), sides[i][1]).astype(BF16)
     total = dot(dqkv[0], w_t[0]) + dot(dqkv[1], w_t[1]) + dot(dqkv[2], w_t[2])
     parts[...] = total.astype(BF16).reshape(GROUP, OWN, D)
 
@@ -597,35 +571,44 @@
     h_tok, h_iqkv, h_iout, h_iup, h_idown, h_iproj, h_qkv, h_out, h_up, h_down, h_proj,
     o_loss, o_input, o_norms, o_a, o_b, o_c, o_proj,
     tok, iw_qkv, iw_out, iw_up, iw_down, iw_proj, w_qkv, w_out, w_up, w_down, w_proj, load,
-    perm, back, ibias, ia, iap, iqkv, iy, ypool, ihsum, images,
-    bias, mem, mem_t, pair, a1, qkv, probs, att, p_att, l_att, x1, x1_pool, a2, dgelu, hsum, p_pool, l_pool,
+    ibias, iap, iqkv, stage, iy, ypool, ihsum, images,
+    bias, mem, mem_t, pair, a1, qkv, probs, att, p_att, l_att, x1, x1_pool, a2, dgelu, hsum, p_pool, pools,
     tf, scale, pooled, s_ref, e_ref, row_sums, col_sums, dts, de, dz, gp, dx2, du, p_da2, l_da2, dx1, dy,
     dqkv, p_da1, l_da1, proj, proj_all, vec, vec_all,
     g_a, g_b, g_c, m_a, m_b, m_c, r_a, r_b, r_c, n_a, n_b, f_a, f_b, f_c,
-    group_sems, image_sems, rank_sems, sum_sems, proj_sems, store,
+    group_sems, image_sems, rank_sems, sum_sems, proj_sems, store_sems,
 ):
     links = Links()
-    t, dp = links.t, links.dp
+    t, dp, core, chip = links.t, links.dp, links.core, links.chip
     loads = {}
-    for i, (name, src, dst) in enumerate((
-        ("tok", h_tok, tok), ("iqkv", h_iqkv, iw_qkv), ("qkv", h_qkv, w_qkv), ("out", h_out, w_out), ("iout", h_iout, iw_out),
-        ("iup", h_iup, iw_up), ("up", h_up, w_up), ("down", h_down, w_down), ("idown", h_idown, iw_down),
-        ("iproj", h_iproj, iw_proj), ("proj", h_proj, w_proj),
-    )):
-        loads[name] = pltpu.make_async_copy(src, dst, load.at[i])
+
+    def fetch(at, name, src, dst):
+        loads[name] = pltpu.make_async_copy(src, dst, load.at[at])
         loads[name].start()
 
+    fetch(0, "tok", h_tok, tok)
+    fetch(1, "iqkv", h_iqkv, iw_qkv)
     links.greet()
+    text_norm_one(x, as_row(gain_one), a1, t)
     pair[t] = column(pair_in)
+    links.met()
+    copies = group_share(links, a1, group_sems.at[1])
     pair_copies = group_share(links, pair, group_sems.at[0])
-    text_norm_one(x, as_row(gain_one), a1, t)
-    copies = group_share(links, a1, group_sems.at[1])
+    fetch(2, "qkv", h_qkv, w_qkv)
+    fetch(3, "out", h_out, w_out)
+    fetch(4, "iout", h_iout, iw_out)
 
     text_masks(seg_t, pad_t, bias, mem, mem_t)
-    image_masks(perm, back, ibias)
+    image_bias(ibias)
     loads["tok"].wait()
-    image_norm_one(tok, as_row(img_gain_one), ia)
-    image_permute(perm, ia, iap)
+    image_norm_one(tok, as_row(img_gain_one), stage)
+    fetch(5, "iup", h_iup, iw_up)
+    fetch(6, "up", h_up, w_up)
+    fetch(7, "down", h_down, w_down)
+    fetch(8, "idown", h_idown, iw_down)
+    fetch(9, "iproj", h_iproj, iw_proj)
+    fetch(10, "proj", h_proj, w_proj)
+    image_permute(stage, iap)
     loads["iqkv"].wait()
     image_qkv(iap, iw_qkv, iqkv)
 
@@ -635,45 +618,36 @@
     text_attention(a1, w_qkv, bias, w_out, qkv, probs, att, p_att)
     copies = group_scatter(links, p_att, l_att, group_sems.at[2])
 
-    image_attention(iqkv, ibias, iap, 0, 8)
+    image_attention(iqkv, ibias, stage, 0, 8)
+    loads["iout"].wait()
+    image_out(stage, tok, iw_out, iy)
+    image_norm_two(iy, as_row(img_gain_two), iap.at[:IROWS], ypool)
 
     finish(copies)
     text_norm_two(x, p_att, l_att, as_row(gain_two), mem, x1, a2, x1_pool, t)
     copies = group_share(links, a2, group_sems.at[3])
     text_pool_one(x1, mem, x1_pool, t)
 
-    loads["iout"].wait()
-    image_out(back, iap, ia, tok, iw_out, iy)
-    image_norm_two(iy, as_row(img_gain_two), ia, ypool)
     loads["iup"].wait()
-    image_up(ia, iw_up, ihsum, 0, 6)
+    image_up(iap.at[:IROWS], iw_up, ihsum, 0, FF // UP_TILE)
+    loads["idown"].wait()
+    loads["iproj"].wait()
+    images[core, chip] = image_finish(ihsum, ypool, iw_down, iw_proj)
+    own = images.at[core, chip]
+    image_copies = [send(own, own, image_sems, k, links.chip_peer(k)) for k in range(1, CHIPS)]
 
     finish(copies)
     loads["up"].wait()
     loads["down"].wait()
-    text_up(a2, w_up, mem, w_down, dgelu, hsum, p_pool)
-    copies = group_scatter(links, p_pool, l_pool, group_sems.at[4])
-
-    image_up(ia, iw_up, ihsum, 6, 10)
-    finish(copies)
-    text_pool(p_pool, l_pool, x1_pool, mem, pooled, t)
-    copies = group_share(links, pooled, group_sems.at[5])
-
-    image_up(ia, iw_up, ihsum, 10, 12)
-    loads["idown"].wait()
-    loads["iproj"].wait()
-    core, chip = links.core, links.chip
-    images[core, chip] = image_finish(ihsum, ypool, iw_down, iw_proj)
-    own = images.at[core, chip]
-    image_copies = [send(own, own, image_sems, k, links.chip_peer(k)) for k in range(1, CHIPS)]
-
-    finish(copies)
-    loads["proj"].wait()
-    text_embed(pooled, w_proj, tf, scale)
+    text_up(a2, w_up, mem, w_down, x1_pool, dgelu, du, hsum, p_pool, pools, t)
+    copies = group_share(links, pools, group_sems.at[4])
     finish(image_copies)
     own = images.at[core]
     image_copies = [send(own, own, image_sems, 0, links.sibling())]
     finish(pair_copies)
+    loads["proj"].wait()
+    finish(copies)
+    text_embed(pools, mem, w_proj, pooled, tf, scale)
     finish(image_copies)
 
     score_sums(tf, images, s_ref, e_ref, row_sums, col_sums, t, dp)
@@ -731,7 +705,7 @@
     proj_copies = [send(own, own, proj_sems, 0, links.sibling())]
     red_a.done()
     red_b.done()
-    stores = [pltpu.make_async_copy(f_a, o_a, store.at[0]), pltpu.make_async_copy(f_b, o_b, store.at[1])]
+    stores = [pltpu.make_async_copy(f_a, o_a, store_sems.at[0]), pltpu.make_async_copy(f_b, o_b, store_sems.at[1])]
     for copy in stores:
         copy.start()
     finish(vec_copies)
@@ -741,11 +715,11 @@
     o_norms[...] = total[:, :1536]
     o_loss[...] = total[:, 1536:] * (1.0 / 4096.0)
     finish(proj_copies)
-    stores.append(pltpu.make_async_copy(proj_all, o_proj, store.at[2]))
+    stores.append(pltpu.make_async_copy(proj_all, o_proj, store_sems.at[2]))
     stores[-1].start()
     red_c.share()
     red_c.done()
-    stores.append(pltpu.make_async_copy(f_c, o_c, store.at[3]))
+    stores.append(pltpu.make_async_copy(f_c, o_c, store_sems.at[3]))
     stores[-1].start()
     for copy in stores:
         copy.wait()
@@ -805,14 +779,13 @@
     scratch = [
         VM((IROWS, D), BF16), VM((3, D, D), BF16), VM((D, D), BF16), VM((D, FF), BF16), VM((FF, D), BF16), VM((D, D), BF16),
         VM((3, BAND, D), BF16), VM((BAND, D), BF16), VM((D, HID), BF16), VM((HID, D), BF16), VM((D, D), BF16), dma((11,)),
-        VM((PROWS, IROWS), BF16), VM((IROWS, PROWS), BF16), VM((2 * PAIR, PAIR), F32), VM((IROWS, D), BF16), VM((PROWS, D), BF16),
-        VM((3, PROWS, D), BF16), VM((IROWS, D), F32), VM((IMGS, D), F32),
-        VM((IMGS, FF), F32), VM((2, CHIPS, IMGS, D), BF16),
+        VM((2 * PAIR, PAIR), F32), VM((PROWS, D), BF16), VM((3, PROWS, D), BF16), VM((6, PROWS, 128), F32), VM((IROWS, D), F32),
+        VM((IMGS, D), F32), VM((IMGS, FF), F32), VM((2, CHIPS, IMGS, D), BF16),
         VM((4, 128, 128), F32), VM((CAPS, ROWS), BF16), VM((ROWS, 128), BF16), VM((GROUP, OWN_CAPS, 128), I32),
         VM((GROUP, OWN, D), BF16), VM((3, ROWS, BAND), BF16), VM((4, HALF, 128), F32), VM((ROWS, BAND), BF16),
         VM((GROUP, OWN, D), BF16), VM((3, OWN, D), BF16), VM((OWN, D), F32), VM((OWN_CAPS, D), F32), VM((GROUP, OWN, D), BF16),
-        VM((ROWS, HID), F32), VM((CAPS, HID), F32), VM((GROUP, OWN_CAPS, D), F32), VM((3, OWN_CAPS, D), F32),
-        VM((CAPS, D), F32), VM((CAPS, 128), F32), VM((GROUP, OWN_CAPS, D), BF16), VM((CAPS, ROWS), F32),
+        VM((ROWS, HID), F32), VM((CAPS, HID), F32), VM((GROUP, OWN_CAPS, D), F32), VM((GROUP, CAPS, D), BF16),
+        VM((CAPS, D), F32), VM((CAPS, 128), F32), VM((CAPS, D), BF16), VM((CAPS, ROWS), F32),
         VM((CAPS, ROWS), F32), VM((GROUP, CAPS, 128), F32), VM((RANKS, 1, ROWS), F32), VM((GROUP, CAPS, D), BF16),
         VM((CAPS, D), BF16), VM((CAPS, D), BF16), VM((CAPS, D), F32),
         VM((OWN, D), F32), VM((ROWS, HID), BF16), VM((GROUP, OWN, D), BF16), VM((3, OWN, D), BF16), VM((OWN, D), F32),

time: 148 us -> 132 us (0.89)
  Pallas kernels: 147 us -> 131 us
    pallas_call x1, Pallas kernels: 140 us -> 125 us  [on_device(): pl.pallas_call(body, out_shape=(shape((1, 128), F32), shape((OWN, D), F32...]
where the time goes in v3:
time: 132 us
  Pallas kernels  131 us (99%)
    pallas_call x1, Pallas kernels, on_device(): pl.pallas_call(body, out_shape=(shape((1, 128), F32), shape((OWN, D), F32...  125 us
    pallas_call x1, Pallas kernels, on_device(): pl.pallas_call(widen, out_shape=(shape((1, 1), F32), shape((OWN, D), F32)...  6.66 us

profile of v3, /device:TPU:1, one launch (start us, length us, event | category | flops | bytes accessed | tf_op | source)
XLA Modules:
  0.0 132.0 jit_solution(10231008339682608123)
XLA Ops:
  0.7 124.5 %lit.1 = (f32[1,128]{1,0:T(1,128)}, f32[128,768]{1,0:T(8,128)}, f32[1,1536]{1,0:T(1,128)}, bf16[2,4,4,64,384]{4,3,2,1,0:T(8,128)(2,1)}, bf16[2,4,4,48,384]{4,3,2...) custom-call(bf16[128,768]{1,0:T(8,128)(2,1)} %x.1, s32[16,32]{1,0:T(8,128)} %bitcast.12, ...), custom_call_target="tpu_custom_call" | custom-call | tf_op jit(solution)/shard_map/lit/pallas_call | solution.py:799
  125.2 6.7 %widen.1 = (f32[1,1]{1,0:T(1,128)}, f32[128,768]{1,0:T(8,128)}, f32[768]{0:T(1024)}, f32[768]{0:T(1024)}, f32[768,768]{1,0:T(8,128)}, /*index=5*/f32[768,768]{1,...) custom-call(f32[1,128]{1,0:T(1,128)} %get-tuple-element.25.loss, f32[1,1536]{1,0:T(1,128)} %get-tuple-element.26.norms, ...), custom_call_target="tpu_custom_call" | custom-call | tf_op jit(solution)/shard_map/widen/pallas_call | solution.py:816

commit v4 on v3

--- a/solution.py
+++ b/solution.py
@@ -176,6 +176,7 @@
 HALF = 384
 MESH = pl.DeviceIdType.MESH
 VEC = 1664
+PAIRS = 34
 
 
 class Links:
@@ -221,31 +222,46 @@
         pl.semaphore_wait(pltpu.get_barrier_semaphore(), GROUP - 1 + RANKS - 1)
 
 
-def send(src, dst, sems, at, peer):
-    copy = pltpu.make_async_remote_copy(
-        src, dst, sems.at[0, at], sems.at[1, at], device_id=peer, device_id_type=MESH
-    )
-    copy.start()
-    return copy
-
-
-def finish(copies):
-    for copy in copies:
-        copy.wait()
+def send(src, dst, sems, peer):
+    pltpu.make_async_remote_copy(src, dst, sems.at[0], sems.at[1], device_id=peer, device_id_type=MESH).start()
+
+
+def finish(exchange):
+    sems, span = exchange
+    for i in range(2):
+        pltpu.make_async_copy(span, span, sems.at[i]).wait()
 
 
 def group_share(links, buf, sems):
     own = buf.at[links.t]
-    return [send(own, own, sems, k - 1, links.group_peer(k)) for k in (2, 1, 3)]
+    for k in (2, 1, 3):
+        send(own, own, sems, links.group_peer(k))
+    return sems, buf.at[pl.ds(0, 3)]
 
 
 def group_scatter(links, parts, landed, sems):
-    return [send(parts.at[links.rank(k)], landed.at[k - 1], sems, k - 1, links.group_peer(k)) for k in (2, 1, 3)]
+    for k in (2, 1, 3):
+        send(parts.at[links.rank(k)], landed.at[k - 1], sems, links.group_peer(k))
+    return sems, landed
 
 
 def rank_share(links, buf, sems):
     own = buf.at[links.dp]
-    return [send(own, own, sems, k - 1, links.rank_peer(k)) for k in range(1, RANKS)]
+    for k in range(1, RANKS):
+        send(own, own, sems, links.rank_peer(k))
+    return sems, buf.at[pl.ds(0, RANKS - 1)]
+
+
+def chip_share(links, buf, sems):
+    own = buf.at[links.chip]
+    for k in range(1, CHIPS):
+        send(own, own, sems, links.chip_peer(k))
+    return sems, buf.at[pl.ds(0, CHIPS - 1)]
+
+
+def sibling_send(links, src, dst, sems):
+    send(src, dst, sems, links.sibling())
+    return sems, src
 
 
 def text_masks(seg_t, pad_t, bias, mem, mem_t):
@@ -488,99 +504,107 @@
 
 
 class Reduction:
-    def __init__(self, links, g, met, landed, full, sems):
-        self.links, self.g, self.met, self.landed, self.full, self.sems = links, g, met, landed, full, sems
+    def __init__(self, links, g, met, landed, full, pair):
+        self.links, self.g, self.met, self.landed, self.full, self.pair = links, g, met, landed, full, pair
 
     def cores(self):
-        other = 1 - self.links.core
-        self.copies = [send(self.g.at[other], self.met, self.sems, 0, self.links.sibling())]
+        self.open = sibling_send(self.links, self.g.at[1 - self.links.core], self.met, self.pair())
 
     def both_cores(self):
-        finish(self.copies)
+        finish(self.open)
         self.met[...] = (self.g[self.links.core].astype(F32) + self.met[...].astype(F32)).astype(BF16)
 
     def scatter(self):
         self.both_cores()
-        self.copies = [
-            send(self.met.at[self.links.chip_of(k)], self.landed.at[k - 1], self.sems, k, self.links.chip_peer(k))
-            for k in range(1, CHIPS)
-        ]
+        sems = self.pair()
+        for k in range(1, CHIPS):
+            send(self.met.at[self.links.chip_of(k)], self.landed.at[k - 1], sems, self.links.chip_peer(k))
+        self.open = sems, self.landed
 
     def gather(self):
-        finish(self.copies)
+        finish(self.open)
         total = self.met[self.links.chip].astype(F32)
         for k in range(CHIPS - 1):
             total = total + self.landed[k].astype(F32)
-        core, chip = self.links.core, self.links.chip
-        self.full[core, chip] = total.astype(BF16)
-        own = self.full.at[core, chip]
-        self.copies = [send(own, own, self.sems, 15 + k, self.links.chip_peer(k)) for k in range(1, CHIPS)]
+        half = self.full.at[self.links.core]
+        half[self.links.chip] = total.astype(BF16)
+        self.open = chip_share(self.links, half, self.pair())
 
     def share(self):
-        finish(self.copies)
-        own = self.full.at[self.links.core]
-        self.copies = [send(own, own, self.sems, 31, self.links.sibling())]
+        finish(self.open)
+        half = self.full.at[self.links.core]
+        self.open = sibling_send(self.links, half, half, self.pair())
 
     def done(self):
-        finish(self.copies)
+        finish(self.open)
 
 
 class TwoAxes(Reduction):
-    def __init__(self, links, g, met, landed, near, full, sems, first, second):
-        super().__init__(links, g, met, landed, full, sems)
+    def __init__(self, links, g, met, landed, near, full, pair, first, second):
+        super().__init__(links, g, met, landed, full, pair)
         self.near, self.first, self.second = near, first, second
         self.i, self.j = links.place[first], links.place[second]
 
+    def spread(self, axis, source, target):
+        sems = self.pair()
+        for k in (2, 1, 3):
+            send(source(k), target(k), sems, self.links.axis_peer(axis, k))
+        return sems
+
     def scatter(self):
         self.both_cores()
-        rank, peer = self.links.axis_rank, self.links.axis_peer
-        self.copies = [
-            send(self.met.at[rank(self.first, k)], self.landed.at[k - 1], self.sems, k, peer(self.first, k)) for k in (2, 1, 3)
-        ]
+        sems = self.spread(
+            self.first, lambda k: self.met.at[self.links.axis_rank(self.first, k)], lambda k: self.landed.at[k - 1]
+        )
+        self.open = sems, self.landed
 
     def scatter_second(self):
-        finish(self.copies)
+        finish(self.open)
         total = self.met[self.i].astype(F32)
         for k in range(3):
             total = total + self.landed[k].astype(F32)
         self.met[self.i] = total.astype(BF16)
-        rank, peer = self.links.axis_rank, self.links.axis_peer
-        self.copies = [
-            send(self.met.at[self.i, rank(self.second, k)], self.near.at[k - 1], self.sems, 3 + k, peer(self.second, k))
-            for k in (2, 1, 3)
-        ]
+        sems = self.spread(
+            self.second, lambda k: self.met.at[self.i, self.links.axis_rank(self.second, k)], lambda k: self.near.at[k - 1]
+        )
+        self.open = sems, self.near
 
     def gather(self):
-        finish(self.copies)
+        finish(self.open)
         total = self.met[self.i, self.j].astype(F32)
         for k in range(3):
             total = total + self.near[k].astype(F32)
         core = self.links.core
         self.full[core, self.i, self.j] = total.astype(BF16)
         own = self.full.at[core, self.i, self.j]
-        self.copies = [send(own, own, self.sems, 6 + k, self.links.axis_peer(self.second, k)) for k in (2, 1, 3)]
+        self.open = self.spread(self.second, lambda k: own, lambda k: own), self.full.at[0, 0, pl.ds(0, 3)]
 
     def gather_second(self):
-        finish(self.copies)
+        finish(self.open)
         own = self.full.at[self.links.core, self.i]
-        self.copies = [send(own, own, self.sems, 9 + k, self.links.axis_peer(self.first, k)) for k in (2, 1, 3)]
+        self.open = self.spread(self.first, lambda k: own, lambda k: own), self.full.at[0, pl.ds(0, 3)]
 
 
 def body(
     x, seg_t, pad_t, pair_in, gain_one, gain_two, img_gain_one, img_gain_two,
     h_tok, h_iqkv, h_iout, h_iup, h_idown, h_iproj, h_qkv, h_out, h_up, h_down, h_proj,
-    o_loss, o_input, o_norms, o_a, o_b, o_c, o_proj,
+    o_loss, o_input, o_norms, f_a, f_b, f_c, proj_all,
     tok, iw_qkv, iw_out, iw_up, iw_down, iw_proj, w_qkv, w_out, w_up, w_down, w_proj, load,
     ibias, iap, iqkv, stage, iy, ypool, ihsum, images,
     bias, mem, mem_t, pair, a1, qkv, probs, att, p_att, l_att, x1, x1_pool, a2, dgelu, hsum, p_pool, pools,
     tf, scale, pooled, s_ref, e_ref, row_sums, col_sums, dts, de, dz, gp, dx2, du, p_da2, l_da2, dx1, dy,
-    dqkv, p_da1, l_da1, proj, proj_all, vec, vec_all,
-    g_a, g_b, g_c, m_a, m_b, m_c, r_a, r_b, r_c, n_a, n_b, f_a, f_b, f_c,
-    group_sems, image_sems, rank_sems, sum_sems, proj_sems, store_sems,
+    dqkv, p_da1, l_da1, proj, vec, vec_all,
+    g_a, g_b, g_c, m_a, m_b, m_c, r_a, r_b, r_c, n_a, n_b,
+    sems,
 ):
     links = Links()
     t, dp, core, chip = links.t, links.dp, links.core, links.chip
     loads = {}
+    count = iter(range(PAIRS))
+
+    def pair_of():
+        return sems.at[next(count)]
+
 
     def fetch(at, name, src, dst):
         loads[name] = pltpu.make_async_copy(src, dst, load.at[at])
@@ -592,8 +616,8 @@
     text_norm_one(x, as_row(gain_one), a1, t)
     pair[t] = column(pair_in)
     links.met()
-    copies = group_share(links, a1, group_sems.at[1])
-    pair_copies = group_share(links, pair, group_sems.at[0])
+    copies = group_share(links, a1, pair_of())
+    pair_copies = group_share(links, pair, pair_of())
     fetch(2, "qkv", h_qkv, w_qkv)
     fetch(3, "out", h_out, w_out)
     fetch(4, "iout", h_iout, iw_out)
@@ -616,34 +640,33 @@
     loads["qkv"].wait()
     loads["out"].wait()
     text_attention(a1, w_qkv, bias, w_out, qkv, probs, att, p_att)
-    copies = group_scatter(links, p_att, l_att, group_sems.at[2])
+    copies = group_scatter(links, p_att, l_att, pair_of())
 
     image_attention(iqkv, ibias, stage, 0, 8)
     loads["iout"].wait()
     image_out(stage, tok, iw_out, iy)
     image_norm_two(iy, as_row(img_gain_two), iap.at[:IROWS], ypool)
 
+    loads["iup"].wait()
+    image_up(iap.at[:IROWS], iw_up, ihsum, 0, 1)
     finish(copies)
     text_norm_two(x, p_att, l_att, as_row(gain_two), mem, x1, a2, x1_pool, t)
-    copies = group_share(links, a2, group_sems.at[3])
+    copies = group_share(links, a2, pair_of())
     text_pool_one(x1, mem, x1_pool, t)
 
-    loads["iup"].wait()
-    image_up(iap.at[:IROWS], iw_up, ihsum, 0, FF // UP_TILE)
+    image_up(iap.at[:IROWS], iw_up, ihsum, 1, FF // UP_TILE)
     loads["idown"].wait()
     loads["iproj"].wait()
     images[core, chip] = image_finish(ihsum, ypool, iw_down, iw_proj)
-    own = images.at[core, chip]
-    image_copies = [send(own, own, image_sems, k, links.chip_peer(k)) for k in range(1, CHIPS)]
+    image_copies = chip_share(links, images.at[core], pair_of())
 
     finish(copies)
     loads["up"].wait()
     loads["down"].wait()
     text_up(a2, w_up, mem, w_down, x1_pool, dgelu, du, hsum, p_pool, pools, t)
-    copies = group_share(links, pools, group_sems.at[4])
+    copies = group_share(links, pools, pair_of())
     finish(image_copies)
-    own = images.at[core]
-    image_copies = [send(own, own, image_sems, 0, links.sibling())]
+    image_copies = sibling_send(links, images.at[core], images.at[core], pair_of())
     finish(pair_copies)
     loads["proj"].wait()
     finish(copies)
@@ -651,21 +674,21 @@
     finish(image_copies)
 
     score_sums(tf, images, s_ref, e_ref, row_sums, col_sums, t, dp)
-    col_copies = rank_share(links, col_sums, rank_sems.at[0])
-    row_copies = group_share(links, row_sums, group_sems.at[6])
+    col_copies = rank_share(links, col_sums, pair_of())
+    row_copies = group_share(links, row_sums, pair_of())
     finish(col_copies)
     finish(row_copies)
     score_grad(s_ref, e_ref, row_sums, col_sums, pair, images, dts, vec, t)
-    finish(group_share(links, dts, group_sems.at[7]))
+    finish(group_share(links, dts, pair_of()))
     embed_grad(dts, tf, scale, w_proj, mem, de, dz, gp)
 
-    red_a = TwoAxes(links, g_a, m_a, r_a, n_a, f_a, sum_sems.at[0], "x", "z")
-    red_b = TwoAxes(links, g_b, m_b, r_b, n_b, f_b, sum_sems.at[1], "z", "x")
-    red_c = Reduction(links, g_c, m_c, r_c, f_c, sum_sems.at[2])
+    red_a = TwoAxes(links, g_a, m_a, r_a, n_a, f_a, pair_of, "x", "z")
+    red_b = TwoAxes(links, g_b, m_b, r_b, n_b, f_b, pair_of, "z", "x")
+    red_c = Reduction(links, g_c, m_c, r_c, f_c, pair_of)
 
     hidden_grad(dz, w_down, mem_t, dgelu, du)
     hidden_spread(du, w_up, p_da2)
-    copies = group_scatter(links, p_da2, l_da2, group_sems.at[8])
+    copies = group_scatter(links, p_da2, l_da2, pair_of())
     down_proj_grad(hsum, dz, de, pooled, proj, g_a, t)
     red_a.cores()
     row_grad(gp, mem, dx2, t)
@@ -675,14 +698,14 @@
     red_b.scatter()
     finish(copies)
     norm_two_grad(p_da2, l_da2, x1, as_row(gain_two), dx2, dx1, dy, vec, t)
-    copies = group_share(links, dy, group_sems.at[9])
+    copies = group_share(links, dy, pair_of())
     red_a.scatter_second()
     red_b.scatter_second()
     red_a.gather()
     red_b.gather()
     finish(copies)
     attention_grad(dy, w_out, w_qkv, qkv, probs, dqkv, p_da1)
-    copies = group_scatter(links, p_da1, l_da1, group_sems.at[10])
+    copies = group_scatter(links, p_da1, l_da1, pair_of())
     out_qkv_grad(att, dy, dqkv, a1, g_c)
     red_c.cores()
     red_a.gather_second()
@@ -690,24 +713,19 @@
     red_c.scatter()
     finish(copies)
     norm_one_grad(p_da1, l_da1, x, as_row(gain_one), dx1, o_input, vec, t)
-    vec_copies = group_share(links, vec, group_sems.at[11])
+    vec_copies = group_share(links, vec, pair_of())
     red_a.share()
     red_b.share()
     proj_all[core, t] = f_a[core, 3, :3]
-    own = proj_all.at[core, t]
-    proj_copies = [send(own, own, proj_sems, k, links.group_peer(k)) for k in (2, 1, 3)]
+    proj_copies = group_share(links, proj_all.at[core], pair_of())
     finish(vec_copies)
     vec_all[dp] = vec[0] + vec[1] + vec[2] + vec[3]
-    vec_copies = rank_share(links, vec_all, rank_sems.at[1])
+    vec_copies = rank_share(links, vec_all, pair_of())
     red_c.gather()
     finish(proj_copies)
-    own = proj_all.at[core]
-    proj_copies = [send(own, own, proj_sems, 0, links.sibling())]
+    proj_copies = sibling_send(links, proj_all.at[core], proj_all.at[core], pair_of())
     red_a.done()
     red_b.done()
-    stores = [pltpu.make_async_copy(f_a, o_a, store_sems.at[0]), pltpu.make_async_copy(f_b, o_b, store_sems.at[1])]
-    for copy in stores:
-        copy.start()
     finish(vec_copies)
     total = vec_all[0]
     for i in range(1, RANKS):
@@ -715,25 +733,15 @@
     o_norms[...] = total[:, :1536]
     o_loss[...] = total[:, 1536:] * (1.0 / 4096.0)
     finish(proj_copies)
-    stores.append(pltpu.make_async_copy(proj_all, o_proj, store_sems.at[2]))
-    stores[-1].start()
     red_c.share()
     red_c.done()
-    stores.append(pltpu.make_async_copy(f_c, o_c, store_sems.at[3]))
-    stores[-1].start()
-    for copy in stores:
-        copy.wait()
 
 
 def widen(
-    loss, norms, h_input, h_a, h_b, h_c, h_proj,
+    loss, norms, grad, full_a, full_b, full_c, full_proj,
     o_loss, o_input, o_one, o_two, o_down, o_up, o_out, o_qkv, o_proj,
-    grad, full_a, full_b, full_c, full_proj, down, up, out, qkv, proj, loaded, stored,
+    down, up, out, qkv, proj, stored,
 ):
-    sources = ((h_a, full_a), (h_b, full_b), (h_proj, full_proj), (h_c, full_c), (h_input, grad))
-    loads = [pltpu.make_async_copy(src, dst, loaded.at[i]) for i, (src, dst) in enumerate(sources)]
-    for copy in loads:
-        copy.start()
     stores = []
 
     def write(buf, target):
@@ -744,22 +752,17 @@
         for j in range(2):
             target[:, j * HALF : (j + 1) * HALF] = parts[j].reshape(rows, HALF).astype(F32)
 
-    loads[0].wait()
+    write(grad, o_input)
     halves(down, full_a[:, :3], HID)
     write(down, o_down)
-    loads[1].wait()
     halves(up, full_b, D)
     write(up, o_up)
-    loads[2].wait()
     halves(proj, full_proj, D)
     write(proj, o_proj)
-    loads[3].wait()
     halves(out, full_c[:, :4], BAND)
     write(out, o_out)
     halves(qkv, full_c[:, 4:], 3 * BAND)
     write(qkv, o_qkv)
-    loads[4].wait()
-    write(grad, o_input)
     o_loss[0, 0] = loss[0, 0]
     o_one[...] = norms[:, :D].reshape(D)
     o_two[...] = norms[:, D:].reshape(D)
@@ -790,22 +793,22 @@
         VM((CAPS, D), BF16), VM((CAPS, D), BF16), VM((CAPS, D), F32),
         VM((OWN, D), F32), VM((ROWS, HID), BF16), VM((GROUP, OWN, D), BF16), VM((3, OWN, D), BF16), VM((OWN, D), F32),
         VM((GROUP, OWN, D), BF16), VM((3, ROWS, BAND), BF16), VM((GROUP, OWN, D), BF16), VM((3, OWN, D), BF16),
-        VM((GROUP, BAND, D), BF16), VM((2, GROUP, 3, 64, HALF), BF16), VM((GROUP, 1, VEC), F32), VM((RANKS, 1, VEC), F32),
+        VM((GROUP, BAND, D), BF16), VM((GROUP, 1, VEC), F32), VM((RANKS, 1, VEC), F32),
     ]
     scratch += [VM((2,) + s, BF16) for s in sums] + [VM(s, BF16) for s in sums]
     scratch += [VM((3,) + sums[0][1:], BF16), VM((3,) + sums[1][1:], BF16), VM((15,) + sums[2][1:], BF16)]
-    scratch += [VM((3,) + s[2:], BF16) for s in sums[:2]] + [VM((2,) + s, BF16) for s in sums]
-    scratch += [dma((12, 2, 3)), dma((2, 16)), dma((2, 2, 31)), dma((3, 2, 32)), dma((2, 4)), dma((4,))]
+    scratch += [VM((3,) + s[2:], BF16) for s in sums[:2]]
+    scratch += [dma((PAIRS, 2))]
     loss, input_grad, norms, full_a, full_b, full_c, full_proj = pl.pallas_call(
         body,
         out_shape=(
-            shape((1, 128), F32), shape((OWN, D), F32), shape((1, 1536), F32),
-            *(shape((2,) + s, BF16) for s in sums), shape((2, GROUP, 3, 64, HALF), BF16),
+            VM((1, 128), F32), VM((OWN, D), F32), VM((1, 1536), F32),
+            *(VM((2,) + s, BF16) for s in sums), VM((2, GROUP, 3, 64, HALF), BF16),
         ),
         in_specs=[vmem] * 3 + [pl.BlockSpec(memory_space=pltpu.SMEM)] + [vmem] * 4 + [hbm] * 11,
-        out_specs=(vmem, vmem, vmem, hbm, hbm, hbm, hbm),
+        out_specs=(vmem,) * 7,
         scratch_shapes=scratch,
-        compiler_params=pltpu.CompilerParams(collective_id=0, has_side_effects=True, vmem_limit_bytes=63 << 20),
+        compiler_params=pltpu.CompilerParams(collective_id=0, has_side_effects=True, vmem_limit_bytes=57 << 20),
         name="lit",
     )(
         text_input, segment_ids.T, pad_mask.T, pairing, ln_first, ln_second, img_ln_first, img_ln_second,
@@ -819,14 +822,13 @@
             shape((1, 1), F32), shape((OWN, D), F32), shape((D,), F32), shape((D,), F32), shape((HID, D), F32),
             shape((D, HID), F32), shape((BAND, D), F32), shape((3 * BAND, D), F32), shape((D, D), F32),
         ),
-        in_specs=[vmem] * 2 + [hbm] * 5,
+        in_specs=[vmem] * 7,
         out_specs=(pl.BlockSpec(memory_space=pltpu.SMEM), hbm, vmem, vmem, hbm, hbm, hbm, hbm, hbm),
         scratch_shapes=[
-            VM((OWN, D), F32), *(VM((2,) + s, BF16) for s in sums), VM((2, GROUP, 3, 64, HALF), BF16),
             VM((HID, D), F32), VM((D, HID), F32), VM((BAND, D), F32), VM((3 * BAND, D), F32), VM((D, D), F32),
-            dma((5,)), dma((6,)),
+            dma((6,)),
         ],
-        compiler_params=pltpu.CompilerParams(vmem_limit_bytes=60 << 20),
+        compiler_params=pltpu.CompilerParams(vmem_limit_bytes=40 << 20),
         name="widen",
     )(loss, norms, input_grad, full_a, full_b, full_c, full_proj)
     return (loss.reshape(()), input_grad, one, qkv.reshape(3, BAND, D).swapaxes(1, 2), out, two, up, down, proj)

time: 132 us -> 124 us (0.939)
  Pallas kernels: 131 us -> 123 us
    pallas_call x1, Pallas kernels: 125 us -> 119 us  [on_device(): pl.pallas_call(body, out_shape=(VM((1, 128), F32), VM((OWN, D), F32), VM(...]
    pallas_call x1, Pallas kernels: 6.66 us -> 4.45 us  [on_device(): pl.pallas_call(widen, out_shape=(shape((1, 1), F32), shape((OWN, D), F32)...]
where the time goes in v4:
time: 124 us
  Pallas kernels  123 us (99%)
    pallas_call x1, Pallas kernels, on_device(): pl.pallas_call(body, out_shape=(VM((1, 128), F32), VM((OWN, D), F32), VM(...  119 us
    pallas_call x1, Pallas kernels, on_device(): pl.pallas_call(widen, out_shape=(shape((1, 1), F32), shape((OWN, D), F32)...  4.45 us

profile of v4, /device:TPU:1, one launch (start us, length us, event | category | flops | bytes accessed | tf_op | source)
XLA Modules:
  0.0 123.9 jit_solution(4735810983900790899)
XLA Ops:
  0.7 118.6 %lit.1 = (f32[1,128]{1,0:T(1,128)S(1)}, f32[128,768]{1,0:T(8,128)S(1)}, f32[1,1536]{1,0:T(1,128)S(1)}, bf16[2,4,4,64,384]{4,3,2,1,0:T(8,128)(2,1)S(1)}, bf16[2,4...) custom-call(bf16[128,768]{1,0:T(8,128)(2,1)} %x.1, ...), custom_call_target="tpu_custom_call" | custom-call | tf_op jit(solution)/shard_map/lit/pallas_call | solution.py:802
  119.3 4.5 %widen.1 = (f32[1,1]{1,0:T(1,128)}, f32[128,768]{1,0:T(8,128)}, f32[768]{0:T(1024)}, f32[768]{0:T(1024)}, f32[768,768]{1,0:T(8,128)}, /*index=5*/f32[768,768]{1,...) custom-call(f32[1,128]{1,0:T(1,128)S(1)} %get-tuple-element.25.loss, ...), custom_call_target="tpu_custom_call" | custom-call | tf_op jit(solution)/shard_map/widen/pallas_call | solution.py:819

commit v5 on v4

--- a/solution.py
+++ b/solution.py
@@ -172,11 +172,12 @@
 GROUP, RANKS, CHIPS = 4, 32, 16
 OWN, ROWS = 128, 512
 CAPS, OWN_CAPS = 64, 16
+PART = OWN // 2
 BAND = 192
 HALF = 384
 MESH = pl.DeviceIdType.MESH
 VEC = 1664
-PAIRS = 34
+PAIRS = 53
 
 
 class Links:
@@ -232,17 +233,44 @@
         pltpu.make_async_copy(span, span, sems.at[i]).wait()
 
 
+def sent(exchange):
+    sems, span = exchange
+    pltpu.make_async_copy(span, span, sems.at[0]).wait()
+
+
+def arrived(exchange):
+    sems, span = exchange
+    pltpu.make_async_copy(span, span, sems.at[1]).wait()
+
+
 def group_share(links, buf, sems):
     own = buf.at[links.t]
-    for k in (2, 1, 3):
+    for k in (1, 3, 2):
         send(own, own, sems, links.group_peer(k))
     return sems, buf.at[pl.ds(0, 3)]
 
 
 def group_scatter(links, parts, landed, sems):
-    for k in (2, 1, 3):
+    for k in (1, 3, 2):
         send(parts.at[links.rank(k)], landed.at[k - 1], sems, links.group_peer(k))
     return sems, landed
+
+
+def half_rows(h):
+    return pl.ds(h * PART, PART)
+
+
+def share_half(links, buf, sems, h):
+    own = buf.at[links.t, half_rows(h)]
+    for k in (1, 3, 2):
+        send(own, own, sems, links.group_peer(k))
+    return sems, buf.at[pl.ds(0, 3), half_rows(h)]
+
+
+def scatter_half(links, parts, landed, sems, h):
+    for k in (1, 3, 2):
+        send(parts.at[links.rank(k), half_rows(h)], landed.at[k - 1, half_rows(h)], sems, links.group_peer(k))
+    return sems, landed.at[pl.ds(0, 3), half_rows(h)]
 
 
 def rank_share(links, buf, sems):
@@ -319,8 +347,8 @@
     parts[...] = dot(att[...], w_out[...]).astype(BF16).reshape(GROUP, OWN, D)
 
 
-def summed(parts, landed, t):
-    return parts[t].astype(F32) + landed[0].astype(F32) + landed[1].astype(F32) + landed[2].astype(F32)
+def summed(parts, landed, t, rows):
+    return parts[t, rows].astype(F32) + landed[0, rows].astype(F32) + landed[1, rows].astype(F32) + landed[2, rows].astype(F32)
 
 
 def split3(x):
@@ -334,11 +362,12 @@
     return mem[pl.ds(pl.multiple_of(t * OWN_CAPS, OWN_CAPS), OWN_CAPS), pl.ds(pl.multiple_of(t * OWN, OWN), OWN)]
 
 
-def text_norm_two(x, parts, landed, gain, mem, x1, a2, x1_pool, t):
-    y = x[...].astype(F32) + summed(parts, landed, t)
-    x1[...] = y
+def text_norm_two(h, x, parts, landed, gain, x1, a2, t):
+    rows = half_rows(h)
+    y = x[rows, :].astype(F32) + summed(parts, landed, t, rows)
+    x1[rows, :] = y
     n, _ = normalized(y)
-    a2[t] = (n * gain).astype(BF16)
+    a2[t, rows] = (n * gain).astype(BF16)
 
 
 def text_pool_one(x1, mem, x1_pool, t):
@@ -379,12 +408,14 @@
     s_ref[...] = s
     e = jnp.exp(s - 40.0)
     e_ref[...] = e
-    row_sums[t] = jnp.broadcast_to(jnp.sum(e, axis=1, keepdims=True), (CAPS, 128))
+    diagonal = iota((CAPS, 128), 0) == iota((CAPS, 128), 1)
+    row_sums[t] = jnp.sum(jnp.where(diagonal, jnp.sum(e, axis=1, keepdims=True), 0.0), axis=0, keepdims=True)
     col_sums[dp] = jnp.sum(e, axis=0, keepdims=True)
 
 
 def score_grad(s_ref, e_ref, row_sums, col_sums, pair, images, dts, vec, t):
-    rows = jnp.sum(row_sums[...], axis=0)[:, :1]
+    diagonal = iota((CAPS, 128), 0) == iota((CAPS, 128), 1)
+    rows = jnp.sum(jnp.where(diagonal, row_sums[0] + row_sums[1] + row_sums[2] + row_sums[3], 0.0), axis=1, keepdims=True)
     cols = col_sums[0]
     for i in range(1, RANKS):
         cols = cols + col_sums[i]
@@ -417,52 +448,62 @@
     dx2[...] = t_dot(jnp.concatenate([own, own, own], axis=0), split3(gp))
 
 
-def hidden_grad(dz, w_down, mem_t, dgelu, du):
-    dh = split_rows(dot_t(dz[...], w_down[...]))
-    for i in range(3):
-        s = slice(i * TILE, i * TILE + TILE)
-        du[:, s] = (dot(mem_t[...], dh[:, s]) * dgelu[:, s]).astype(BF16)
-
-
-def hidden_spread(du, w_up, parts):
-    parts[...] = dot_t(du[...], w_up[...]).astype(BF16).reshape(GROUP, OWN, D)
-
-
-def put_halves(g, first, count, rows, values):
-    for j in range(2):
-        part = values[:, j * HALF : (j + 1) * HALF].reshape(count, rows, HALF).astype(BF16)
-        if len(g.shape) == 4:
-            g[j, first : first + count] = part
-        elif count == 3:
-            g[j, first // 4, :3] = part
-        else:
-            g[j, first // 4 : (first + count) // 4] = part.reshape(count // 4, 4, rows, HALF)
-
-
-def down_proj_grad(hsum, dz, de, pooled, proj, g, t):
+def hidden_grad(dz, w_down):
+    return split_rows(dot_t(dz[...], w_down[...]))
+
+
+def hidden_spread(h, dh, mem_t, dgelu, w_up, du, parts):
+    blocks = [pl.ds(r * OWN + h * PART, PART) for r in range(GROUP)]
+    member = jnp.concatenate([mem_t[b, :] for b in blocks], axis=0)
+    slope = jnp.concatenate([dgelu[b, :] for b in blocks], axis=0)
+    rows = (dot(member, dh) * slope).astype(BF16)
+    total = dot_t(rows, w_up[...]).astype(BF16)
+    for r, b in enumerate(blocks):
+        du[b, :] = rows[r * PART : (r + 1) * PART]
+        parts[r, half_rows(h)] = total[r * PART : (r + 1) * PART]
+
+
+def gain_grad(parts, normed, gain):
+    total = jnp.zeros((1, D), F32)
+    for r in range(GROUP):
+        total = total + jnp.sum(parts[r].astype(F32) * normed[r].astype(F32), axis=0, keepdims=True)
+    return total / gain
+
+
+def put_chunks(g, first, values):
+    rows = g.shape[-2]
+    for c in range(values.shape[0] // rows):
+        at = first + c
+        place = (at,) if len(g.shape) == 4 else (at // 4, at % 4)
+        for j in range(2):
+            g[(j, *place)] = values[c * rows : (c + 1) * rows, j * HALF : (j + 1) * HALF].astype(BF16)
+
+
+def down_proj_grad(hsum, dz, de, pooled, proj, g, h, t):
     hs = split_rows(hsum[...])
     dz2 = jnp.concatenate([dz[...], dz[...]], axis=0)
+    put_chunks(g, 0, t_dot(hs[:, :256], dz2))
+    put_chunks(g, 8, t_dot(hs[:, 256:512], dz2))
+    put_chunks(h, 0, t_dot(hs[:, 512:], dz2))
+    proj[...] = t_dot(pooled[...], de[...]).astype(BF16).reshape(GROUP, BAND, D)
+    put_chunks(h, 8, proj[t])
+    h[:, 3, 2:] = jnp.zeros((2, 2, 32, HALF), BF16)
+
+
+def up_grad(a2, du, g, h):
     for i in range(3):
-        put_halves(g, 4 * i, 4, 64, t_dot(hs[:, i * TILE : (i + 1) * TILE], dz2))
-    proj[...] = t_dot(pooled[...], de[...]).astype(BF16).reshape(GROUP, BAND, D)
-    put_halves(g, 12, 3, 64, proj[t])
-    g[:, 3, 3] = jnp.zeros((2, 64, HALF), BF16)
-
-
-def up_grad(a2, du, g):
-    for i in range(2):
-        rows = a2[:, :, i * HALF : (i + 1) * HALF].reshape(ROWS, HALF)
-        put_halves(g, 8 * i, 8, 48, t_dot(rows, du[...]))
-
-
-def norm_two_grad(parts, landed, x1, gain, dx2, dx1, dy, vec, t):
-    da = summed(parts, landed, t)
-    n, scale = normalized(x1[...])
-    vec[t, :, 768:1536] = jnp.sum(da * n, axis=0, keepdims=True)
-    h = da * gain
-    g = dx2[...] + (h - jnp.mean(h, axis=-1, keepdims=True) - n * jnp.mean(h * n, axis=-1, keepdims=True)) * scale
-    dx1[...] = g
-    dy[t] = g.astype(BF16)
+        rows = t_dot(a2[:, :, i * 256 : (i + 1) * 256].reshape(ROWS, 256), du[...])
+        put_chunks(g if i < 2 else h, 8 * i if i < 2 else 0, rows)
+
+
+def norm_two_grad(h, parts, landed, x1, gain, dx2, dx1, dy, t):
+    rows = half_rows(h)
+    da = summed(parts, landed, t, rows)
+    n, scale = normalized(x1[rows, :])
+    d = da * gain
+    g = dx2[rows, :] + (d - jnp.mean(d, axis=-1, keepdims=True) - n * jnp.mean(d * n, axis=-1, keepdims=True)) * scale
+    dx1[rows, :] = g
+    dy[t, rows] = g.astype(BF16)
 
 
 def attention_grad(dy, w_out, w_t, qkv, probs, dqkv, parts):
@@ -489,16 +530,22 @@
     parts[...] = total.astype(BF16).reshape(GROUP, OWN, D)
 
 
-def out_qkv_grad(att, dy, dqkv, a1, g):
-    put_halves(g, 0, 4, 48, t_dot(att[...], dy[...].reshape(ROWS, D)))
-    for j in range(3):
-        put_halves(g, 4 + 4 * j, 4, 48, t_dot(dqkv[j], a1[...].reshape(ROWS, D)))
-
-
-def norm_one_grad(parts, landed, x, gain, dx1, out, vec, t):
-    da = summed(parts, landed, t)
+def out_grad(att, dy, g):
+    put_chunks(g, 0, t_dot(att[...], dy[...].reshape(ROWS, D)))
+
+
+def qkv_grad(dqkv, a1, g, h):
+    rows = a1[...].reshape(ROWS, D)
+    put_chunks(g, 6, t_dot(dqkv[0], rows))
+    keys = t_dot(dqkv[1], rows)
+    put_chunks(g, 12, keys[:128])
+    put_chunks(h, 0, keys[128:])
+    put_chunks(h, 4, t_dot(dqkv[2], rows))
+
+
+def norm_one_grad(parts, landed, x, gain, dx1, out, t):
+    da = summed(parts, landed, t, slice(0, OWN))
     n, scale = normalized(x[...].astype(F32))
-    vec[t, :, :768] = jnp.sum(da * n, axis=0, keepdims=True)
     h = da * gain
     out[...] = dx1[...] + (h - jnp.mean(h, axis=-1, keepdims=True) - n * jnp.mean(h * n, axis=-1, keepdims=True)) * scale
 
@@ -547,7 +594,7 @@
 
     def spread(self, axis, source, target):
         sems = self.pair()
-        for k in (2, 1, 3):
+        for k in (1, 3, 2):
             send(source(k), target(k), sems, self.links.axis_peer(axis, k))
         return sems
 
@@ -588,15 +635,17 @@
 def body(
     x, seg_t, pad_t, pair_in, gain_one, gain_two, img_gain_one, img_gain_two,
     h_tok, h_iqkv, h_iout, h_iup, h_idown, h_iproj, h_qkv, h_out, h_up, h_down, h_proj,
-    o_loss, o_input, o_norms, f_a, f_b, f_c, proj_all,
+    o_loss, o_input, o_norms, f_a0, f_a1, f_b0, f_b1, f_c0, f_c1, proj_all,
     tok, iw_qkv, iw_out, iw_up, iw_down, iw_proj, w_qkv, w_out, w_up, w_down, w_proj, load,
     ibias, iap, iqkv, stage, iy, ypool, ihsum, images,
     bias, mem, mem_t, pair, a1, qkv, probs, att, p_att, l_att, x1, x1_pool, a2, dgelu, hsum, p_pool, pools,
     tf, scale, pooled, s_ref, e_ref, row_sums, col_sums, dts, de, dz, gp, dx2, du, p_da2, l_da2, dx1, dy,
     dqkv, p_da1, l_da1, proj, vec, vec_all,
-    g_a, g_b, g_c, m_a, m_b, m_c, r_a, r_b, r_c, n_a, n_b,
-    sems,
+    *work,
 ):
+    g_a, g_b, g_c, m_a, m_b, m_c, r_a, r_b, r_c, n_a, n_b = (work[i : i + 2] for i in range(0, 22, 2))
+    f_a, f_b, f_c = (f_a0, f_a1), (f_b0, f_b1), (f_c0, f_c1)
+    sems = work[22]
     links = Links()
     t, dp, core, chip = links.t, links.dp, links.core, links.chip
     loads = {}
@@ -640,18 +689,23 @@
     loads["qkv"].wait()
     loads["out"].wait()
     text_attention(a1, w_qkv, bias, w_out, qkv, probs, att, p_att)
-    copies = group_scatter(links, p_att, l_att, pair_of())
-
-    image_attention(iqkv, ibias, stage, 0, 8)
+    copies = [scatter_half(links, p_att, l_att, pair_of(), 0)]
+
+    image_attention(iqkv, ibias, stage, 0, 4)
+    copies.append(scatter_half(links, p_att, l_att, pair_of(), 1))
+    image_attention(iqkv, ibias, stage, 4, 8)
+    finish(copies[0])
+    text_norm_two(0, x, p_att, l_att, as_row(gain_two), x1, a2, t)
+    copies[0] = share_half(links, a2, pair_of(), 0)
     loads["iout"].wait()
     image_out(stage, tok, iw_out, iy)
+    finish(copies[1])
+    text_norm_two(1, x, p_att, l_att, as_row(gain_two), x1, a2, t)
+    copies[1] = share_half(links, a2, pair_of(), 1)
     image_norm_two(iy, as_row(img_gain_two), iap.at[:IROWS], ypool)
 
     loads["iup"].wait()
     image_up(iap.at[:IROWS], iw_up, ihsum, 0, 1)
-    finish(copies)
-    text_norm_two(x, p_att, l_att, as_row(gain_two), mem, x1, a2, x1_pool, t)
-    copies = group_share(links, a2, pair_of())
     text_pool_one(x1, mem, x1_pool, t)
 
     image_up(iap.at[:IROWS], iw_up, ihsum, 1, FF // UP_TILE)
@@ -660,7 +714,8 @@
     images[core, chip] = image_finish(ihsum, ypool, iw_down, iw_proj)
     image_copies = chip_share(links, images.at[core], pair_of())
 
-    finish(copies)
+    finish(copies[0])
+    finish(copies[1])
     loads["up"].wait()
     loads["down"].wait()
     text_up(a2, w_up, mem, w_down, x1_pool, dgelu, du, hsum, p_pool, pools, t)
@@ -674,58 +729,69 @@
     finish(image_copies)
 
     score_sums(tf, images, s_ref, e_ref, row_sums, col_sums, t, dp)
+    row_copies = group_share(links, row_sums, pair_of())
     col_copies = rank_share(links, col_sums, pair_of())
-    row_copies = group_share(links, row_sums, pair_of())
     finish(col_copies)
     finish(row_copies)
     score_grad(s_ref, e_ref, row_sums, col_sums, pair, images, dts, vec, t)
     finish(group_share(links, dts, pair_of()))
     embed_grad(dts, tf, scale, w_proj, mem, de, dz, gp)
 
-    red_a = TwoAxes(links, g_a, m_a, r_a, n_a, f_a, pair_of, "x", "z")
-    red_b = TwoAxes(links, g_b, m_b, r_b, n_b, f_b, pair_of, "z", "x")
-    red_c = Reduction(links, g_c, m_c, r_c, f_c, pair_of)
-
-    hidden_grad(dz, w_down, mem_t, dgelu, du)
-    hidden_spread(du, w_up, p_da2)
-    copies = group_scatter(links, p_da2, l_da2, pair_of())
-    down_proj_grad(hsum, dz, de, pooled, proj, g_a, t)
-    red_a.cores()
+    red_a = [TwoAxes(links, g_a[i], m_a[i], r_a[i], n_a[i], f_a[i], pair_of, "x", "z") for i in range(2)]
+    red_b = [TwoAxes(links, g_b[i], m_b[i], r_b[i], n_b[i], f_b[i], pair_of, "z", "x") for i in range(2)]
+    red_c = [Reduction(links, g_c[i], m_c[i], r_c[i], f_c[i], pair_of) for i in range(2)]
+
+    def each(*steps):
+        for step in steps:
+            step()
+
+    dh = hidden_grad(dz, w_down)
+    hidden_spread(0, dh, mem_t, dgelu, w_up, du, p_da2)
+    copies = [scatter_half(links, p_da2, l_da2, pair_of(), 0)]
+    hidden_spread(1, dh, mem_t, dgelu, w_up, du, p_da2)
+    down_proj_grad(hsum, dz, de, pooled, proj, g_a[0], g_a[1], t)
+    each(red_a[0].cores, red_a[1].cores)
+    up_grad(a2, du, g_b[0], g_b[1])
+    each(red_b[0].cores, red_b[1].cores)
+    sent(copies[0])
+    copies.append(scatter_half(links, p_da2, l_da2, pair_of(), 1))
     row_grad(gp, mem, dx2, t)
-    up_grad(a2, du, g_b)
-    red_b.cores()
-    red_a.scatter()
-    red_b.scatter()
-    finish(copies)
-    norm_two_grad(p_da2, l_da2, x1, as_row(gain_two), dx2, dx1, dy, vec, t)
-    copies = group_share(links, dy, pair_of())
-    red_a.scatter_second()
-    red_b.scatter_second()
-    red_a.gather()
-    red_b.gather()
-    finish(copies)
+    vec[t, :, 768:1536] = gain_grad(p_da2, a2, as_row(gain_two))
+    each(red_a[0].scatter, red_b[0].scatter, red_a[1].scatter, red_b[1].scatter)
+    arrived(copies[0])
+    norm_two_grad(0, p_da2, l_da2, x1, as_row(gain_two), dx2, dx1, dy, t)
+    copies[0] = share_half(links, dy, pair_of(), 0)
+    finish(copies[1])
+    norm_two_grad(1, p_da2, l_da2, x1, as_row(gain_two), dx2, dx1, dy, t)
+    copies[1] = share_half(links, dy, pair_of(), 1)
+    each(red_a[0].scatter_second, red_b[0].scatter_second)
+    each(red_a[1].scatter_second, red_b[1].scatter_second)
+    each(red_a[0].gather, red_b[0].gather)
+    each(red_a[1].gather, red_b[1].gather)
+    each(red_a[0].gather_second, red_b[0].gather_second)
+    finish(copies[0])
+    finish(copies[1])
+    each(red_a[1].gather_second, red_b[1].gather_second)
+    out_grad(att, dy, g_c[0])
     attention_grad(dy, w_out, w_qkv, qkv, probs, dqkv, p_da1)
+    vec[t, :, :768] = gain_grad(p_da1, a1, as_row(gain_one))
+    vec_copies = group_share(links, vec, pair_of())
     copies = group_scatter(links, p_da1, l_da1, pair_of())
-    out_qkv_grad(att, dy, dqkv, a1, g_c)
-    red_c.cores()
-    red_a.gather_second()
-    red_b.gather_second()
-    red_c.scatter()
-    finish(copies)
-    norm_one_grad(p_da1, l_da1, x, as_row(gain_one), dx1, o_input, vec, t)
-    vec_copies = group_share(links, vec, pair_of())
-    red_a.share()
-    red_b.share()
-    proj_all[core, t] = f_a[core, 3, :3]
-    proj_copies = group_share(links, proj_all.at[core], pair_of())
+    qkv_grad(dqkv, a1, g_c[0], g_c[1])
+    each(red_c[0].cores, red_c[1].cores, red_c[0].scatter, red_c[1].scatter)
     finish(vec_copies)
     vec_all[dp] = vec[0] + vec[1] + vec[2] + vec[3]
     vec_copies = rank_share(links, vec_all, pair_of())
-    red_c.gather()
+    each(red_a[1].share, red_a[0].share, red_b[0].share, red_b[1].share)
+    proj_all[core, t, :4] = f_a1[core, 2]
+    proj_all[core, t, 4:] = f_a1[core, 3, :2]
+    proj_copies = group_share(links, proj_all.at[core], pair_of())
+    each(red_c[0].gather, red_c[1].gather)
+    finish(copies)
+    norm_one_grad(p_da1, l_da1, x, as_row(gain_one), dx1, o_input, t)
     finish(proj_copies)
     proj_copies = sibling_send(links, proj_all.at[core], proj_all.at[core], pair_of())
-    red_a.done()
-    red_b.done()
+    each(red_a[0].done, red_a[1].done, red_b[0].done, red_b[1].done)
     finish(vec_copies)
     total = vec_all[0]
     for i in range(1, RANKS):
@@ -733,14 +799,12 @@
     o_norms[...] = total[:, :1536]
     o_loss[...] = total[:, 1536:] * (1.0 / 4096.0)
     finish(proj_copies)
-    red_c.share()
-    red_c.done()
+    each(red_c[0].share, red_c[1].share, red_c[0].done, red_c[1].done)
 
 
 def widen(
-    loss, norms, grad, full_a, full_b, full_c, full_proj,
-    o_loss, o_input, o_one, o_two, o_down, o_up, o_out, o_qkv, o_proj,
-    down, up, out, qkv, proj, stored,
+    loss, norms, grad, a0, a1, b0, b1, c0, c1, full_proj,
+    o_loss, o_input, o_one, o_two, o_down, o_up, o_out, o_qkv, o_proj, down, up, out, qkv, proj, stored,
 ):
     stores = []
 
@@ -748,20 +812,23 @@
         stores.append(pltpu.make_async_copy(buf, target, stored.at[len(stores)]))
         stores[-1].start()
 
-    def halves(target, parts, rows):
+    def halves(target, first, parts, rows):
         for j in range(2):
-            target[:, j * HALF : (j + 1) * HALF] = parts[j].reshape(rows, HALF).astype(F32)
+            target[first : first + rows, j * HALF : (j + 1) * HALF] = parts[j].reshape(rows, HALF).astype(F32)
 
     write(grad, o_input)
-    halves(down, full_a[:, :3], HID)
+    halves(down, 0, a0, 512)
+    halves(down, 512, a1[:, :2], 256)
     write(down, o_down)
-    halves(up, full_b, D)
+    halves(up, 0, b0, 512)
+    halves(up, 512, b1, 256)
     write(up, o_up)
-    halves(proj, full_proj, D)
+    halves(proj, 0, full_proj, D)
     write(proj, o_proj)
-    halves(out, full_c[:, :4], BAND)
+    halves(out, 0, c0[:, :6], BAND)
     write(out, o_out)
-    halves(qkv, full_c[:, 4:], 3 * BAND)
+    halves(qkv, 0, c0[:, 6:], 320)
+    halves(qkv, 320, c1, 256)
     write(qkv, o_qkv)
     o_loss[0, 0] = loss[0, 0]
     o_one[...] = norms[:, :D].reshape(D)
@@ -777,7 +844,7 @@
     vmem = pl.BlockSpec(memory_space=VM)
     hbm = pl.BlockSpec(memory_space=pl.ANY)
     shape = jax.ShapeDtypeStruct
-    sums = ((4, 4, 64, HALF), (4, 4, 48, HALF), (16, 48, HALF))
+    sums = ((4, 4, 32, HALF),) * 2 + ((4, 4, 32, HALF), (4, 4, 16, HALF)) + ((16, 32, HALF), (16, 16, HALF))
     dma = pltpu.SemaphoreType.DMA
     scratch = [
         VM((IROWS, D), BF16), VM((3, D, D), BF16), VM((D, D), BF16), VM((D, FF), BF16), VM((FF, D), BF16), VM((D, D), BF16),
@@ -789,24 +856,23 @@
         VM((GROUP, OWN, D), BF16), VM((3, OWN, D), BF16), VM((OWN, D), F32), VM((OWN_CAPS, D), F32), VM((GROUP, OWN, D), BF16),
         VM((ROWS, HID), F32), VM((CAPS, HID), F32), VM((GROUP, OWN_CAPS, D), F32), VM((GROUP, CAPS, D), BF16),
         VM((CAPS, D), F32), VM((CAPS, 128), F32), VM((CAPS, D), BF16), VM((CAPS, ROWS), F32),
-        VM((CAPS, ROWS), F32), VM((GROUP, CAPS, 128), F32), VM((RANKS, 1, ROWS), F32), VM((GROUP, CAPS, D), BF16),
+        VM((CAPS, ROWS), F32), VM((GROUP, 1, 128), F32), VM((RANKS, 1, ROWS), F32), VM((GROUP, CAPS, D), BF16),
         VM((CAPS, D), BF16), VM((CAPS, D), BF16), VM((CAPS, D), F32),
         VM((OWN, D), F32), VM((ROWS, HID), BF16), VM((GROUP, OWN, D), BF16), VM((3, OWN, D), BF16), VM((OWN, D), F32),
         VM((GROUP, OWN, D), BF16), VM((3, ROWS, BAND), BF16), VM((GROUP, OWN, D), BF16), VM((3, OWN, D), BF16),
         VM((GROUP, BAND, D), BF16), VM((GROUP, 1, VEC), F32), VM((RANKS, 1, VEC), F32),
     ]
     scratch += [VM((2,) + s, BF16) for s in sums] + [VM(s, BF16) for s in sums]
-    scratch += [VM((3,) + sums[0][1:], BF16), VM((3,) + sums[1][1:], BF16), VM((15,) + sums[2][1:], BF16)]
-    scratch += [VM((3,) + s[2:], BF16) for s in sums[:2]]
-    scratch += [dma((PAIRS, 2))]
-    loss, input_grad, norms, full_a, full_b, full_c, full_proj = pl.pallas_call(
+    scratch += [VM((3,) + s[1:], BF16) for s in sums[:4]] + [VM((15,) + s[1:], BF16) for s in sums[4:]]
+    scratch += [VM((3,) + s[2:], BF16) for s in sums[:4]] + [dma((PAIRS, 2))]
+    loss, input_grad, norms, *full = pl.pallas_call(
         body,
         out_shape=(
             VM((1, 128), F32), VM((OWN, D), F32), VM((1, 1536), F32),
-            *(VM((2,) + s, BF16) for s in sums), VM((2, GROUP, 3, 64, HALF), BF16),
+            *(VM((2,) + s, BF16) for s in sums), VM((2, GROUP, 6, 32, HALF), BF16),
         ),
         in_specs=[vmem] * 3 + [pl.BlockSpec(memory_space=pltpu.SMEM)] + [vmem] * 4 + [hbm] * 11,
-        out_specs=(vmem,) * 7,
+        out_specs=(vmem,) * 10,
         scratch_shapes=scratch,
         compiler_params=pltpu.CompilerParams(collective_id=0, has_side_effects=True, vmem_limit_bytes=57 << 20),
         name="lit",
@@ -822,7 +888,7 @@
             shape((1, 1), F32), shape((OWN, D), F32), shape((D,), F32), shape((D,), F32), shape((HID, D), F32),
             shape((D, HID), F32), shape((BAND, D), F32), shape((3 * BAND, D), F32), shape((D, D), F32),
         ),
-        in_specs=[vmem] * 7,
+        in_specs=[vmem] * 10,
         out_specs=(pl.BlockSpec(memory_space=pltpu.SMEM), hbm, vmem, vmem, hbm, hbm, hbm, hbm, hbm),
         scratch_shapes=[
             VM((HID, D), F32), VM((D, HID), F32), VM((BAND, D), F32), VM((3 * BAND, D), F32), VM((D, D), F32),
@@ -830,7 +896,7 @@
         ],
         compiler_params=pltpu.CompilerParams(vmem_limit_bytes=40 << 20),
         name="widen",
-    )(loss, norms, input_grad, full_a, full_b, full_c, full_proj)
+    )(loss, norms, input_grad, *full)
     return (loss.reshape(()), input_grad, one, qkv.reshape(3, BAND, D).swapaxes(1, 2), out, two, up, down, proj)
 
 

time: 124 us -> 119 us (0.960)
  Pallas kernels: 123 us -> 118 us
    pallas_call x1, Pallas kernels: 119 us -> 114 us  [on_device(): pl.pallas_call(body, out_shape=(VM((1, 128), F32), VM((OWN, D), F32), VM(...]
where the time goes in v5:
time: 119 us
  Pallas kernels  118 us (99%)
    pallas_call x1, Pallas kernels, on_device(): pl.pallas_call(body, out_shape=(VM((1, 128), F32), VM((OWN, D), F32), VM(...  114 us
    pallas_call x1, Pallas kernels, on_device(): pl.pallas_call(widen, out_shape=(shape((1, 1), F32), shape((OWN, D), F32)...  4.45 us

profile of v5, /device:TPU:1, one launch (start us, length us, event | category | flops | bytes accessed | tf_op | source)
XLA Modules:
  0.0 119.1 jit_solution(749687684018326485)
XLA Ops:
  0.7 113.9 %lit.1 = (f32[1,128]{1,0:T(1,128)S(1)}, f32[128,768]{1,0:T(8,128)S(1)}, f32[1,1536]{1,0:T(1,128)S(1)}, bf16[2,4,4,32,384]{4,3,2,1,0:T(8,128)(2,1)S(1)}, bf16[2,4...) custom-call(bf16[128,768]{1,0:T(8,128)(2,1)} %x.1, ...), custom_call_target="tpu_custom_call" | custom-call | tf_op jit(solution)/shard_map/lit/pallas_call | solution.py:868
  114.5 4.4 %widen.1 = (f32[1,1]{1,0:T(1,128)}, f32[128,768]{1,0:T(8,128)}, f32[768]{0:T(1024)}, f32[768]{0:T(1024)}, f32[768,768]{1,0:T(8,128)}, /*index=5*/f32[768,768]{1,...) custom-call(f32[1,128]{1,0:T(1,128)S(1)} %get-tuple-element.28.loss, ...), custom_call_target="tpu_custom_call" | custom-call | tf_op jit(solution)/shard_map/widen/pallas_call | solution.py:885

commit v6 on v5

--- a/solution.py
+++ b/solution.py
@@ -771,9 +771,9 @@
     each(red_a[0].gather_second, red_b[0].gather_second)
     finish(copies[0])
     finish(copies[1])
-    each(red_a[1].gather_second, red_b[1].gather_second)
     out_grad(att, dy, g_c[0])
     attention_grad(dy, w_out, w_qkv, qkv, probs, dqkv, p_da1)
+    each(red_a[1].gather_second, red_b[1].gather_second)
     vec[t, :, :768] = gain_grad(p_da1, a1, as_row(gain_one))
     vec_copies = group_share(links, vec, pair_of())
     copies = group_scatter(links, p_da1, l_da1, pair_of())
@@ -786,9 +786,9 @@
     proj_all[core, t, :4] = f_a1[core, 2]
     proj_all[core, t, 4:] = f_a1[core, 3, :2]
     proj_copies = group_share(links, proj_all.at[core], pair_of())
-    each(red_c[0].gather, red_c[1].gather)
     finish(copies)
     norm_one_grad(p_da1, l_da1, x, as_row(gain_one), dx1, o_input, t)
+    each(red_c[0].gather, red_c[1].gather)
     finish(proj_copies)
     proj_copies = sibling_send(links, proj_all.at[core], proj_all.at[core], pair_of())
     each(red_a[0].done, red_a[1].done, red_b[0].done, red_b[1].done)

time: 119 us -> 117 us (0.983)
  Pallas kernels: 118 us -> 116 us
    pallas_call x1, Pallas kernels: 114 us -> 112 us  [on_device(): pl.pallas_call(body, out_shape=(VM((1, 128), F32), VM((OWN, D), F32), VM(...]
where the time goes in v6:
time: 117 us
  Pallas kernels  116 us (99%)
    pallas_call x1, Pallas kernels, on_device(): pl.pallas_call(body, out_shape=(VM((1, 128), F32), VM((OWN, D), F32), VM(...  112 us
    pallas_call x1, Pallas kernels, on_device(): pl.pallas_call(widen, out_shape=(shape((1, 1), F32), shape((OWN, D), F32)...  4.45 us

profile of v6, /device:TPU:1, one launch (start us, length us, event | category | flops | bytes accessed | tf_op | source)
XLA Modules:
  0.0 116.9 jit_solution(17199309565537931907)
XLA Ops:
  0.7 111.6 %lit.1 = (f32[1,128]{1,0:T(1,128)S(1)}, f32[128,768]{1,0:T(8,128)S(1)}, f32[1,1536]{1,0:T(1,128)S(1)}, bf16[2,4,4,32,384]{4,3,2,1,0:T(8,128)(2,1)S(1)}, bf16[2,4...) custom-call(bf16[128,768]{1,0:T(8,128)(2,1)} %x.1, ...), custom_call_target="tpu_custom_call" | custom-call | tf_op jit(solution)/shard_map/lit/pallas_call | solution.py:868
  112.3 4.4 %widen.1 = (f32[1,1]{1,0:T(1,128)}, f32[128,768]{1,0:T(8,128)}, f32[768]{0:T(1024)}, f32[768]{0:T(1024)}, f32[768,768]{1,0:T(8,128)}, /*index=5*/f32[768,768]{1,...) custom-call(f32[1,128]{1,0:T(1,128)S(1)} %get-tuple-element.28.loss, ...), custom_call_target="tpu_custom_call" | custom-call | tf_op jit(solution)/shard_map/widen/pallas_call | solution.py:885

commit v7 on v6

--- a/solution.py
+++ b/solution.py
@@ -177,7 +177,7 @@
 HALF = 384
 MESH = pl.DeviceIdType.MESH
 VEC = 1664
-PAIRS = 53
+PAIRS = 55
 
 
 class Links:
@@ -192,9 +192,6 @@
     def group_peer(self, k):
         return {"dp": self.dp, "tensor": self.rank(k)}
 
-    def rank_peer(self, k):
-        return {"dp": lax.rem(self.dp + k, RANKS), "tensor": self.t}
-
     def chip_of(self, k):
         return lax.rem(self.chip + k, CHIPS)
 
@@ -216,11 +213,12 @@
         barrier = pltpu.get_barrier_semaphore()
         for k in range(1, GROUP):
             pl.semaphore_signal(barrier, 1, device_id=self.group_peer(k), device_id_type=MESH)
-        for k in range(1, RANKS):
-            pl.semaphore_signal(barrier, 1, device_id=self.rank_peer(k), device_id_type=MESH)
+        for k in range(1, CHIPS):
+            pl.semaphore_signal(barrier, 1, device_id=self.chip_peer(k), device_id_type=MESH)
+        pl.semaphore_signal(barrier, 1, device_id=self.sibling(), device_id_type=MESH)
 
     def met(self):
-        pl.semaphore_wait(pltpu.get_barrier_semaphore(), GROUP - 1 + RANKS - 1)
+        pl.semaphore_wait(pltpu.get_barrier_semaphore(), GROUP - 1 + CHIPS)
 
 
 def send(src, dst, sems, peer):
@@ -273,16 +271,14 @@
     return sems, landed.at[pl.ds(0, 3), half_rows(h)]
 
 
-def rank_share(links, buf, sems):
-    own = buf.at[links.dp]
-    for k in range(1, RANKS):
-        send(own, own, sems, links.rank_peer(k))
-    return sems, buf.at[pl.ds(0, RANKS - 1)]
+def distance(k):
+    x, z = k // 2 % 4, k // 8
+    return -(min(x, 4 - x) + min(z, 4 - z))
 
 
 def chip_share(links, buf, sems):
     own = buf.at[links.chip]
-    for k in range(1, CHIPS):
+    for k in sorted(range(1, CHIPS), key=lambda k: distance(2 * k)):
         send(own, own, sems, links.chip_peer(k))
     return sems, buf.at[pl.ds(0, CHIPS - 1)]
 
@@ -403,21 +399,21 @@
     scale[...] = jnp.broadcast_to(rs, (CAPS, 128))
 
 
-def score_sums(tf, images, s_ref, e_ref, row_sums, col_sums, t, dp):
+def score_sums(tf, images, s_ref, e_ref, row_sums, col_sums, t):
     s = 40.0 * dot_t(tf[...].astype(BF16), images[...].reshape(ROWS, D))
     s_ref[...] = s
     e = jnp.exp(s - 40.0)
     e_ref[...] = e
     diagonal = iota((CAPS, 128), 0) == iota((CAPS, 128), 1)
     row_sums[t] = jnp.sum(jnp.where(diagonal, jnp.sum(e, axis=1, keepdims=True), 0.0), axis=0, keepdims=True)
-    col_sums[dp] = jnp.sum(e, axis=0, keepdims=True)
+    col_sums[0] = jnp.sum(e, axis=0, keepdims=True)
 
 
 def score_grad(s_ref, e_ref, row_sums, col_sums, pair, images, dts, vec, t):
     diagonal = iota((CAPS, 128), 0) == iota((CAPS, 128), 1)
     rows = jnp.sum(jnp.where(diagonal, row_sums[0] + row_sums[1] + row_sums[2] + row_sums[3], 0.0), axis=1, keepdims=True)
     cols = col_sums[0]
-    for i in range(1, RANKS):
+    for i in range(1, CHIPS):
         cols = cols + col_sums[i]
     lane = iota((CAPS, ROWS), 1)
     image = ((lane >> 4) & 15) * (2 * CAPS) + (lane >> 8) * CAPS + (lane & 15) + OWN_CAPS * t
@@ -639,8 +635,8 @@
     tok, iw_qkv, iw_out, iw_up, iw_down, iw_proj, w_qkv, w_out, w_up, w_down, w_proj, load,
     ibias, iap, iqkv, stage, iy, ypool, ihsum, images,
     bias, mem, mem_t, pair, a1, qkv, probs, att, p_att, l_att, x1, x1_pool, a2, dgelu, hsum, p_pool, pools,
-    tf, scale, pooled, s_ref, e_ref, row_sums, col_sums, dts, de, dz, gp, dx2, du, p_da2, l_da2, dx1, dy,
-    dqkv, p_da1, l_da1, proj, vec, vec_all,
+    tf, scale, pooled, s_ref, e_ref, row_sums, core_sums, col_sums, dts, de, dz, gp, dx2, du, p_da2, l_da2, dx1, dy,
+    dqkv, p_da1, l_da1, proj, vec, vec_core, vec_all,
     *work,
 ):
     g_a, g_b, g_c, m_a, m_b, m_c, r_a, r_b, r_c, n_a, n_b = (work[i : i + 2] for i in range(0, 22, 2))
@@ -728,9 +724,11 @@
     text_embed(pools, mem, w_proj, pooled, tf, scale)
     finish(image_copies)
 
-    score_sums(tf, images, s_ref, e_ref, row_sums, col_sums, t, dp)
+    score_sums(tf, images, s_ref, e_ref, row_sums, core_sums, t)
     row_copies = group_share(links, row_sums, pair_of())
-    col_copies = rank_share(links, col_sums, pair_of())
+    finish(sibling_send(links, core_sums.at[0], core_sums.at[1], pair_of()))
+    col_sums[chip] = core_sums[0] + core_sums[1]
+    col_copies = chip_share(links, col_sums, pair_of())
     finish(col_copies)
     finish(row_copies)
     score_grad(s_ref, e_ref, row_sums, col_sums, pair, images, dts, vec, t)
@@ -748,16 +746,16 @@
     dh = hidden_grad(dz, w_down)
     hidden_spread(0, dh, mem_t, dgelu, w_up, du, p_da2)
     copies = [scatter_half(links, p_da2, l_da2, pair_of(), 0)]
-    hidden_spread(1, dh, mem_t, dgelu, w_up, du, p_da2)
     down_proj_grad(hsum, dz, de, pooled, proj, g_a[0], g_a[1], t)
     each(red_a[0].cores, red_a[1].cores)
+    hidden_spread(1, dh, mem_t, dgelu, w_up, du, p_da2)
     up_grad(a2, du, g_b[0], g_b[1])
-    each(red_b[0].cores, red_b[1].cores)
+    each(red_b[0].cores, red_b[1].cores, red_a[0].scatter, red_a[1].scatter)
+    row_grad(gp, mem, dx2, t)
     sent(copies[0])
     copies.append(scatter_half(links, p_da2, l_da2, pair_of(), 1))
-    row_grad(gp, mem, dx2, t)
+    each(red_b[0].scatter, red_b[1].scatter)
     vec[t, :, 768:1536] = gain_grad(p_da2, a2, as_row(gain_two))
-    each(red_a[0].scatter, red_b[0].scatter, red_a[1].scatter, red_b[1].scatter)
     arrived(copies[0])
     norm_two_grad(0, p_da2, l_da2, x1, as_row(gain_two), dx2, dx1, dy, t)
     copies[0] = share_half(links, dy, pair_of(), 0)
@@ -774,14 +772,17 @@
     out_grad(att, dy, g_c[0])
     attention_grad(dy, w_out, w_qkv, qkv, probs, dqkv, p_da1)
     each(red_a[1].gather_second, red_b[1].gather_second)
+    qkv_grad(dqkv, a1, g_c[0], g_c[1])
+    each(red_c[0].cores, red_c[1].cores)
     vec[t, :, :768] = gain_grad(p_da1, a1, as_row(gain_one))
     vec_copies = group_share(links, vec, pair_of())
     copies = group_scatter(links, p_da1, l_da1, pair_of())
-    qkv_grad(dqkv, a1, g_c[0], g_c[1])
-    each(red_c[0].cores, red_c[1].cores, red_c[0].scatter, red_c[1].scatter)
+    each(red_c[0].scatter, red_c[1].scatter)
     finish(vec_copies)
-    vec_all[dp] = vec[0] + vec[1] + vec[2] + vec[3]
-    vec_copies = rank_share(links, vec_all, pair_of())
+    vec_core[0] = vec[0] + vec[1] + vec[2] + vec[3]
+    finish(sibling_send(links, vec_core.at[0], vec_core.at[1], pair_of()))
+    vec_all[chip] = vec_core[0] + vec_core[1]
+    vec_copies = chip_share(links, vec_all, pair_of())
     each(red_a[1].share, red_a[0].share, red_b[0].share, red_b[1].share)
     proj_all[core, t, :4] = f_a1[core, 2]
     proj_all[core, t, 4:] = f_a1[core, 3, :2]
@@ -794,7 +795,7 @@
     each(red_a[0].done, red_a[1].done, red_b[0].done, red_b[1].done)
     finish(vec_copies)
     total = vec_all[0]
-    for i in range(1, RANKS):
+    for i in range(1, CHIPS):
         total = total + vec_all[i]
     o_norms[...] = total[:, :1536]
     o_loss[...] = total[:, 1536:] * (1.0 / 4096.0)
@@ -856,11 +857,11 @@
         VM((GROUP, OWN, D), BF16), VM((3, OWN, D), BF16), VM((OWN, D), F32), VM((OWN_CAPS, D), F32), VM((GROUP, OWN, D), BF16),
         VM((ROWS, HID), F32), VM((CAPS, HID), F32), VM((GROUP, OWN_CAPS, D), F32), VM((GROUP, CAPS, D), BF16),
         VM((CAPS, D), F32), VM((CAPS, 128), F32), VM((CAPS, D), BF16), VM((CAPS, ROWS), F32),
-        VM((CAPS, ROWS), F32), VM((GROUP, 1, 128), F32), VM((RANKS, 1, ROWS), F32), VM((GROUP, CAPS, D), BF16),
+        VM((CAPS, ROWS), F32), VM((GROUP, 1, 128), F32), VM((2, 1, ROWS), F32), VM((CHIPS, 1, ROWS), F32), VM((GROUP, CAPS, D), BF16),
         VM((CAPS, D), BF16), VM((CAPS, D), BF16), VM((CAPS, D), F32),
         VM((OWN, D), F32), VM((ROWS, HID), BF16), VM((GROUP, OWN, D), BF16), VM((3, OWN, D), BF16), VM((OWN, D), F32),
         VM((GROUP, OWN, D), BF16), VM((3, ROWS, BAND), BF16), VM((GROUP, OWN, D), BF16), VM((3, OWN, D), BF16),
-        VM((GROUP, BAND, D), BF16), VM((GROUP, 1, VEC), F32), VM((RANKS, 1, VEC), F32),
+        VM((GROUP, BAND, D), BF16), VM((GROUP, 1, VEC), F32), VM((2, 1, VEC), F32), VM((CHIPS, 1, VEC), F32),
     ]
     scratch += [VM((2,) + s, BF16) for s in sums] + [VM(s, BF16) for s in sums]
     scratch += [VM((3,) + s[1:], BF16) for s in sums[:4]] + [VM((15,) + s[1:], BF16) for s in sums[4:]]

time: 117 us -> 115 us (0.983)
  Pallas kernels: 116 us -> 114 us
    pallas_call x1, Pallas kernels: 112 us -> 110 us  [on_device(): pl.pallas_call(body, out_shape=(VM((1, 128), F32), VM((OWN, D), F32), VM(...]
where the time goes in v7:
time: 115 us
  Pallas kernels  114 us (99%)
    pallas_call x1, Pallas kernels, on_device(): pl.pallas_call(body, out_shape=(VM((1, 128), F32), VM((OWN, D), F32), VM(...  110 us
    pallas_call x1, Pallas kernels, on_device(): pl.pallas_call(widen, out_shape=(shape((1, 1), F32), shape((OWN, D), F32)...  4.45 us

profile of v7, /device:TPU:1, one launch (start us, length us, event | category | flops | bytes accessed | tf_op | source)
XLA Modules:
  0.0 115.0 jit_solution(10371298065964717811)
XLA Ops:
  0.7 109.8 %lit.1 = (f32[1,128]{1,0:T(1,128)S(1)}, f32[128,768]{1,0:T(8,128)S(1)}, f32[1,1536]{1,0:T(1,128)S(1)}, bf16[2,4,4,32,384]{4,3,2,1,0:T(8,128)(2,1)S(1)}, bf16[2,4...) custom-call(bf16[128,768]{1,0:T(8,128)(2,1)} %x.1, ...), custom_call_target="tpu_custom_call" | custom-call | tf_op jit(solution)/shard_map/lit/pallas_call | solution.py:869
  110.4 4.4 %widen.1 = (f32[1,1]{1,0:T(1,128)}, f32[128,768]{1,0:T(8,128)}, f32[768]{0:T(1024)}, f32[768]{0:T(1024)}, f32[768,768]{1,0:T(8,128)}, /*index=5*/f32[768,768]{1,...) custom-call(f32[1,128]{1,0:T(1,128)S(1)} %get-tuple-element.28.loss, ...), custom_call_target="tpu_custom_call" | custom-call | tf_op jit(solution)/shard_map/widen/pallas_call | solution.py:886

commit v8 on v7

--- a/solution.py
+++ b/solution.py
@@ -783,13 +783,14 @@
     finish(sibling_send(links, vec_core.at[0], vec_core.at[1], pair_of()))
     vec_all[chip] = vec_core[0] + vec_core[1]
     vec_copies = chip_share(links, vec_all, pair_of())
-    each(red_a[1].share, red_a[0].share, red_b[0].share, red_b[1].share)
+    red_a[1].share()
     proj_all[core, t, :4] = f_a1[core, 2]
     proj_all[core, t, 4:] = f_a1[core, 3, :2]
     proj_copies = group_share(links, proj_all.at[core], pair_of())
     finish(copies)
     norm_one_grad(p_da1, l_da1, x, as_row(gain_one), dx1, o_input, t)
     each(red_c[0].gather, red_c[1].gather)
+    each(red_a[0].share, red_b[0].share, red_b[1].share)
     finish(proj_copies)
     proj_copies = sibling_send(links, proj_all.at[core], proj_all.at[core], pair_of())
     each(red_a[0].done, red_a[1].done, red_b[0].done, red_b[1].done)
@@ -813,24 +814,21 @@
         stores.append(pltpu.make_async_copy(buf, target, stored.at[len(stores)]))
         stores[-1].start()
 
-    def halves(target, first, parts, rows):
+    def block(buf, target, first, parts, rows):
         for j in range(2):
-            target[first : first + rows, j * HALF : (j + 1) * HALF] = parts[j].reshape(rows, HALF).astype(F32)
+            buf[first : first + rows, j * HALF : (j + 1) * HALF] = parts[j].reshape(rows, HALF).astype(F32)
+        write(buf.at[pl.ds(first, rows)], target.at[pl.ds(first, rows)])
 
     write(grad, o_input)
-    halves(down, 0, a0, 512)
-    halves(down, 512, a1[:, :2], 256)
-    write(down, o_down)
-    halves(up, 0, b0, 512)
-    halves(up, 512, b1, 256)
-    write(up, o_up)
-    halves(proj, 0, full_proj, D)
-    write(proj, o_proj)
-    halves(out, 0, c0[:, :6], BAND)
-    write(out, o_out)
-    halves(qkv, 0, c0[:, 6:], 320)
-    halves(qkv, 320, c1, 256)
-    write(qkv, o_qkv)
+    for buf, target, whole, rest in ((down, o_down, a0, a1[:, :2]), (up, o_up, b0, b1)):
+        block(buf, target, 0, whole[:, :2], 256)
+        block(buf, target, 256, whole[:, 2:], 256)
+        block(buf, target, 512, rest, 256)
+    for r in range(GROUP):
+        block(proj, o_proj, r * BAND, full_proj[:, r], BAND)
+    block(qkv, o_qkv, 0, c0[:, 6:], 320)
+    block(qkv, o_qkv, 320, c1, 256)
+    block(out, o_out, 0, c0[:, :6], BAND)
     o_loss[0, 0] = loss[0, 0]
     o_one[...] = norms[:, :D].reshape(D)
     o_two[...] = norms[:, D:].reshape(D)
@@ -893,7 +891,7 @@
         out_specs=(pl.BlockSpec(memory_space=pltpu.SMEM), hbm, vmem, vmem, hbm, hbm, hbm, hbm, hbm),
         scratch_shapes=[
             VM((HID, D), F32), VM((D, HID), F32), VM((BAND, D), F32), VM((3 * BAND, D), F32), VM((D, D), F32),
-            dma((6,)),
+            dma((14,)),
         ],
         compiler_params=pltpu.CompilerParams(vmem_limit_bytes=40 << 20),
         name="widen",

time: 115 us -> 115 us (level)
  no operation moved by 1% of the time
where the time goes in v8:
time: 115 us
  Pallas kernels  114 us (99%)
    pallas_call x1, Pallas kernels, on_device(): pl.pallas_call(body, out_shape=(VM((1, 128), F32), VM((OWN, D), F32), VM(...  110 us
    pallas_call x1, Pallas kernels, on_device(): pl.pallas_call(widen, out_shape=(shape((1, 1), F32), shape((OWN, D), F32)...  4.44 us

profile of v8, /device:TPU:1, one launch (start us, length us, event | category | flops | bytes accessed | tf_op | source)
XLA Modules:
  0.0 115.0 jit_solution(8715914610024383241)
XLA Ops:
  0.7 109.8 %lit.1 = (f32[1,128]{1,0:T(1,128)S(1)}, f32[128,768]{1,0:T(8,128)S(1)}, f32[1,1536]{1,0:T(1,128)S(1)}, bf16[2,4,4,32,384]{4,3,2,1,0:T(8,128)(2,1)S(1)}, bf16[2,4...) custom-call(bf16[128,768]{1,0:T(8,128)(2,1)} %x.1, ...), custom_call_target="tpu_custom_call" | custom-call | tf_op jit(solution)/shard_map/lit/pallas_call | solution.py:867
  110.4 4.4 %widen.1 = (f32[1,1]{1,0:T(1,128)}, f32[128,768]{1,0:T(8,128)}, f32[768]{0:T(1024)}, f32[768]{0:T(1024)}, f32[768,768]{1,0:T(8,128)}, /*index=5*/f32[768,768]{1,...) custom-call(f32[1,128]{1,0:T(1,128)S(1)} %get-tuple-element.28.loss, ...), custom_call_target="tpu_custom_call" | custom-call | tf_op jit(solution)/shard_map/widen/pallas_call | solution.py:884
